TPU v7x, 32 devices: a whole 2x2x4 slice. The times are simulated.
32 devices in a mesh: pipe: 8 (over y, x, core), xs: 4 (over z).
Axes of the slice: x: 2, y: 2, z: 4, core: 2. Of those that a mesh axis runs over, the one named last changes fastest.
Arguments:
- start_vectors: bfloat16 [64, 16, 32, 512], P('pipe', None, 'xs'), may hold values from -36 to 36
- diag_blocks: bfloat16 [32, 512, 512], P('xs'), may hold values from -0.125 to 0.125
- face_blocks: bfloat16 [32, 4, 64, 512], P('xs'), may hold values from -0.1875 to 0.1875
- axial_blocks: bfloat16 [8, 512, 512], replicated, may hold values from -0.0625 to 0.0625
- neighbor_ids: int32 [32, 4], P('xs'), may hold values from 0 to 31
- neighbor_face: int32 [32, 4], P('xs'), may hold values from 0 to 3
- face_mask: int32 [32, 4], P('xs'), may hold values 0 or 1
Outputs:
- filtered: bfloat16 [64, 16, 32, 512], P('pipe', None, 'xs')
- gram: float32 [16, 16], replicated
- projected: float32 [16, 16], replicated
Inputs may be any that keep to these rules, and one draw needn't show every extreme that they name: `neighbor_ids`: an element number of the cross-section. `neighbor_face`: a face number.
All inputs are finite; a program needn't handle non-finite values. No bound on the sum of `face_mask` on one device may be relied on, other than what follows from the above.
Results may differ from a plain program's by a relative error of at most 0.0042.
Values may be sent and summed in bfloat16 or wider, within the bound.
No kernel may reach another device: no remote copies, remote signals or barrier semaphores. Data moves between devices by JAX's collectives and lax.ppermute only.
A program may use at most 192 MiB of HBM per device.

v0:
```python
import jax
import jax.numpy as jnp
from jax import lax
from jax.sharding import PartitionSpec as P

P_SIZE = 8
F = 4
HW = 4


shift_center = 0.3
half_width = 1.2


def extended_2(block, sides, width):
    for axis, dim in sides:
        count = lax.axis_size(axis)
        forward = [(i, i + 1) for i in range(count - 1)]
        forward.append((count - 1, 0))
        backward = [(target, source) for source, target in forward]
        low = lax.ppermute(
            lax.slice_in_dim(block, block.shape[dim] - width, None, axis=dim), axis, forward
        )
        high = lax.ppermute(lax.slice_in_dim(block, 0, width, axis=dim), axis, backward)
        block = jnp.concatenate([low, block, high], axis=dim)
    return block


def face_traces(vectors):
    layer_count, vector_count, element_count, block_width = vectors.shape
    cube = vectors.reshape(layer_count, vector_count, element_count, P_SIZE, P_SIZE, P_SIZE)
    stacked = jnp.stack(
        [
            cube[:, :, :, 0],
            cube[:, :, :, P_SIZE - 1],
            cube[:, :, :, :, 0],
            cube[:, :, :, :, P_SIZE - 1],
        ],
        axis=3,
    )
    return stacked.reshape(layer_count, vector_count, element_count, F * P_SIZE * P_SIZE)


def face_values(trace_rows, neighbor_ids, neighbor_face, face_mask):
    layer_count, vector_count, owned, trace_all = trace_rows.shape
    trace_width = trace_all // F
    shard_rows = lax.all_gather(trace_rows, "xs", axis=2, tiled=True)
    piece_rows = shard_rows.shape[2]
    element_ids = jnp.arange(piece_rows, dtype=jnp.int32)
    matched = (neighbor_ids[:, :, None] == element_ids[None, None, :]) & (
        face_mask[:, :, None] == 1
    )
    face_match = neighbor_face[:, :, None] == jnp.arange(F, dtype=jnp.int32)[None, None, :]
    selector = (matched[:, :, :, None] & face_match[:, :, None, :]).astype(jnp.bfloat16)
    reshaped = shard_rows.reshape(layer_count, vector_count, piece_rows, F, trace_width)
    picked = jnp.einsum("lnjgt,efjg->lneft", reshaped, selector, preferred_element_type=jnp.float32)
    collected = picked.reshape(layer_count, vector_count, owned, trace_all)
    return collected.astype(jnp.bfloat16).reshape(layer_count, vector_count, owned, F, trace_width)


def operate(extended, neighbor_vals, diag_blocks, face_blocks, axial_blocks):
    layer_count = extended.shape[0] - 2 * HW
    center = extended[HW : HW + layer_count]
    summed = jnp.einsum("lneb,ebc->lnec", center, diag_blocks, preferred_element_type=jnp.float32)
    summed = summed + jnp.einsum(
        "lneft,eftc->lnec", neighbor_vals, face_blocks, preferred_element_type=jnp.float32
    )
    block_width = center.shape[-1]
    for position in range(2 * HW):
        offset = position - HW if position < HW else position - HW + 1
        shifted = extended[HW + offset : HW + offset + layer_count]
        product = jnp.dot(
            shifted.reshape(-1, block_width),
            axial_blocks[position],
            preferred_element_type=jnp.float32,
        )
        summed = summed + product.reshape(summed.shape)
    return summed


def apply_once(
    vectors, diag_blocks, face_blocks, axial_blocks, neighbor_ids, neighbor_face, face_mask
):
    extended = extended_2(vectors, (("pipe", 0),), HW)
    neighbor_vals = face_values(face_traces(vectors), neighbor_ids, neighbor_face, face_mask)
    return operate(extended, neighbor_vals, diag_blocks, face_blocks, axial_blocks)


def local(
    start_vectors, diag_blocks, face_blocks, axial_blocks, neighbor_ids, neighbor_face, face_mask
):
    weights = (diag_blocks, face_blocks, axial_blocks)
    pattern = (neighbor_ids, neighbor_face, face_mask)
    local_layers = start_vectors.shape[0]
    first_image = apply_once(start_vectors, *weights, *pattern)
    first = ((first_image - shift_center * start_vectors.astype(jnp.float32)) / half_width).astype(
        jnp.bfloat16
    )
    second_image = apply_once(first, *weights, *pattern)
    filtered = (
        2.0 * (second_image - shift_center * first.astype(jnp.float32)) / half_width
        - start_vectors.astype(jnp.float32)
    ).astype(jnp.bfloat16)
    image = apply_once(filtered, *weights, *pattern)
    gram_local = jnp.einsum("lneb,lmeb->nm", filtered, filtered, preferred_element_type=jnp.float32)
    projected_local = jnp.einsum(
        "lneb,lmeb->nm", filtered.astype(jnp.float32), image, precision=lax.Precision.HIGHEST
    )
    gram_all, projected_all = lax.psum((gram_local, projected_local), ("pipe", "xs"))
    count_all = float(
        local_layers
        * lax.axis_size("pipe")
        * start_vectors.shape[2]
        * lax.axis_size("xs")
        * start_vectors.shape[3]
    )
    return (filtered, gram_all / count_all, projected_all / count_all)


def solution(mesh):
    in_specs = (
        P("pipe", None, "xs", None),
        P("xs", None, None),
        P("xs", None, None, None),
        P(),
        P("xs", None),
        P("xs", None),
        P("xs", None),
    )
    out_specs = (P("pipe", None, "xs", None), P(), P())
    return jax.shard_map(local, mesh=mesh, in_specs=in_specs, out_specs=out_specs, check_vma=False)
```

profile of v0, /device:TPU:0, one launch (start us, length us, event | category | flops | bytes accessed | tf_op | source)
XLA Modules:
  0.0 1041.3 jit_solution(12725043025280666828)
XLA Ops:
  7.2 7.7 copy.53
  19.6 2.9 copy.57
  25.3 2.9 collective-permute-start.1
  30.4 5.2 fusion.144
  35.6 2.7 collective-permute-done
  43.9 2.1 fusion.55
  46.0 2.0 fusion.57
  48.0 2.0 fusion.59
  50.5 2.0 fusion.61
  52.6 2.1 fusion.63
  54.7 2.0 fusion.65
  56.7 2.1 fusion.67
  58.9 253.3 %all-gather.4.cloned.1.call-done = bf16[8,16,32,256]{1,3,2,0:T(8,128)(2,1)} async-done(((bf16[8,16,8,256]{1,3,2,0:T(8,128)(2,1)}), bf16[8,16,32,256]{1,3,2,0:T(8,128)(2,1)}) %all-gather.4.cloned.1.call-update) | async-done | bytes 2097168 | tf_op jit(solution)/shard_map/all_gather | solution.py:47
  312.2 16.6 %copy.95 = bf16[8,16,32,4,64,1]{4,2,3,1,0,5:T(8,128)(2,1)} copy(bf16[8,16,32,4,64,1]{1,4,3,2,0,5:T(8,128)(2,1)} %bitcast.293) | data formatting | bytes 4194304 | tf_op jit(solution)/shard_map/reshape | solution.py:55
  328.8 3.2 fusion.141
  335.2 5.1 fusion.6
  340.4 5.9 copy.67
  350.8 2.9 copy.71
  354.1 2.6 collective-permute-start.3
  356.7 4.5 fusion.2
  361.1 6.1 collective-permute-done.2
  367.3 2.1 fusion.108
  369.3 2.1 fusion.103
  371.4 2.0 fusion.98
  373.4 2.0 fusion.93
  377.4 2.1 fusion.83
  379.6 2.0 fusion.78
  381.6 257.3 %all-gather.6.cloned.1.call-done = bf16[8,16,32,256]{1,3,2,0:T(8,128)(2,1)} async-done(((bf16[8,16,8,256]{1,3,2,0:T(8,128)(2,1)}), bf16[8,16,32,256]{1,3,2,0:T(8,128)(2,1)}) %all-gather.6.cloned.1.call-update) | async-done | bytes 2097168 | tf_op jit(solution)/shard_map/all_gather | solution.py:47
  638.9 16.6 %copy.116 = bf16[8,16,32,4,64,1]{4,2,3,1,0,5:T(8,128)(2,1)} copy(bf16[8,16,32,4,64,1]{1,4,3,2,0,5:T(8,128)(2,1)} %bitcast.295) | data formatting | bytes 4194304 | tf_op jit(solution)/shard_map/reshape | solution.py:55
  655.5 3.2 fusion.142
  661.8 5.4 fusion.7
  667.2 5.9 copy.88
  679.3 2.9 copy.92
  682.5 2.6 collective-permute-start.5
  685.6 2.1 fusion
  687.7 8.0 collective-permute-done.4
  695.7 2.1 fusion.106
  697.8 2.0 fusion.101
  699.8 2.1 fusion.96
  701.9 2.0 fusion.91
  703.9 2.0 fusion.86
  707.9 2.1 fusion.76
  710.0 2.0 fusion.69
  712.1 255.3 %all-gather.8.cloned.1.call-done = bf16[8,16,32,256]{1,3,2,0:T(8,128)(2,1)} async-done(((bf16[8,16,8,256]{1,3,2,0:T(8,128)(2,1)}), bf16[8,16,32,256]{1,3,2,0:T(8,128)(2,1)}) %all-gather.8.cloned.1.call-update) | async-done | bytes 2097168 | tf_op jit(solution)/shard_map/all_gather | solution.py:47
  967.4 16.6 %copy.136 = bf16[8,16,32,4,64,1]{4,2,3,1,0,5:T(8,128)(2,1)} copy(bf16[8,16,32,4,64,1]{1,4,3,2,0,5:T(8,128)(2,1)} %bitcast.294) | data formatting | bytes 4194304 | tf_op jit(solution)/shard_map/reshape | solution.py:55
  984.0 3.2 fusion.143
  990.1 5.4 fusion.42
  995.6 38.6 %all-reduce = (f32[16,16]{1,0:T(8,128)S(1)}, f32[16,16]{1,0:T(8,128)S(1)}) all-reduce(f32[16,16]{1,0:T(8,128)S(1)} %convolution_bitcast_fusion, f32[16,16]{1,0:T(8,128)S(1)} %fusion.42), channel_id=1, replica_groups=mesh['pipe'=8,'xs'=4] {'pipe','xs'}, use_global_device_ids=true, to_apply=%region_0.0 | all-reduce | flops 512 | bytes 4096 | tf_op jit(solution)/shard_map/psum | solution.py:109
  (110 shorter events, 41.2 us)
Async XLA Ops:
  7.2 324.8 %copy-start = (bf16[8,4,64,512]{3,2,1,0:T(8,128)(2,1)S(1)}, bf16[8,4,64,512]{3,2,1,0:T(8,128)(2,1)}, u32[]{:S(2)}) copy-start(bf16[8,4,64,512]{3,2,1,0:T(8,128)(2,1)} %param.9) | copy-start | bytes 6291460
  7.2 305.0 %all-gather.4.cloned.1.call-start = ((), (), s32[]{:S(2)}) async-start(), calls=%async_computation | async-start | bytes 20971520 | tf_op jit(solution)/shard_map/all_gather | solution.py:47
  22.5 1.2 copy-start.4
  22.5 6.9 copy-start.29
  22.6 7.0 copy-start.31
  22.6 7.1 copy-start.30
  22.6 616.3 %all-gather.6.cloned.1.call-start = ((), (), s32[]{:S(2)}) async-start(), calls=%async_computation.1 | async-start | bytes 20971520 | tf_op jit(solution)/shard_map/all_gather | solution.py:47
  24.9 13.5 %collective-permute-start = (bf16[4,16,8,512]{3,2,1,0:T(8,128)(2,1)}, bf16[4,16,8,512]{3,2,1,0:T(8,128)(2,1)}, u32[]{:S(2)}, u32[]{:S(2)}) collective-permute-start(bf16[4,16,8,512]{3,2,1,0:T(8,128)(2,1)} %get-tuple-element.37), channel_id=1, source_target_pairs={{0,4},{4,8},{8,12},{12,16},{16,20},{20,24},{24,28},{28,0},{1,5},{5... | collective-permute-start | bytes 1572872 | tf_op jit(solution)/shard_map/ppermute | solution.py:21
  25.3 14.5 %collective-permute-start.1 = (bf16[4,16,8,512]{3,2,1,0:T(8,128)(2,1)}, bf16[4,16,8,512]{3,2,1,0:T(8,128)(2,1)}, u32[]{:S(2)}, u32[]{:S(2)}) collective-permute-start(bf16[4,16,8,512]{3,2,1,0:T(8,128)(2,1)} %get-tuple-element.38), channel_id=1, source_target_pairs={{4,0},{8,4},{12,8},{16,12},{20,16},{24,20},{28,24},{0,28},{5,1},{9... | collective-permute-start | bytes 1572872 | tf_op jit(solution)/shard_map/ppermute | solution.py:24
  41.0 2.9 copy-start.7
  328.8 3.8 copy-start.23
  328.8 3.8 copy-start.24
  328.8 4.1 copy-start.25
  328.8 4.7 copy-start.26
  332.0 1.9 copy-start.5
  332.0 2.6 copy-start.21
  332.0 3.2 copy-start.22
  340.3 39.2 %copy-start.1 = (bf16[8,16,8,512]{3,1,0,2:T(8,128)(2,1)}, bf16[8,16,8,512]{3,1,0,2:T(8,128)(2,1)S(1)}, u32[]{:S(2)}) copy-start(bf16[8,16,8,512]{3,1,0,2:T(8,128)(2,1)S(1)} %fusion.6) | copy-start | bytes 3145732
  353.8 613.6 %all-gather.8.cloned.1.call-start = ((), (), s32[]{:S(2)}) async-start(), calls=%async_computation.2 | async-start | bytes 20971520 | tf_op jit(solution)/shard_map/all_gather | solution.py:47
  354.0 13.3 %collective-permute-start.2 = (bf16[4,16,8,512]{3,1,0,2:T(8,128)(2,1)S(1)}, bf16[4,16,8,512]{3,1,0,2:T(8,128)(2,1)S(1)}, u32[]{:S(2)}, u32[]{:S(2)}) collective-permute-start(bf16[4,16,8,512]{3,1,0,2:T(8,128)(2,1)S(1)} %get-tuple-element.33), channel_id=1, source_target_pairs={{0,4},{4,8},{8,12},{12,16},{16,20},{20,24},{24,28},{28,0},{1,5},{5... | collective-permute-start | bytes 1572872 | tf_op jit(solution)/shard_map/ppermute | solution.py:21
  354.1 13.2 %copy-start.8 = (bf16[8,512,512]{2,1,0:T(8,128)(2,1)S(1)}, bf16[8,512,512]{2,1,0:T(8,128)(2,1)}, u32[]{:S(2)}) copy-start(bf16[8,512,512]{2,1,0:T(8,128)(2,1)} %param.10) | copy-start | bytes 12582916
  354.1 21.4 %collective-permute-start.3 = (bf16[4,16,8,512]{3,1,0,2:T(8,128)(2,1)S(1)}, bf16[4,16,8,512]{3,1,0,2:T(8,128)(2,1)S(1)}, u32[]{:S(2)}, u32[]{:S(2)}) collective-permute-start(bf16[4,16,8,512]{3,1,0,2:T(8,128)(2,1)S(1)} %get-tuple-element.34), channel_id=1, source_target_pairs={{4,0},{8,4},{12,8},{16,12},{20,16},{24,20},{28,24},{0,28},{5,1},{9... | collective-permute-start | bytes 1572872 | tf_op jit(solution)/shard_map/ppermute | solution.py:24
  375.4 4.1 copy-start.27
  655.5 3.8 copy-start.17
  655.5 3.8 copy-start.18
  655.5 4.1 copy-start.19
  655.5 4.2 copy-start.28
  658.7 1.5 copy-start.2
  658.7 1.8 copy-start.6
  658.8 2.5 copy-start.11
  658.8 3.1 copy-start.16
  682.3 3.3 copy-start.3
  682.4 13.3 %collective-permute-start.4 = (bf16[4,16,8,512]{3,1,0,2:T(8,128)(2,1)S(1)}, bf16[4,16,8,512]{3,1,0,2:T(8,128)(2,1)S(1)}, u32[]{:S(2)}, u32[]{:S(2)}) collective-permute-start(bf16[4,16,8,512]{3,1,0,2:T(8,128)(2,1)S(1)} %get-tuple-element.31), channel_id=1, source_target_pairs={{0,4},{4,8},{8,12},{12,16},{16,20},{20,24},{24,28},{28,0},{1,5},{5... | collective-permute-start | bytes 1572872 | tf_op jit(solution)/shard_map/ppermute | solution.py:21
  682.5 21.4 %collective-permute-start.5 = (bf16[4,16,8,512]{3,1,0,2:T(8,128)(2,1)S(1)}, bf16[4,16,8,512]{3,1,0,2:T(8,128)(2,1)S(1)}, u32[]{:S(2)}, u32[]{:S(2)}) collective-permute-start(bf16[4,16,8,512]{3,1,0,2:T(8,128)(2,1)S(1)} %get-tuple-element.32), channel_id=1, source_target_pairs={{4,0},{8,4},{12,8},{16,12},{20,16},{24,20},{28,24},{0,28},{5,1},{9... | collective-permute-start | bytes 1572872 | tf_op jit(solution)/shard_map/ppermute | solution.py:24
  685.6 10.1 copy-start.9
  984.0 3.7 copy-start.13
  984.0 3.8 copy-start.14
  984.0 4.1 copy-start.15
  984.0 4.7 copy-start.20
  987.2 2.3 copy-start.10
  987.2 2.9 copy-start.12
Sparse Core Ops, SparseCore 0:
  22.7 289.4 all-gather.3
  353.9 284.9 all-gather.5
  682.4 284.9 all-gather.7
where the time goes:
time: 1040 us
  waiting for transfers between devices  783 us (75%)
  local copies, waits for them, and re-layouts  108 us (10%)
  matrix products  84.5 us (8%)
  blocking collectives  38.6 us (4%)
  between operations  14.1 us (1%)
    all_gather x3, waiting for transfers between devices, face_values(): shard_rows = lax.all_gather(trace_rows, 'xs', axis=2, tiled=True)  766 us
    dot_general x24, matrix products, operate(): jnp.dot(shifted.reshape(-1, block_width), axial_blocks[position], preferr...  55.6 us
    reshape x3, local copies, waits for them, and re-layouts, face_values(): shard_rows.reshape(layer_count, vector_count, piece_rows, F, trace_width)  49.8 us
    psum x1, blocking collectives, local(): lax.psum((gram_local, projected_local), ('pipe', 'xs'))  38.6 us
    unnamed x73, local copies, waits for them, and re-layouts  27.3 us
  transfers between devices with their start and end apart: 9, of which 7 were waited for; matrix products, arithmetic and copies ran while one was open for 6% of the time, Pallas kernels for 0%

commit v1 on v0

v1 whole, which is shorter than its diff:
```python
import functools

import jax
import jax.numpy as jnp
from jax import lax
from jax.experimental import pallas as pl
from jax.experimental.pallas import tpu as pltpu
from jax.sharding import PartitionSpec as P

P_SIZE = 8
F = 4
HW = 4
TR = P_SIZE * P_SIZE
LANES = 128
CHUNKS = 1
PAIR_CAP = 12
ROW_TILE = 256
VMEM_BYTES = 48 * 1024 * 1024

shift_center = 0.3
half_width = 1.2

VMEM = pl.BlockSpec(memory_space=pltpu.VMEM)
SMEM = pl.BlockSpec(memory_space=pltpu.SMEM)
ANY = pl.BlockSpec(memory_space=pl.ANY)
bf16 = jnp.bfloat16
f32 = jnp.float32


def dot(a, b):
    return jnp.dot(a, b, preferred_element_type=f32)


def trace_selector(block):
    node = lax.broadcasted_iota(jnp.int32, (block, F * TR), 0)
    column = lax.broadcasted_iota(jnp.int32, (block, F * TR), 1)
    face, entry = column // TR, column % TR
    major, minor = entry // P_SIZE, entry % P_SIZE
    fixed = jnp.where(face % 2 == 0, 0, P_SIZE - 1)
    on_i = fixed * TR + major * P_SIZE + minor
    on_j = major * TR + fixed * P_SIZE + minor
    return (node == jnp.where(face < 2, on_i, on_j)).astype(bf16)


def left_half(shape):
    return lax.broadcasted_iota(jnp.int32, shape, len(shape) - 1) < TR


def read_wide(ref, index):
    return jnp.concatenate([ref[k, index, :] for k in range(ref.shape[0])], axis=1)


def write_wide(ref, index, value):
    for k in range(ref.shape[0]):
        ref[k, index, :] = value[:, k * LANES : (k + 1) * LANES]


def of_element(ref, e, elements):
    return pl.ds(e, ref.shape[1] // elements, stride=elements)


def store_traces(wide_ref, selector, traces_ref, elements):
    half = wide_ref.shape[1] // elements // 2
    for e in range(elements):
        values = dot(read_wide(wide_ref, of_element(wide_ref, e, elements)).astype(bf16), selector)
        for pair in range(F // 2):
            a = values[:half, pair * LANES : (pair + 1) * LANES]
            b = values[half:, pair * LANES : (pair + 1) * LANES]
            left = left_half(a.shape)
            traces_ref[e * F + 2 * pair] = jnp.where(left, a, pltpu.roll(b, TR, 1)).astype(bf16)
            traces_ref[e * F + 2 * pair + 1] = jnp.where(left, pltpu.roll(a, TR, 1), b).astype(bf16)


def pick_traces(lists_ref, traces_ref, sent_refs):
    for shift, sent in enumerate(sent_refs):

        def body(j, carry, shift=shift, sent=sent):
            sent[j] = traces_ref[lists_ref[shift, j]]
            return carry

        lax.fori_loop(0, sent.shape[0], body, 0)


def lifted_rows(e, refs_ref, traces_ref, arrived_refs):
    per = traces_ref.shape[0]
    slots = []
    for f in range(F):
        code = refs_ref[0, e * F + f]
        source, place = code // per, code % per
        value = jnp.where(source == 0, traces_ref[place].astype(f32), 0.0)
        for shift, arrived in enumerate(arrived_refs):
            here = source == shift + 1
            value = jnp.where(here, arrived[jnp.where(here, place, 0)].astype(f32), value)
        slots.append(value)
    tops, bottoms = [], []
    for pair in range(F // 2):
        a, b = slots[2 * pair], slots[2 * pair + 1]
        left = left_half(a.shape)
        tops.append(jnp.where(left, a, pltpu.roll(b, TR, 1)))
        bottoms.append(jnp.where(left, pltpu.roll(a, TR, 1), b))
    both = jnp.concatenate([jnp.concatenate(tops, 1), jnp.concatenate(bottoms, 1)], 0)
    return both.astype(bf16)


def opening_kernel(start_ref, selector_ref, low_ref, high_ref, traces_ref, wide):
    layers, width, elements, block = start_ref.shape
    edge = low_ref.shape[0]
    values = start_ref[...].reshape(layers * width * elements, block)
    low_ref[...] = values[:edge]
    high_ref[...] = values[-edge:]
    write_wide(wide, slice(None), values.astype(f32))
    store_traces(wide, selector_ref[...], traces_ref, elements)


def picking_kernel(lists_ref, traces_ref, *sent_refs):
    pick_traces(lists_ref, traces_ref, sent_refs)


def pattern_kernel(*refs):
    codes_refs, (me_ref, lists_ref, places_ref, most_ref) = refs[:-4], refs[-4:]
    shards = len(codes_refs)
    per = codes_refs[0].shape[0]
    every = shards * per
    me = me_ref[0]
    lane = lax.broadcasted_iota(jnp.int32, (per, every), 1)
    asked = [codes[:, :1] == lane for codes in codes_refs]
    need = jnp.concatenate(
        [jnp.max(a.astype(f32), axis=0, keepdims=True) for a in asked]
        + [jnp.zeros((8 - shards % 8, every), f32)] * (shards % 8 != 0),
        axis=0,
    ).astype(bf16)
    row = lax.broadcasted_iota(jnp.int32, (every, every), 0)
    column = lax.broadcasted_iota(jnp.int32, (every, every), 1)
    same = row // per == column // per
    before = (same & (row < column)).astype(bf16)
    rank = dot(need, before)
    total = dot(need, same.astype(bf16))
    over = (((0,), (1,)), ((), ()))
    rank_down = lax.dot_general(before, need, over, preferred_element_type=f32)
    need_down = lax.dot_general((row == column).astype(bf16), need, over, preferred_element_type=f32)
    block_of = lax.broadcasted_iota(jnp.int32, total.shape, 1) // per
    asker = lax.rem(lax.broadcasted_iota(jnp.int32, total.shape, 0) + me, shards)
    most = jnp.max(jnp.max(jnp.where(block_of == asker, 0.0, total), axis=1, keepdims=True), axis=0, keepdims=True)
    most_ref[...] = jnp.broadcast_to(most, most_ref.shape).astype(jnp.int32)
    trace = lax.broadcasted_iota(jnp.int32, (every, LANES), 0)
    slot = lax.broadcasted_iota(jnp.int32, (every, LANES), 1)
    mine = trace // per == me
    lists_ref[...] = jnp.zeros_like(lists_ref)
    for shift in range(1, shards):
        sent = mine & (need_down[:, shift : shift + 1] > 0.5) & (
            rank_down[:, shift : shift + 1].astype(jnp.int32) == slot
        )
        listed = jnp.sum(jnp.where(sent, (trace - me * per).astype(f32), 0.0), axis=0, keepdims=True)
        lists_ref[shift - 1 : shift, :] = listed.astype(jnp.int32)
    owner = lax.rem(me + shards - lane // per, shards)
    place = jnp.where(owner == 0, lane % per, rank[:1].astype(jnp.int32))
    code = jnp.where(asked[0], owner * per + place, 0).astype(f32)
    found = jnp.sum(code, axis=1, keepdims=True)
    hit = jnp.sum(asked[0].astype(f32), axis=1, keepdims=True)
    found = jnp.where(hit > 0.5, found, float(every))
    down = lax.broadcasted_iota(jnp.int32, (per, LANES), 0)
    across = lax.broadcasted_iota(jnp.int32, (per, LANES), 1)
    turned = jnp.sum(jnp.where(down == across, jnp.broadcast_to(found, (per, LANES)), 0.0), axis=0, keepdims=True)
    places_ref[...] = turned.astype(jnp.int32)


def round_kernel(step, shards, elements, *refs):
    refs = list(refs)
    take = lambda n: [refs.pop(0) for _ in range(n)]
    places_ref, lists_ref, here_ref, low_ref, high_ref, traces_ref = take(6)
    arrived_refs = take(shards - 1)
    diag_hbm, face_hbm, axial_hbm, selector_ref = take(4)
    if step == 2:
        (start_ref,) = take(1)
    if step == 3:
        gram_ref, projected_ref = take(2)
    else:
        out_ref, out_low_ref, out_high_ref, out_traces_ref = take(4)
        sent_refs = take(shards - 1)
    ext, wide, acc, diag, face, axial, sems = refs
    rows, block = here_ref.shape
    edge = low_ref.shape[0]
    layer = edge // HW

    loads = [
        pltpu.make_async_copy(diag_hbm, diag, sems.at[0]),
        pltpu.make_async_copy(face_hbm, face, sems.at[1]),
        pltpu.make_async_copy(axial_hbm, axial, sems.at[2]),
    ]
    for load in loads:
        load.start()
    ext[:edge] = low_ref[...]
    ext[edge : edge + rows] = here_ref[...]
    ext[edge + rows :] = high_ref[...]
    write_wide(wide, slice(None), here_ref[...].astype(f32))
    loads[0].wait()
    loads[1].wait()
    for e in range(elements):
        own = read_wide(wide, of_element(wide, e, elements)).astype(bf16)
        lifted = lifted_rows(e, places_ref, traces_ref, arrived_refs)
        write_wide(acc, of_element(acc, e, elements), dot(own, diag[e]) + dot(lifted, face[e]))
    loads[2].wait()
    tile = min(ROW_TILE, rows)

    def along(i, carry):
        base = pl.multiple_of(i * tile, tile)
        sides = []
        for position in range(2 * HW):
            offset = position if position < HW else position + 1
            sides.append(ext[pl.ds(pl.multiple_of(base + offset * layer, 16), tile), :])
        total = read_wide(acc, pl.ds(base, tile)) + dot(jnp.concatenate(sides, 1), axial[...])
        here = here_ref[pl.ds(base, tile), :].astype(f32)
        if step == 1:
            new = (total - shift_center * here) * (1.0 / half_width)
        elif step == 2:
            begun = start_ref[pl.ds(base, tile), :].astype(f32)
            new = (total - shift_center * here) * (2.0 / half_width) - begun
        else:
            write_wide(acc, pl.ds(base, tile), total)
            return carry
        new = new.astype(bf16)
        out_ref[pl.ds(base, tile), :] = new
        write_wide(acc, pl.ds(base, tile), new.astype(f32))
        return carry

    lax.fori_loop(0, rows // tile, along, 0)
    if step != 3:
        out_low_ref[...] = out_ref[:edge]
        out_high_ref[...] = out_ref[rows - edge :]
        store_traces(acc, selector_ref[...], out_traces_ref, elements)
        pick_traces(lists_ref, out_traces_ref, sent_refs)
        return

    over = (((1,), (1,)), ((), ()))
    gram = jnp.zeros((layer, layer), f32)
    projected = jnp.zeros((layer, layer), f32)
    for l in range(rows // layer):
        own = here_ref[l * layer : (l + 1) * layer]
        image = read_wide(acc, slice(l * layer, (l + 1) * layer))
        upper = image.astype(bf16)
        lower = (image - upper.astype(f32)).astype(bf16)
        gram += lax.dot_general(own, own, over, preferred_element_type=f32)
        projected += lax.dot_general(own, upper, over, preferred_element_type=f32)
        projected += lax.dot_general(own, lower, over, preferred_element_type=f32)
    vectors = layer // elements
    down = lax.broadcasted_iota(jnp.int32, (layer, layer), 0)
    across = lax.broadcasted_iota(jnp.int32, (layer, layer), 1)
    keep = down % elements == across % elements
    group = (
        lax.broadcasted_iota(jnp.int32, (layer, LANES), 0) // elements
        == lax.broadcasted_iota(jnp.int32, (layer, LANES), 1)
    ).astype(f32)
    for ref, value in ((gram_ref, gram), (projected_ref, projected)):
        value = jnp.where(keep, value, 0.0).reshape(vectors, elements, layer).sum(1)
        ref[...] = jnp.dot(value, group, precision=lax.Precision.HIGHEST, preferred_element_type=f32)


def shape(dims, dtype=bf16):
    return jax.ShapeDtypeStruct(dims, dtype)


def params():
    return pltpu.CompilerParams(vmem_limit_bytes=VMEM_BYTES)


def rotate(value, axis, shift):
    count = lax.axis_size(axis)
    return lax.ppermute(value, axis, [(i, (i + shift) % count) for i in range(count)])


def add_over(value, axis):
    count = lax.axis_size(axis)
    if count & (count - 1):
        return lax.psum(value, axis)
    step = 1
    while step < count:
        value = value + lax.ppermute(value, axis, [(i, i ^ step) for i in range(count)])
        step *= 2
    return value


def local(start_vectors, diag_blocks, face_blocks, axial_blocks, neighbor_ids, neighbor_face, face_mask):
    layers, vectors, elements, block = start_vectors.shape
    shards = lax.axis_size("xs")
    me = lax.axis_index("xs").astype(jnp.int32)
    per = elements * F
    width = vectors
    rows = layers * width * elements
    edge = HW * width * elements
    half = layers * width // 2
    face_flat = face_blocks.reshape(elements, F * TR, block)
    axial_flat = axial_blocks.reshape(2 * HW * block, block)
    selector = trace_selector(block)

    codes = jnp.where(face_mask == 1, neighbor_ids * F + neighbor_face, -1).reshape(per, 1)
    codes = jnp.broadcast_to(codes, (per, LANES)).astype(jnp.int32)
    all_codes = [codes] + [rotate(codes, "xs", -shift) for shift in range(1, shards)]
    lists, places, most = pl.pallas_call(
        pattern_kernel,
        out_shape=[shape((8, LANES), jnp.int32), shape((1, LANES), jnp.int32), shape((1, LANES), jnp.int32)],
        in_specs=[VMEM] * shards + [SMEM],
        out_specs=[VMEM] * 3,
        compiler_params=params(),
        name="pattern",
    )(*all_codes, me.reshape(1))

    low, high, traces = pl.pallas_call(
        opening_kernel,
        out_shape=[shape((edge, block)), shape((edge, block)), shape((per, half, LANES))],
        in_specs=[VMEM] * 2,
        out_specs=[VMEM] * 3,
        scratch_shapes=[pltpu.VMEM((block // LANES, rows, LANES), f32)],
        compiler_params=params(),
        name="opening",
    )(start_vectors, selector)

    start_flat = start_vectors.reshape(rows, block)
    macs = rows * block * (block * (1 + 2 * HW) + F * TR)

    def one_round(step, cap, here, low, high, traces, sent):
        from_low = rotate(high, "pipe", 1)
        from_high = rotate(low, "pipe", -1)
        arrived = [rotate(s, "xs", shift + 1) for shift, s in enumerate(sent)]
        operands = [places, lists, here, from_low, from_high, traces, *arrived]
        operands += [diag_blocks, face_flat, axial_flat, selector]
        specs = [SMEM] * 2 + [VMEM] * (4 + shards - 1) + [ANY] * 3 + [VMEM]
        if step == 2:
            operands.append(start_flat)
            specs.append(VMEM)
        if step == 3:
            outs = [shape((vectors, LANES), f32)] * 2
        else:
            outs = [shape((rows, block)), shape((edge, block)), shape((edge, block)), shape((per, half, LANES))]
            outs += [shape((cap, half, LANES))] * (shards - 1)
        return pl.pallas_call(
            functools.partial(round_kernel, step, shards, elements),
            out_shape=outs,
            in_specs=specs,
            out_specs=[VMEM] * len(outs),
            scratch_shapes=[
                pltpu.VMEM((rows + 2 * edge, block), bf16),
                pltpu.VMEM((block // LANES, rows, LANES), f32),
                pltpu.VMEM((block // LANES, rows, LANES), f32),
                pltpu.VMEM((elements, block, block), bf16),
                pltpu.VMEM((elements, F * TR, block), bf16),
                pltpu.VMEM((2 * HW * block, block), bf16),
                pltpu.SemaphoreType.DMA((3,)),
            ],
            compiler_params=params(),
            cost_estimate=pl.CostEstimate(flops=2 * macs, bytes_accessed=14 * 2**20, transcendentals=0),
            name=f"round_{step}",
        )(*operands)

    def run(cap):
        sent = pl.pallas_call(
            picking_kernel,
            out_shape=[shape((cap, half, LANES))] * (shards - 1),
            in_specs=[SMEM, VMEM],
            out_specs=[VMEM] * (shards - 1),
            compiler_params=params(),
            name="picking",
        )(lists, traces)
        first, *rest = one_round(1, cap, start_flat, low, high, traces, sent)
        filtered, *rest = one_round(2, cap, first, rest[0], rest[1], rest[2], rest[3:])
        gram, projected = one_round(3, cap, filtered, rest[0], rest[1], rest[2], rest[3:])
        return filtered, gram, projected

    filtered, gram, projected = lax.cond(
        most[0, 0] <= PAIR_CAP, lambda: run(min(PAIR_CAP, per)), lambda: run(per)
    )
    both = jnp.concatenate([gram, projected], axis=0)
    both = add_over(add_over(both, "pipe"), "xs")
    count_all = float(layers * lax.axis_size("pipe") * elements * shards * block)
    both = both[:, :vectors] / count_all
    return filtered.reshape(start_vectors.shape), both[:vectors], both[vectors:]


def solution(mesh):
    in_specs = (
        P("pipe", None, "xs", None),
        P("xs", None, None),
        P("xs", None, None, None),
        P(),
        P("xs", None),
        P("xs", None),
        P("xs", None),
    )
    out_specs = (P("pipe", None, "xs", None), P(), P())
    return jax.shard_map(local, mesh=mesh, in_specs=in_specs, out_specs=out_specs, check_vma=False)
```

time: 1040 us -> 129 us (0.12)
  waiting for transfers between devices: 783 us -> 47 us
  local copies, waits for them, and re-layouts: 108 us -> 0.87 us
  matrix products: 84.5 us -> 0 us
  Pallas kernels: 0 us -> 38.7 us
  blocking collectives: 38.6 us -> 0 us
  starting transfers between devices: 8.85 us -> 39.9 us
  between operations: 14.1 us -> 0.75 us
    all_gather x3 -> x0, waiting for transfers between devices: 766 us -> none  [face_values(): shard_rows = lax.all_gather(trace_rows, 'xs', axis=2, tiled=True)]
    dot_general x34 -> x0, matrix products: 79.3 us -> none  [the longest x24 55.6 us: operate(): jnp.dot(shifted.reshape(-1, block_width), axial_blocks[position], preferr...]
    reshape x3 -> x0, local copies, waits for them, and re-layouts: 49.8 us -> none  [face_values(): shard_rows.reshape(layer_count, vector_count, piece_rows, F, trace_width)]
    pallas_call x0 -> x6, Pallas kernels: none -> 38.7 us  [the longest x3 35 us: one_round(): pl.pallas_call(functools.partial(round_kernel, step, shards, elements), o...]
    psum x1 -> x0, blocking collectives: 38.6 us -> none  [local(): lax.psum((gram_local, projected_local), ('pipe', 'xs'))]
    ppermute x6 -> x23, starting transfers between devices: 8.73 us -> 39.9 us  [the longest x18 33.2 us: rotate(): lax.ppermute(value, axis, [(i, (i + shift) % count) for i in range(count)])]
    ppermute x6 -> x23, waiting for transfers between devices: 17 us -> 47 us  [the longest x18 34 us: rotate(): lax.ppermute(value, axis, [(i, (i + shift) % count) for i in range(count)])]
    unnamed x73 -> x1, local copies, waits for them, and re-layouts: 27.3 us -> 0.01 us
  transfers between devices with their start and end apart: 9 -> 23, of which waited for: 7 -> 11; matrix products, arithmetic and copies ran while one was open for 6% -> 0% of each run, Pallas kernels for 0% -> 3%
where the time goes in v1:
time: 129 us; the launch traced here: 128 us
  waiting for transfers between devices  47 us (36%)
  starting transfers between devices  39.9 us (31%)
  Pallas kernels  38.7 us (30%)
    pallas_call x3, Pallas kernels, one_round(): pl.pallas_call(functools.partial(round_kernel, step, shards, elements), o...  35 us
    ppermute x18, waiting for transfers between devices, rotate(): lax.ppermute(value, axis, [(i, (i + shift) % count) for i in range(count)])  34 us
    ppermute x18, starting transfers between devices, rotate(): lax.ppermute(value, axis, [(i, (i + shift) % count) for i in range(count)])  33.2 us
    ppermute x5, waiting for transfers between devices, add_over(): lax.ppermute(value, axis, [(i, i ^ step) for i in range(count)])  13 us
    ppermute x5, starting transfers between devices, add_over(): lax.ppermute(value, axis, [(i, i ^ step) for i in range(count)])  6.76 us
  transfers between devices with their start and end apart: 23, of which 11 were waited for; matrix products, arithmetic and copies ran while one was open for 0% of the time, Pallas kernels for 3%

profile of v1, /device:TPU:0, one launch (start us, length us, event | category | flops | bytes accessed | tf_op | source)
XLA Modules:
  0.0 128.5 jit_solution(1157123901961750361)
XLA Ops:
  0.6 0.7 add_select_fusion.3
  1.4 0.1 copy.11
  1.4 0.1 broadcast_in_dim.18
  1.5 0.1 broadcast_in_dim.19.refs_0_
  1.6 3.0 %collective-permute-start.32 = (s32[32,128]{1,0:T(8,128)S(1)}, s32[32,128]{1,0:T(8,128)S(1)}, u32[]{:S(2)}, u32[]{:S(2)}) collective-permute-start(s32[32,128]{1,0:T(8,128)S(1)} %broadcast_in_dim.19.refs_0_), channel_id=1, source_target_pairs={{0,1},{1,2},{2,3},{3,0},{4,5},{5,6},{6,7},{7,4},{8,9},{9,10},{10,1... | collective-permute-start | bytes 49160 | tf_op jit(solution)/shard_map/ppermute | solution.py:268
  4.6 2.6 %collective-permute-start.31 = (s32[32,128]{1,0:T(8,128)S(1)}, s32[32,128]{1,0:T(8,128)S(1)}, u32[]{:S(2)}, u32[]{:S(2)}) collective-permute-start(s32[32,128]{1,0:T(8,128)S(1)} %broadcast_in_dim.19.refs_0_), channel_id=1, source_target_pairs={{0,2},{1,3},{2,0},{3,1},{4,6},{5,7},{6,4},{7,5},{8,10},{9,11},{10,... | collective-permute-start | bytes 49160 | tf_op jit(solution)/shard_map/ppermute | solution.py:268
  7.2 1.3 %collective-permute-start.30 = (s32[32,128]{1,0:T(8,128)S(1)}, s32[32,128]{1,0:T(8,128)S(1)}, u32[]{:S(2)}, u32[]{:S(2)}) collective-permute-start(s32[32,128]{1,0:T(8,128)S(1)} %broadcast_in_dim.19.refs_0_), channel_id=1, source_target_pairs={{0,3},{1,0},{2,1},{3,2},{4,7},{5,4},{6,5},{7,6},{8,11},{9,8},{10,9... | collective-permute-start | bytes 49160 | tf_op jit(solution)/shard_map/ppermute | solution.py:268
  8.6 0.1 fusion.12.selector_ref
  8.7 2.4 %opening.1 = (bf16[512,512]{1,0:T(8,128)(2,1)S(1)}, bf16[512,512]{1,0:T(8,128)(2,1)}, bf16[32,64,128]{2,1,0:T(8,128)(2,1)S(1)}) custom-call(bf16[8,16,8,512]{3,2,1,0:T(8,128)(2,1)} %start_ref.1, bf16[512,256]{1,0:T(8,128)(2,1)S(1)} %fusion.12.selector_ref), custom_call_target="tpu_custom_call" | custom-call | tf_op jit(solution)/shard_map/opening/pallas_call | solution.py:307
  11.1 0.4 pattern.1
  11.6 96.4 %conditional.1 = (bf16[1024,512]{1,0:T(8,128)(2,1)}, f32[16,128]{1,0:T(8,128)S(1)}, f32[16,128]{1,0:T(8,128)S(1)}) conditional(s32[]{:T(128)} %bitcast.1, (bf16[512,512]{1,0:T(8,128)(2,1)}, bf16[512,512]{1,0:T(8,128)(2,1)S(1)}, s32[8,128]{1,0:T(8,128)S(1)}, bf16[32,64,128]{2,1,0:T(8,128)(2,1)S(1)}, s32[1,128]{1,0:T(1,128)S(1)}, ...), branch_computations={%region_0.1_spmd, %region_1.2_spmd} | conditional | flops 15300820992 | bytes 115344104 | solution.py:368
  11.8 0.1 collective-permute-start.15
  11.9 2.6 %collective-permute-start.16 = (bf16[512,512]{1,0:T(8,128)(2,1)S(1)}, bf16[512,512]{1,0:T(8,128)(2,1)S(1)}, u32[]{:S(2)}, u32[]{:S(2)}) collective-permute-start(bf16[512,512]{1,0:T(8,128)(2,1)S(1)} %get-tuple-element.79), channel_id=1, source_target_pairs={{0,28},{4,0},{8,4},{12,8},{16,12},{20,16},{24,20},{28,24},{1,29},{... | collective-permute-start | bytes 1572872 | tf_op jit(solution)/shard_map/cond/branch_1_fun/ppermute | solution.py:268
  14.5 0.9 picking.3
  15.4 0.7 collective-permute-start.17
  16.1 2.9 %collective-permute-start.18 = (bf16[12,64,128]{2,1,0:T(8,128)(2,1)S(1)}, bf16[12,64,128]{2,1,0:T(8,128)(2,1)S(1)}, u32[]{:S(2)}, u32[]{:S(2)}) collective-permute-start(bf16[12,64,128]{2,1,0:T(8,128)(2,1)S(1)} %get-tuple-element.82), channel_id=1, source_target_pairs={{0,2},{1,3},{2,0},{3,1},{4,6},{5,7},{6,4},{7,5},{8,10},{9,11},{10,... | collective-permute-start | bytes 589832 | tf_op jit(solution)/shard_map/cond/branch_1_fun/ppermute | solution.py:268
  19.0 0.3 collective-permute-start.19
  19.3 5.9 %collective-permute-done.17.refs_6_ = bf16[12,64,128]{2,1,0:T(8,128)(2,1)S(1)} collective-permute-done((bf16[12,64,128]{2,1,0:T(8,128)(2,1)S(1)}, bf16[12,64,128]{2,1,0:T(8,128)(2,1)S(1)}, u32[]{:S(2)}, u32[]{:S(2)}) %collective-permute-start.17) | collective-permute-done | bytes 196640 | tf_op jit(solution)/shard_map/cond/branch_1_fun/ppermute | solution.py:268
  25.2 6.5 %collective-permute-done.18.refs_7_ = bf16[12,64,128]{2,1,0:T(8,128)(2,1)S(1)} collective-permute-done((bf16[12,64,128]{2,1,0:T(8,128)(2,1)S(1)}, bf16[12,64,128]{2,1,0:T(8,128)(2,1)S(1)}, u32[]{:S(2)}, u32[]{:S(2)}) %collective-permute-start.18) | collective-permute-done | bytes 196640 | tf_op jit(solution)/shard_map/cond/branch_1_fun/ppermute | solution.py:268
  31.6 0.0 copy-start.1
  31.7 0.0 copy-start.3
  31.7 12.6 %round_1.3 = (bf16[1024,512]{1,0:T(8,128)(2,1)S(1)}, bf16[512,512]{1,0:T(8,128)(2,1)S(1)}, bf16[512,512]{1,0:T(8,128)(2,1)S(1)}, bf16[32,64,128]{2,1,0:T(8,128)(...) custom-call(s32[1,128]{1,0:T(1,128)S(1)} %get-tuple-element.75.refs_0, ...), custom_call_target="tpu_custom_call" | custom-call | flops 5100273664 | bytes 14680064 | tf_op jit(solution)/shard_map/cond/branch_1_fun/round_1/pallas_call | solution.py:335
  44.3 0.1 collective-permute-start.20
  44.4 2.6 %collective-permute-start.21 = (bf16[512,512]{1,0:T(8,128)(2,1)S(1)}, bf16[512,512]{1,0:T(8,128)(2,1)S(1)}, u32[]{:S(2)}, u32[]{:S(2)}) collective-permute-start(bf16[512,512]{1,0:T(8,128)(2,1)S(1)} %get-tuple-element.90), channel_id=1, source_target_pairs={{0,28},{4,0},{8,4},{12,8},{16,12},{20,16},{24,20},{28,24},{1,29},{... | collective-permute-start | bytes 1572872 | tf_op jit(solution)/shard_map/cond/branch_1_fun/ppermute | solution.py:268
  47.0 4.4 %collective-permute-start.22 = (bf16[12,64,128]{2,1,0:T(8,128)(2,1)S(1)}, bf16[12,64,128]{2,1,0:T(8,128)(2,1)S(1)}, u32[]{:S(2)}, u32[]{:S(2)}) collective-permute-start(bf16[12,64,128]{2,1,0:T(8,128)(2,1)S(1)} %get-tuple-element.92), channel_id=1, source_target_pairs={{0,1},{1,2},{2,3},{3,0},{4,5},{5,6},{6,7},{7,4},{8,9},{9,10},{10,1... | collective-permute-start | bytes 589832 | tf_op jit(solution)/shard_map/cond/branch_1_fun/ppermute | solution.py:268
  51.4 0.1 collective-permute-start.23
  51.5 2.3 %collective-permute-start.24 = (bf16[12,64,128]{2,1,0:T(8,128)(2,1)S(1)}, bf16[12,64,128]{2,1,0:T(8,128)(2,1)S(1)}, u32[]{:S(2)}, u32[]{:S(2)}) collective-permute-start(bf16[12,64,128]{2,1,0:T(8,128)(2,1)S(1)} %get-tuple-element.94), channel_id=1, source_target_pairs={{0,3},{1,0},{2,1},{3,2},{4,7},{5,4},{6,5},{7,6},{8,11},{9,8},{10,9... | collective-permute-start | bytes 589832 | tf_op jit(solution)/shard_map/cond/branch_1_fun/ppermute | solution.py:268
  53.7 3.0 %collective-permute-done.22.refs_6_ = bf16[12,64,128]{2,1,0:T(8,128)(2,1)S(1)} collective-permute-done((bf16[12,64,128]{2,1,0:T(8,128)(2,1)S(1)}, bf16[12,64,128]{2,1,0:T(8,128)(2,1)S(1)}, u32[]{:S(2)}, u32[]{:S(2)}) %collective-permute-start.22) | collective-permute-done | bytes 196640 | tf_op jit(solution)/shard_map/cond/branch_1_fun/ppermute | solution.py:268
  56.7 6.7 %collective-permute-done.23.refs_7_ = bf16[12,64,128]{2,1,0:T(8,128)(2,1)S(1)} collective-permute-done((bf16[12,64,128]{2,1,0:T(8,128)(2,1)S(1)}, bf16[12,64,128]{2,1,0:T(8,128)(2,1)S(1)}, u32[]{:S(2)}, u32[]{:S(2)}) %collective-permute-start.23) | collective-permute-done | bytes 196640 | tf_op jit(solution)/shard_map/cond/branch_1_fun/ppermute | solution.py:268
  63.5 11.3 %round_2.3 = (bf16[1024,512]{1,0:T(8,128)(2,1)}, bf16[512,512]{1,0:T(8,128)(2,1)S(1)}, bf16[512,512]{1,0:T(8,128)(2,1)S(1)}, bf16[32,64,128]{2,1,0:T(8,128)(2,1)...) custom-call(s32[1,128]{1,0:T(1,128)S(1)} %get-tuple-element.75.refs_0_, ...), custom_call_target="tpu_custom_call" | custom-call | flops 5100273664 | bytes 14680064 | tf_op jit(solution)/shard_map/cond/branch_1_fun/round_2/pallas_call | solution.py:335
  74.8 0.1 collective-permute-start.25
  74.9 2.6 %collective-permute-start.26 = (bf16[512,512]{1,0:T(8,128)(2,1)S(1)}, bf16[512,512]{1,0:T(8,128)(2,1)S(1)}, u32[]{:S(2)}, u32[]{:S(2)}) collective-permute-start(bf16[512,512]{1,0:T(8,128)(2,1)S(1)} %get-tuple-element.98), channel_id=1, source_target_pairs={{0,28},{4,0},{8,4},{12,8},{16,12},{20,16},{24,20},{28,24},{1,29},{... | collective-permute-start | bytes 1572872 | tf_op jit(solution)/shard_map/cond/branch_1_fun/ppermute | solution.py:268
  77.5 4.7 %collective-permute-start.27 = (bf16[12,64,128]{2,1,0:T(8,128)(2,1)S(1)}, bf16[12,64,128]{2,1,0:T(8,128)(2,1)S(1)}, u32[]{:S(2)}, u32[]{:S(2)}) collective-permute-start(bf16[12,64,128]{2,1,0:T(8,128)(2,1)S(1)} %get-tuple-element.100), channel_id=1, source_target_pairs={{0,1},{1,2},{2,3},{3,0},{4,5},{5,6},{6,7},{7,4},{8,9},{9,10},{10,1... | collective-permute-start | bytes 589832 | tf_op jit(solution)/shard_map/cond/branch_1_fun/ppermute | solution.py:268
  82.2 2.8 %collective-permute-start.28 = (bf16[12,64,128]{2,1,0:T(8,128)(2,1)S(1)}, bf16[12,64,128]{2,1,0:T(8,128)(2,1)S(1)}, u32[]{:S(2)}, u32[]{:S(2)}) collective-permute-start(bf16[12,64,128]{2,1,0:T(8,128)(2,1)S(1)} %get-tuple-element.101), channel_id=1, source_target_pairs={{0,2},{1,3},{2,0},{3,1},{4,6},{5,7},{6,4},{7,5},{8,10},{9,11},{10,... | collective-permute-start | bytes 589832 | tf_op jit(solution)/shard_map/cond/branch_1_fun/ppermute | solution.py:268
  85.0 5.3 %collective-permute-done.27.refs_6_ = bf16[12,64,128]{2,1,0:T(8,128)(2,1)S(1)} collective-permute-done((bf16[12,64,128]{2,1,0:T(8,128)(2,1)S(1)}, bf16[12,64,128]{2,1,0:T(8,128)(2,1)S(1)}, u32[]{:S(2)}, u32[]{:S(2)}) %collective-permute-start.27) | collective-permute-done | bytes 196640 | tf_op jit(solution)/shard_map/cond/branch_1_fun/ppermute | solution.py:268
  90.4 6.6 %collective-permute-done.28.refs_7_ = bf16[12,64,128]{2,1,0:T(8,128)(2,1)S(1)} collective-permute-done((bf16[12,64,128]{2,1,0:T(8,128)(2,1)S(1)}, bf16[12,64,128]{2,1,0:T(8,128)(2,1)S(1)}, u32[]{:S(2)}, u32[]{:S(2)}) %collective-permute-start.28) | collective-permute-done | bytes 196640 | tf_op jit(solution)/shard_map/cond/branch_1_fun/ppermute | solution.py:268
  97.0 11.0 %round_3.3 = (f32[16,128]{1,0:T(8,128)S(1)}, f32[16,128]{1,0:T(8,128)S(1)}) custom-call(s32[1,128]{1,0:T(1,128)S(1)} %get-tuple-element.75.refs_0_, s32[8,128]{1,0:T(8,128)S(1)} %get-tuple-element.76.lists_ref.refs_1_, bf16[1024,512]{1,0:T(8,128)(2,1)} %get-tuple-element.138.refs_2_, bf16[512,512]{1,0:T(8,128)(2,1)S(1)} %collective-permute-done.25.refs_3_, ...), custom_call_target="tpu_custom_call" | custom-call | flops 5100273664 | bytes 14680064 | tf_op jit(solution)/shard_map/cond/branch_1_fun/round_3/pallas_call | solution.py:335
  108.1 0.1 collective-permute-start.33
  108.1 1.2 collective-permute-done.33
  109.3 0.5 collective-permute-start.34
  109.8 3.3 %collective-permute-done.34 = f32[32,128]{1,0:T(8,128)S(1)} collective-permute-done((f32[32,128]{1,0:T(8,128)S(1)}, f32[32,128]{1,0:T(8,128)S(1)}, u32[]{:S(2)}, u32[]{:S(2)}) %collective-permute-start.34) | collective-permute-done | bytes 16416 | tf_op jit(solution)/shard_map/ppermute | solution.py:277
  113.1 0.5 collective-permute-start.35
  113.6 3.2 %collective-permute-done.35 = f32[32,128]{1,0:T(8,128)S(1)} collective-permute-done((f32[32,128]{1,0:T(8,128)S(1)}, f32[32,128]{1,0:T(8,128)S(1)}, u32[]{:S(2)}, u32[]{:S(2)}) %collective-permute-start.35) | collective-permute-done | bytes 16416 | tf_op jit(solution)/shard_map/ppermute | solution.py:277
  116.8 4.7 %collective-permute-start.36 = (f32[32,128]{1,0:T(8,128)S(1)}, f32[32,128]{1,0:T(8,128)S(1)}, u32[]{:S(2)}, u32[]{:S(2)}) collective-permute-start(f32[32,128]{1,0:T(8,128)S(1)} %add.142), channel_id=1, source_target_pairs={{0,1},{1,0},{2,3},{3,2},{4,5},{5,4},{6,7},{7,6},{8,9},{9,8},{10,11... | collective-permute-start | bytes 49160 | tf_op jit(solution)/shard_map/ppermute | solution.py:277
  121.5 1.7 %collective-permute-done.36 = f32[32,128]{1,0:T(8,128)S(1)} collective-permute-done((f32[32,128]{1,0:T(8,128)S(1)}, f32[32,128]{1,0:T(8,128)S(1)}, u32[]{:S(2)}, u32[]{:S(2)}) %collective-permute-start.36) | collective-permute-done | bytes 16416 | tf_op jit(solution)/shard_map/ppermute | solution.py:277
  123.2 1.0 collective-permute-start.37
  124.2 3.6 %collective-permute-done.37 = f32[32,128]{1,0:T(8,128)S(1)} collective-permute-done((f32[32,128]{1,0:T(8,128)S(1)}, f32[32,128]{1,0:T(8,128)S(1)}, u32[]{:S(2)}, u32[]{:S(2)}) %collective-permute-start.37) | collective-permute-done | bytes 16416 | tf_op jit(solution)/shard_map/ppermute | solution.py:277
  127.8 0.6 fusion.16
  (27 shorter events, 0.1 us)
Async XLA Ops:
  1.6 9.5 %collective-permute-start.32 = (s32[32,128]{1,0:T(8,128)S(1)}, s32[32,128]{1,0:T(8,128)S(1)}, u32[]{:S(2)}, u32[]{:S(2)}) collective-permute-start(s32[32,128]{1,0:T(8,128)S(1)} %broadcast_in_dim.19.refs_0_), channel_id=1, source_target_pairs={{0,1},{1,2},{2,3},{3,0},{4,5},{5,6},{6,7},{7,4},{8,9},{9,10},{10,1... | collective-permute-start | bytes 49160 | tf_op jit(solution)/shard_map/ppermute | solution.py:268
  4.6 6.5 %collective-permute-start.31 = (s32[32,128]{1,0:T(8,128)S(1)}, s32[32,128]{1,0:T(8,128)S(1)}, u32[]{:S(2)}, u32[]{:S(2)}) collective-permute-start(s32[32,128]{1,0:T(8,128)S(1)} %broadcast_in_dim.19.refs_0_), channel_id=1, source_target_pairs={{0,2},{1,3},{2,0},{3,1},{4,6},{5,7},{6,4},{7,5},{8,10},{9,11},{10,... | collective-permute-start | bytes 49160 | tf_op jit(solution)/shard_map/ppermute | solution.py:268
  7.2 3.9 %collective-permute-start.30 = (s32[32,128]{1,0:T(8,128)S(1)}, s32[32,128]{1,0:T(8,128)S(1)}, u32[]{:S(2)}, u32[]{:S(2)}) collective-permute-start(s32[32,128]{1,0:T(8,128)S(1)} %broadcast_in_dim.19.refs_0_), channel_id=1, source_target_pairs={{0,3},{1,0},{2,1},{3,2},{4,7},{5,4},{6,5},{7,6},{8,11},{9,8},{10,9... | collective-permute-start | bytes 49160 | tf_op jit(solution)/shard_map/ppermute | solution.py:268
  11.8 19.8 %collective-permute-start.15 = (bf16[512,512]{1,0:T(8,128)(2,1)}, bf16[512,512]{1,0:T(8,128)(2,1)S(1)}, u32[]{:S(2)}, u32[]{:S(2)}) collective-permute-start(bf16[512,512]{1,0:T(8,128)(2,1)} %get-tuple-element.78), channel_id=1, source_target_pairs={{0,4},{4,8},{8,12},{12,16},{16,20},{20,24},{24,28},{28,0},{1,5},{5... | collective-permute-start | bytes 1572872 | tf_op jit(solution)/shard_map/cond/branch_1_fun/ppermute | solution.py:268
  11.9 19.7 %collective-permute-start.16 = (bf16[512,512]{1,0:T(8,128)(2,1)S(1)}, bf16[512,512]{1,0:T(8,128)(2,1)S(1)}, u32[]{:S(2)}, u32[]{:S(2)}) collective-permute-start(bf16[512,512]{1,0:T(8,128)(2,1)S(1)} %get-tuple-element.79), channel_id=1, source_target_pairs={{0,28},{4,0},{8,4},{12,8},{16,12},{20,16},{24,20},{28,24},{1,29},{... | collective-permute-start | bytes 1572872 | tf_op jit(solution)/shard_map/cond/branch_1_fun/ppermute | solution.py:268
  15.4 9.7 %collective-permute-start.17 = (bf16[12,64,128]{2,1,0:T(8,128)(2,1)S(1)}, bf16[12,64,128]{2,1,0:T(8,128)(2,1)S(1)}, u32[]{:S(2)}, u32[]{:S(2)}) collective-permute-start(bf16[12,64,128]{2,1,0:T(8,128)(2,1)S(1)} %get-tuple-element.81), channel_id=1, source_target_pairs={{0,1},{1,2},{2,3},{3,0},{4,5},{5,6},{6,7},{7,4},{8,9},{9,10},{10,1... | collective-permute-start | bytes 589832 | tf_op jit(solution)/shard_map/cond/branch_1_fun/ppermute | solution.py:268
  16.1 15.5 %collective-permute-start.18 = (bf16[12,64,128]{2,1,0:T(8,128)(2,1)S(1)}, bf16[12,64,128]{2,1,0:T(8,128)(2,1)S(1)}, u32[]{:S(2)}, u32[]{:S(2)}) collective-permute-start(bf16[12,64,128]{2,1,0:T(8,128)(2,1)S(1)} %get-tuple-element.82), channel_id=1, source_target_pairs={{0,2},{1,3},{2,0},{3,1},{4,6},{5,7},{6,4},{7,5},{8,10},{9,11},{10,... | collective-permute-start | bytes 589832 | tf_op jit(solution)/shard_map/cond/branch_1_fun/ppermute | solution.py:268
  19.0 12.6 %collective-permute-start.19 = (bf16[12,64,128]{2,1,0:T(8,128)(2,1)S(1)}, bf16[12,64,128]{2,1,0:T(8,128)(2,1)S(1)}, u32[]{:S(2)}, u32[]{:S(2)}) collective-permute-start(bf16[12,64,128]{2,1,0:T(8,128)(2,1)S(1)} %get-tuple-element.83), channel_id=1, source_target_pairs={{0,3},{1,0},{2,1},{3,2},{4,7},{5,4},{6,5},{7,6},{8,11},{9,8},{10,9... | collective-permute-start | bytes 589832 | tf_op jit(solution)/shard_map/cond/branch_1_fun/ppermute | solution.py:268
  31.6 31.8 %copy-start.1 = (bf16[1024,512]{1,0:T(8,128)(2,1)S(1)}, bf16[1024,512]{1,0:T(8,128)(2,1)}, u32[]{:S(2)}) copy-start(bf16[1024,512]{1,0:T(8,128)(2,1)} %get-tuple-element.77.refs_2_.refs_13_) | copy-start | bytes 3145732 | tf_op jit(solution)/shard_map/cond
  31.7 31.8 %copy-start.3 = (bf16[8,512,512]{2,1,0:T(8,128)(2,1)S(1)}, bf16[8,512,512]{2,1,0:T(8,128)(2,1)}, u32[]{:S(2)}) copy-start(bf16[8,512,512]{2,1,0:T(8,128)(2,1)} %get-tuple-element.84.refs_9_) | copy-start | bytes 12582916 | tf_op jit(solution)/shard_map/cond
  31.7 31.8 %copy-start.5 = (bf16[4096,512]{1,0:T(8,128)(2,1)S(1)}, bf16[4096,512]{1,0:T(8,128)(2,1)}, u32[]{:S(2)}) copy-start(bf16[4096,512]{1,0:T(8,128)(2,1)} %get-tuple-element.86.refs_11_) | copy-start | bytes 12582916 | tf_op jit(solution)/shard_map/cond
  44.3 19.1 %collective-permute-start.20 = (bf16[512,512]{1,0:T(8,128)(2,1)S(1)}, bf16[512,512]{1,0:T(8,128)(2,1)S(1)}, u32[]{:S(2)}, u32[]{:S(2)}) collective-permute-start(bf16[512,512]{1,0:T(8,128)(2,1)S(1)} %get-tuple-element.89), channel_id=1, source_target_pairs={{0,4},{4,8},{8,12},{12,16},{16,20},{20,24},{24,28},{28,0},{1,5},{5... | collective-permute-start | bytes 1572872 | tf_op jit(solution)/shard_map/cond/branch_1_fun/ppermute | solution.py:268
  44.4 19.1 %collective-permute-start.21 = (bf16[512,512]{1,0:T(8,128)(2,1)S(1)}, bf16[512,512]{1,0:T(8,128)(2,1)S(1)}, u32[]{:S(2)}, u32[]{:S(2)}) collective-permute-start(bf16[512,512]{1,0:T(8,128)(2,1)S(1)} %get-tuple-element.90), channel_id=1, source_target_pairs={{0,28},{4,0},{8,4},{12,8},{16,12},{20,16},{24,20},{28,24},{1,29},{... | collective-permute-start | bytes 1572872 | tf_op jit(solution)/shard_map/cond/branch_1_fun/ppermute | solution.py:268
  47.0 9.7 %collective-permute-start.22 = (bf16[12,64,128]{2,1,0:T(8,128)(2,1)S(1)}, bf16[12,64,128]{2,1,0:T(8,128)(2,1)S(1)}, u32[]{:S(2)}, u32[]{:S(2)}) collective-permute-start(bf16[12,64,128]{2,1,0:T(8,128)(2,1)S(1)} %get-tuple-element.92), channel_id=1, source_target_pairs={{0,1},{1,2},{2,3},{3,0},{4,5},{5,6},{6,7},{7,4},{8,9},{9,10},{10,1... | collective-permute-start | bytes 589832 | tf_op jit(solution)/shard_map/cond/branch_1_fun/ppermute | solution.py:268
  51.4 12.1 %collective-permute-start.23 = (bf16[12,64,128]{2,1,0:T(8,128)(2,1)S(1)}, bf16[12,64,128]{2,1,0:T(8,128)(2,1)S(1)}, u32[]{:S(2)}, u32[]{:S(2)}) collective-permute-start(bf16[12,64,128]{2,1,0:T(8,128)(2,1)S(1)} %get-tuple-element.93), channel_id=1, source_target_pairs={{0,2},{1,3},{2,0},{3,1},{4,6},{5,7},{6,4},{7,5},{8,10},{9,11},{10,... | collective-permute-start | bytes 589832 | tf_op jit(solution)/shard_map/cond/branch_1_fun/ppermute | solution.py:268
  51.5 12.0 %collective-permute-start.24 = (bf16[12,64,128]{2,1,0:T(8,128)(2,1)S(1)}, bf16[12,64,128]{2,1,0:T(8,128)(2,1)S(1)}, u32[]{:S(2)}, u32[]{:S(2)}) collective-permute-start(bf16[12,64,128]{2,1,0:T(8,128)(2,1)S(1)} %get-tuple-element.94), channel_id=1, source_target_pairs={{0,3},{1,0},{2,1},{3,2},{4,7},{5,4},{6,5},{7,6},{8,11},{9,8},{10,9... | collective-permute-start | bytes 589832 | tf_op jit(solution)/shard_map/cond/branch_1_fun/ppermute | solution.py:268
  74.8 22.2 %collective-permute-start.25 = (bf16[512,512]{1,0:T(8,128)(2,1)S(1)}, bf16[512,512]{1,0:T(8,128)(2,1)S(1)}, u32[]{:S(2)}, u32[]{:S(2)}) collective-permute-start(bf16[512,512]{1,0:T(8,128)(2,1)S(1)} %get-tuple-element.97), channel_id=1, source_target_pairs={{0,4},{4,8},{8,12},{12,16},{16,20},{20,24},{24,28},{28,0},{1,5},{5... | collective-permute-start | bytes 1572872 | tf_op jit(solution)/shard_map/cond/branch_1_fun/ppermute | solution.py:268
  74.9 22.1 %collective-permute-start.26 = (bf16[512,512]{1,0:T(8,128)(2,1)S(1)}, bf16[512,512]{1,0:T(8,128)(2,1)S(1)}, u32[]{:S(2)}, u32[]{:S(2)}) collective-permute-start(bf16[512,512]{1,0:T(8,128)(2,1)S(1)} %get-tuple-element.98), channel_id=1, source_target_pairs={{0,28},{4,0},{8,4},{12,8},{16,12},{20,16},{24,20},{28,24},{1,29},{... | collective-permute-start | bytes 1572872 | tf_op jit(solution)/shard_map/cond/branch_1_fun/ppermute | solution.py:268
  77.5 12.9 %collective-permute-start.27 = (bf16[12,64,128]{2,1,0:T(8,128)(2,1)S(1)}, bf16[12,64,128]{2,1,0:T(8,128)(2,1)S(1)}, u32[]{:S(2)}, u32[]{:S(2)}) collective-permute-start(bf16[12,64,128]{2,1,0:T(8,128)(2,1)S(1)} %get-tuple-element.100), channel_id=1, source_target_pairs={{0,1},{1,2},{2,3},{3,0},{4,5},{5,6},{6,7},{7,4},{8,9},{9,10},{10,1... | collective-permute-start | bytes 589832 | tf_op jit(solution)/shard_map/cond/branch_1_fun/ppermute | solution.py:268
  82.2 14.8 %collective-permute-start.28 = (bf16[12,64,128]{2,1,0:T(8,128)(2,1)S(1)}, bf16[12,64,128]{2,1,0:T(8,128)(2,1)S(1)}, u32[]{:S(2)}, u32[]{:S(2)}) collective-permute-start(bf16[12,64,128]{2,1,0:T(8,128)(2,1)S(1)} %get-tuple-element.101), channel_id=1, source_target_pairs={{0,2},{1,3},{2,0},{3,1},{4,6},{5,7},{6,4},{7,5},{8,10},{9,11},{10,... | collective-permute-start | bytes 589832 | tf_op jit(solution)/shard_map/cond/branch_1_fun/ppermute | solution.py:268
  85.0 12.0 %collective-permute-start.29 = (bf16[12,64,128]{2,1,0:T(8,128)(2,1)S(1)}, bf16[12,64,128]{2,1,0:T(8,128)(2,1)S(1)}, u32[]{:S(2)}, u32[]{:S(2)}) collective-permute-start(bf16[12,64,128]{2,1,0:T(8,128)(2,1)S(1)} %get-tuple-element.102), channel_id=1, source_target_pairs={{0,3},{1,0},{2,1},{3,2},{4,7},{5,4},{6,5},{7,6},{8,11},{9,8},{10,9... | collective-permute-start | bytes 589832 | tf_op jit(solution)/shard_map/cond/branch_1_fun/ppermute | solution.py:268
  108.1 1.2 collective-permute-start.33
  109.3 3.7 %collective-permute-start.34 = (f32[32,128]{1,0:T(8,128)S(1)}, f32[32,128]{1,0:T(8,128)S(1)}, u32[]{:S(2)}, u32[]{:S(2)}) collective-permute-start(f32[32,128]{1,0:T(8,128)S(1)} %add.140), channel_id=1, source_target_pairs={{0,8},{4,12},{8,0},{12,4},{16,24},{20,28},{24,16},{28,20},{1,9},{5... | collective-permute-start | bytes 49160 | tf_op jit(solution)/shard_map/ppermute | solution.py:277
  113.1 3.7 %collective-permute-start.35 = (f32[32,128]{1,0:T(8,128)S(1)}, f32[32,128]{1,0:T(8,128)S(1)}, u32[]{:S(2)}, u32[]{:S(2)}) collective-permute-start(f32[32,128]{1,0:T(8,128)S(1)} %add.141), channel_id=1, source_target_pairs={{0,16},{4,20},{8,24},{12,28},{16,0},{20,4},{24,8},{28,12},{1,17},{... | collective-permute-start | bytes 49160 | tf_op jit(solution)/shard_map/ppermute | solution.py:277
  116.8 6.4 %collective-permute-start.36 = (f32[32,128]{1,0:T(8,128)S(1)}, f32[32,128]{1,0:T(8,128)S(1)}, u32[]{:S(2)}, u32[]{:S(2)}) collective-permute-start(f32[32,128]{1,0:T(8,128)S(1)} %add.142), channel_id=1, source_target_pairs={{0,1},{1,0},{2,3},{3,2},{4,5},{5,4},{6,7},{7,6},{8,9},{9,8},{10,11... | collective-permute-start | bytes 49160 | tf_op jit(solution)/shard_map/ppermute | solution.py:277
  123.2 4.6 %collective-permute-start.37 = (f32[32,128]{1,0:T(8,128)S(1)}, f32[32,128]{1,0:T(8,128)S(1)}, u32[]{:S(2)}, u32[]{:S(2)}) collective-permute-start(f32[32,128]{1,0:T(8,128)S(1)} %add.143), channel_id=1, source_target_pairs={{0,2},{1,3},{2,0},{3,1},{4,6},{5,7},{6,4},{7,5},{8,10},{9,11},{10,... | collective-permute-start | bytes 49160 | tf_op jit(solution)/shard_map/ppermute | solution.py:277

commit v2 on v1

v2 whole, which is shorter than its diff:
```python
import functools

import jax
import jax.numpy as jnp
from jax import lax
from jax.experimental import pallas as pl
from jax.experimental.pallas import tpu as pltpu
from jax.sharding import PartitionSpec as P

P_SIZE = 8
F = 4
HW = 4
TR = P_SIZE * P_SIZE
LANES = 128
CAPS = (9, 12)
ROW_TILE = 256
UNROLL = 8
NEAR = 2

shift_center = 0.3
half_width = 1.2

VMEM = pl.BlockSpec(memory_space=pltpu.VMEM)
SMEM = pl.BlockSpec(memory_space=pltpu.SMEM)
ANY = pl.BlockSpec(memory_space=pl.ANY)
bf16 = jnp.bfloat16
f32 = jnp.float32


def dot(a, b):
    return jnp.dot(a, b, preferred_element_type=f32)


def trace_selector(block):
    node = lax.broadcasted_iota(jnp.int32, (block, F * TR), 0)
    column = lax.broadcasted_iota(jnp.int32, (block, F * TR), 1)
    face, entry = column // TR, column % TR
    major, minor = entry // P_SIZE, entry % P_SIZE
    fixed = jnp.where(face % 2 == 0, 0, P_SIZE - 1)
    on_i = fixed * TR + major * P_SIZE + minor
    on_j = major * TR + fixed * P_SIZE + minor
    return (node == jnp.where(face < 2, on_i, on_j)).astype(bf16)


def left_half(shape):
    return lax.broadcasted_iota(jnp.int32, shape, len(shape) - 1) < TR


def read_wide(ref, index):
    return jnp.concatenate([ref[k, index, :] for k in range(ref.shape[0])], axis=1)


def write_wide(ref, index, value):
    for k in range(ref.shape[0]):
        ref[k, index, :] = value[:, k * LANES : (k + 1) * LANES]


def of_element(ref, e, elements):
    return pl.ds(e, ref.shape[1] // elements, stride=elements)


def store_traces(e, values, traces_ref):
    half = values.shape[0] // 2
    for pair in range(F // 2):
        a = values[:half, pair * LANES : (pair + 1) * LANES]
        b = values[half:, pair * LANES : (pair + 1) * LANES]
        left = left_half(a.shape)
        traces_ref[e * F + 2 * pair] = jnp.where(left, a, pltpu.roll(b, TR, 1)).astype(bf16)
        traces_ref[e * F + 2 * pair + 1] = jnp.where(left, pltpu.roll(a, TR, 1), b).astype(bf16)


def aligned(value, multiple):
    return value if isinstance(value, int) else pl.multiple_of(value, multiple)


def each(count, body, unroll=1):
    def step(i, carry):
        body(i)
        return carry

    if unroll >= count:
        for i in range(count):
            body(i)
        return
    lax.fori_loop(0, count, step, 0, unroll=unroll)


def each_tile(rows, tile, body):
    each(rows // tile, lambda i: body(pl.ds(aligned(i * tile, tile), tile)))


def pick_traces(lists_ref, traces_ref, sent_refs):
    for r, sent in enumerate(sent_refs):

        def body(j, r=r, sent=sent):
            sent[j] = traces_ref[lists_ref[r, j]]

        each(sent.shape[0], body)


def lifted_rows(e, refs_ref, traces_ref, arrived_refs):
    per = traces_ref.shape[0]
    slots = []
    for f in range(F):
        code = refs_ref[0, e * F + f]
        source, place = code // per, code % per
        value = jnp.where(source == 0, traces_ref[place].astype(f32), 0.0)
        for shift, arrived in enumerate(arrived_refs):
            here = source == shift + 1
            value = jnp.where(here, arrived[jnp.where(here, place, 0)].astype(f32), value)
        slots.append(value)
    tops, bottoms = [], []
    for pair in range(F // 2):
        a, b = slots[2 * pair], slots[2 * pair + 1]
        left = left_half(a.shape)
        tops.append(jnp.where(left, a, pltpu.roll(b, TR, 1)))
        bottoms.append(jnp.where(left, pltpu.roll(a, TR, 1), b))
    both = jnp.concatenate([jnp.concatenate(tops, 1), jnp.concatenate(bottoms, 1)], 0)
    return both.astype(bf16)


def opening_kernel(elements, unroll, start_ref, selector_ref, low_ref, high_ref, traces_ref, wide):
    rows = start_ref.shape[0]
    edge = low_ref.shape[0]
    low_ref[...] = start_ref[:edge]
    high_ref[...] = start_ref[rows - edge :]

    def widen(index):
        write_wide(wide, index, start_ref[index].astype(f32))

    each_tile(rows, ROW_TILE, widen)

    def element(e):
        own = read_wide(wide, of_element(wide, e, elements)).astype(bf16)
        store_traces(e, dot(own, selector_ref[...]), traces_ref)

    each(elements, element, unroll)


def picking_kernel(lists_ref, traces_ref, *sent_refs):
    pick_traces(lists_ref, traces_ref, sent_refs)


def paired(shards):
    return shards & (shards - 1) == 0


def asker_of(me, r, shards):
    return me ^ r if paired(shards) else lax.rem(me + r, shards)


def permute_of(asker, owner, shards):
    return asker ^ owner if paired(shards) else lax.rem(asker + shards - owner, shards)


def pattern_kernel(*refs):
    codes_refs, (me_ref, lists_ref, places_ref, level_ref) = refs[:-4], refs[-4:]
    shards = len(codes_refs)
    per = codes_refs[0].shape[0]
    every = shards * per
    me = me_ref[0]
    lane = lax.broadcasted_iota(jnp.int32, (per, every), 1)
    asked = [codes[:, :1] == lane for codes in codes_refs]
    need = jnp.concatenate(
        [jnp.max(a.astype(f32), axis=0, keepdims=True) for a in asked]
        + [jnp.zeros((8 - shards % 8, every), f32)] * (shards % 8 != 0),
        axis=0,
    ).astype(bf16)
    row = lax.broadcasted_iota(jnp.int32, (every, every), 0)
    column = lax.broadcasted_iota(jnp.int32, (every, every), 1)
    same = row // per == column // per
    before = (same & (row < column)).astype(bf16)
    rank = dot(need, before)
    total = dot(need, same.astype(bf16))
    over = (((0,), (1,)), ((), ()))
    rank_down = lax.dot_general(before, need, over, preferred_element_type=f32)
    need_down = lax.dot_general((row == column).astype(bf16), need, over, preferred_element_type=f32)
    owner = lax.broadcasted_iota(jnp.int32, total.shape, 1) // per
    number = lax.broadcasted_iota(jnp.int32, total.shape, 0)
    permute = permute_of(asker_of(me, number, shards), owner, shards)
    weighed = jnp.where(permute == 1, total * (1.0 / NEAR), total)
    weighed = jnp.where((permute == 0) | (number >= shards), 0.0, weighed)
    most = jnp.max(jnp.max(weighed, axis=1, keepdims=True), axis=0, keepdims=True)
    level = sum((most > cap).astype(jnp.int32) for cap in CAPS)
    level_ref[...] = jnp.broadcast_to(level, level_ref.shape)
    trace = lax.broadcasted_iota(jnp.int32, (every, LANES), 0)
    slot = lax.broadcasted_iota(jnp.int32, (every, LANES), 1)
    mine = trace // per == me
    lists_ref[...] = jnp.zeros_like(lists_ref)
    for r in range(1, shards):
        sent = mine & (need_down[:, r : r + 1] > 0.5) & (rank_down[:, r : r + 1].astype(jnp.int32) == slot)
        listed = jnp.sum(jnp.where(sent, (trace - me * per).astype(f32), 0.0), axis=0, keepdims=True)
        lists_ref[r - 1 : r, :] = listed.astype(jnp.int32)
    source = permute_of(me, lane // per, shards)
    place = jnp.where(source == 0, lane % per, rank[:1].astype(jnp.int32))
    code = jnp.where(asked[0], source * per + place, 0).astype(f32)
    found = jnp.sum(code, axis=1, keepdims=True)
    hit = jnp.sum(asked[0].astype(f32), axis=1, keepdims=True)
    found = jnp.where(hit > 0.5, found, float(every))
    down = lax.broadcasted_iota(jnp.int32, (per, LANES), 0)
    across = lax.broadcasted_iota(jnp.int32, (per, LANES), 1)
    turned = jnp.sum(jnp.where(down == across, jnp.broadcast_to(found, (per, LANES)), 0.0), axis=0, keepdims=True)
    places_ref[...] = turned.astype(jnp.int32)


def add_to(acc_ref, index, value):
    write_wide(acc_ref, index, read_wide(acc_ref, index) + value)


def near_kernel(step, layer, elements, unroll, *refs):
    if step == 2:
        here_ref, diag_ref, axial_ref, start_ref, acc_ref, wide = refs
    elif step == 3:
        here_ref, diag_ref, axial_ref, acc_ref, gram_ref, wide = refs
    else:
        here_ref, diag_ref, axial_ref, acc_ref, wide = refs
    rows, block = here_ref.shape
    tile = 2 * layer
    if step == 3:
        gram_ref[...] = jnp.zeros_like(gram_ref)

    def widen(i):
        index = pl.ds(aligned(i * tile, tile), tile)
        write_wide(wide, index, here_ref[index, :].astype(f32))

    each(rows // tile, widen)

    def element(e):
        index = of_element(wide, e, elements)
        own = read_wide(wide, index).astype(bf16)
        write_wide(acc_ref, index, dot(own, diag_ref[e]))
        if step == 3:
            gram_ref[...] += across(own, own)

    each(elements, element, unroll)

    layers = rows // layer
    for offset in [*range(-HW, 0), *range(1, HW + 1)]:
        if abs(offset) < layers:
            begin, end = max(0, -offset) * layer, (layers - max(0, offset)) * layer
            position = (offset + HW - (offset > 0)) * block
            values = here_ref[begin + offset * layer : end + offset * layer]
            add_to(acc_ref, slice(begin, end), dot(values, axial_ref[position : position + block]))

    if step != 3:

        def along(i):
            index = pl.ds(aligned(i * tile, tile), tile)
            total = read_wide(acc_ref, index) - shift_center * read_wide(wide, index)
            if step == 2:
                total -= (half_width / 2.0) * start_ref[index, :].astype(f32)
            write_wide(acc_ref, index, total)

        each(rows // tile, along)


def middle_kernel(layer, near_ref, low_ref, high_ref, axial_ref, acc_ref):
    del near_ref
    edge, block = low_ref.shape
    rows = acc_ref.shape[1]
    for reach in range(1, HW + 1):
        far = reach * layer
        below = dot(low_ref[edge - far :], axial_ref[(HW - reach) * block : (HW - reach + 1) * block])
        add_to(acc_ref, slice(0, far), below)
        above = dot(high_ref[:far], axial_ref[(HW + reach - 1) * block : (HW + reach) * block])
        add_to(acc_ref, slice(rows - far, rows), above)


def across(a, b):
    return lax.dot_general(a, b, (((1,), (1,)), ((), ())), preferred_element_type=f32)


def far_kernel(step, shards, elements, unroll, *refs):
    refs = list(refs)
    take = lambda n: [refs.pop(0) for _ in range(n)]
    places_ref, lists_ref, near_ref, traces_ref = take(4)
    arrived_refs = take(shards - 1)
    (face_ref,) = take(1)
    if step == 3:
        here_ref, gram_ref, out_ref, wide, projected = take(5)
        projected[...] = jnp.zeros_like(projected)

        def widen(index):
            write_wide(wide, index, here_ref[index, :].astype(f32))

        each_tile(here_ref.shape[0], ROW_TILE, widen)
    else:
        selector_ref, out_ref, out_low_ref, out_high_ref, out_traces_ref = take(5)
        sent_refs = take(shards - 1)
        (wide,) = take(1)
    scale = {1: 1.0 / half_width, 2: 2.0 / half_width, 3: 1.0}[step]

    def element(e):
        index = of_element(wide, e, elements)
        lifted = lifted_rows(e, places_ref, traces_ref, arrived_refs)
        total = (read_wide(near_ref, index) + dot(lifted, face_ref[e])) * scale
        if step == 3:
            own = read_wide(wide, index).astype(bf16)
            upper = total.astype(bf16)
            lower = (total - upper.astype(f32)).astype(bf16)
            projected[...] += across(own, upper) + across(own, lower)
            return
        new = total.astype(bf16)
        write_wide(wide, index, new.astype(f32))
        store_traces(e, dot(new, selector_ref[...]), out_traces_ref)

    each(elements, element, unroll)
    if step != 3:
        rows = out_ref.shape[0]
        edge = out_low_ref.shape[0]
        pick_traces(lists_ref, out_traces_ref, sent_refs)

        def narrow(index):
            out_ref[index, :] = read_wide(wide, index).astype(bf16)

        each_tile(rows, ROW_TILE, narrow)
        out_low_ref[...] = out_ref[:edge]
        out_high_ref[...] = out_ref[rows - edge :]
        return

    size = projected.shape[0]
    vectors = out_ref.shape[0] // 2
    down = lax.broadcasted_iota(jnp.int32, (size, size), 0)
    over = lax.broadcasted_iota(jnp.int32, (size, size), 1)
    keep = down // vectors == over // vectors
    group = (
        lax.broadcasted_iota(jnp.int32, (size, LANES), 0) % vectors
        == lax.broadcasted_iota(jnp.int32, (size, LANES), 1)
    ).astype(f32)
    for place, ref in enumerate((gram_ref, projected)):
        value = jnp.where(keep, ref[...], 0.0).reshape(size // vectors, vectors, size).sum(0)
        value = jnp.dot(value, group, precision=lax.Precision.HIGHEST, preferred_element_type=f32)
        out_ref[place * vectors : (place + 1) * vectors] = value


def shape(dims, dtype=bf16):
    return jax.ShapeDtypeStruct(dims, dtype)


def params(rows):
    return pltpu.CompilerParams(vmem_limit_bytes=14 * 2**20 + rows * 12 * 2**10)


def rotate(value, axis, shift):
    count = lax.axis_size(axis)
    return lax.ppermute(value, axis, [(i, (i + shift) % count) for i in range(count)])


def send_traces(value, r):
    count = lax.axis_size("xs")
    if paired(count):
        return lax.ppermute(value, "xs", [(i, i ^ r) for i in range(count)])
    return rotate(value, "xs", r)


def add_over(value, axis):
    count = lax.axis_size(axis)
    if not paired(count):
        return lax.psum(value, axis)
    step = 1
    while step < count:
        far = lambda distance: lax.ppermute(value, axis, [(i, i ^ distance) for i in range(count)])
        if (count // step).bit_length() % 2 == 0:
            value = value + far(step)
            step *= 2
        else:
            value = (value + far(step)) + (far(2 * step) + far(3 * step))
            step *= 4
    return value


def local(start_vectors, diag_blocks, face_blocks, axial_blocks, neighbor_ids, neighbor_face, face_mask):
    layers, vectors, elements, block = start_vectors.shape
    shards = lax.axis_size("xs")
    me = lax.axis_index("xs").astype(jnp.int32)
    per = elements * F
    layer = vectors * elements
    rows = layers * layer
    edge = HW * layer
    half = layers * vectors // 2
    wide_rows = (block // LANES, rows, LANES)
    face_flat = face_blocks.reshape(elements, F * TR, block)
    axial_flat = axial_blocks.reshape(2 * HW * block, block)
    selector = trace_selector(block)

    codes = jnp.where(face_mask == 1, neighbor_ids * F + neighbor_face, -1).reshape(per, 1)
    codes = jnp.broadcast_to(codes, (per, LANES)).astype(jnp.int32)
    back = lambda r: send_traces(codes, r if paired(shards) else shards - r)
    all_codes = [codes] + [back(r) for r in range(1, shards)]
    lists, places, level = pl.pallas_call(
        pattern_kernel,
        out_shape=[shape((8, LANES), jnp.int32), shape((1, LANES), jnp.int32), shape((1, LANES), jnp.int32)],
        in_specs=[VMEM] * shards + [SMEM],
        out_specs=[VMEM] * 3,
        compiler_params=params(rows),
        name="pattern",
    )(*all_codes, me.reshape(1))

    start_flat = start_vectors.reshape(rows, block)
    low, high, traces = pl.pallas_call(
        functools.partial(opening_kernel, elements, UNROLL),
        out_shape=[shape((edge, block)), shape((edge, block)), shape((per, half, LANES))],
        in_specs=[VMEM] * 2,
        out_specs=[VMEM] * 3,
        scratch_shapes=[pltpu.VMEM(wide_rows, f32)],
        compiler_params=params(rows),
        name="opening",
    )(start_flat, selector)

    def one_round(step, caps, here, low, high, traces, sent):
        unroll = 1 if min(caps) == per else UNROLL
        arrived = [send_traces(s, r + 1) for r, s in enumerate(sent)]
        from_low = rotate(high, "pipe", 1)
        from_high = rotate(low, "pipe", -1)
        size = layers * vectors
        operands = [here, diag_blocks, axial_flat] + [start_flat] * (step == 2)
        outs = [shape(wide_rows, f32)] + [shape((size, size), f32)] * (step == 3)
        near, *gram = pl.pallas_call(
            functools.partial(near_kernel, step, layer, elements, unroll),
            out_shape=outs,
            in_specs=[VMEM] * len(operands),
            out_specs=[VMEM] * len(outs),
            scratch_shapes=[pltpu.VMEM(wide_rows, f32)],
            compiler_params=params(rows),
            cost_estimate=pl.CostEstimate(flops=14 * rows * block * block, bytes_accessed=10**7, transcendentals=0),
            name=f"near_{step}",
        )(*operands)
        near = pl.pallas_call(
            functools.partial(middle_kernel, layer),
            out_shape=shape(wide_rows, f32),
            in_specs=[VMEM] * 4,
            out_specs=VMEM,
            input_output_aliases={0: 0},
            compiler_params=params(rows),
            cost_estimate=pl.CostEstimate(flops=5 * rows * block * block, bytes_accessed=10**7, transcendentals=0),
            name=f"middle_{step}",
        )(near, from_low, from_high, axial_flat)
        operands = [places, lists, near, traces, *arrived, face_flat]
        scratch = [pltpu.VMEM(wide_rows, f32)]
        if step == 3:
            operands += [here, *gram]
            outs = [shape((2 * vectors, LANES), f32)]
            scratch += [pltpu.VMEM((size, size), f32)]
        else:
            operands += [selector]
            outs = [shape((rows, block)), shape((edge, block)), shape((edge, block)), shape((per, half, LANES))]
            outs += [shape((cap, half, LANES)) for cap in caps]
        return pl.pallas_call(
            functools.partial(far_kernel, step, shards, elements, unroll),
            out_shape=outs,
            in_specs=[SMEM] * 2 + [VMEM] * (len(operands) - 2),
            out_specs=[VMEM] * len(outs),
            scratch_shapes=scratch,
            compiler_params=params(rows),
            cost_estimate=pl.CostEstimate(flops=2 * rows * block * block, bytes_accessed=10**7, transcendentals=0),
            name=f"far_{step}",
        )(*operands)

    def run(cap):
        caps = [min(per, cap * NEAR if r == 0 else cap) for r in range(shards - 1)]
        sent = pl.pallas_call(
            picking_kernel,
            out_shape=[shape((cap, half, LANES)) for cap in caps],
            in_specs=[SMEM, VMEM],
            out_specs=[VMEM] * (shards - 1),
            compiler_params=params(rows),
            name="picking",
        )(lists, traces)
        first, *rest = one_round(1, caps, start_flat, low, high, traces, sent)
        filtered, *rest = one_round(2, caps, first, rest[0], rest[1], rest[2], rest[3:])
        (both,) = one_round(3, caps, filtered, rest[0], rest[1], rest[2], rest[3:])
        return filtered, both

    branches = [functools.partial(run, cap) for cap in (*CAPS, per)]
    filtered, both = lax.switch(level[0, 0], branches)
    both = add_over(add_over(both, "pipe"), "xs")
    count_all = float(layers * lax.axis_size("pipe") * elements * shards * block)
    both = both[:, :vectors] / count_all
    return filtered.reshape(start_vectors.shape), both[:vectors], both[vectors:]


def solution(mesh):
    in_specs = (
        P("pipe", None, "xs", None),
        P("xs", None, None),
        P("xs", None, None, None),
        P(),
        P("xs", None),
        P("xs", None),
        P("xs", None),
    )
    out_specs = (P("pipe", None, "xs", None), P(), P())
    return jax.shard_map(local, mesh=mesh, in_specs=in_specs, out_specs=out_specs, check_vma=False)
```

time: 129 us -> 93.6 us (0.73)
  waiting for transfers between devices: 47 us -> 21.8 us
  starting transfers between devices: 39.9 us -> 32.2 us
  Pallas kernels: 38.7 us -> 36.3 us
    ppermute x18 -> x6, waiting for transfers between devices: 34 us -> 6.24 us  [rotate(): lax.ppermute(value, axis, [(i, (i + shift) % count) for i in range(count)])]
    ppermute x18 -> x6, starting transfers between devices: 33.2 us -> 8.02 us  [rotate(): lax.ppermute(value, axis, [(i, (i + shift) % count) for i in range(count)])]
    ppermute x5 -> x19, starting transfers between devices: 6.76 us -> 24.2 us  [the longest x12 16.2 us: send_traces(): return lax.ppermute(value, 'xs', [(i, i ^ r) for i in range(count)])]
    ppermute x5 -> x19, waiting for transfers between devices: 13 us -> 15.6 us  [the longest x12 9.69 us: send_traces(): return lax.ppermute(value, 'xs', [(i, i ^ r) for i in range(count)])]
    pallas_call x5 -> x11, Pallas kernels: 38.2 us -> 35.8 us  [the longest x3 18.5 us: one_round(): pl.pallas_call(functools.partial(near_kernel, step, layer, elements, unro...]
  transfers between devices with their start and end apart: 23 -> 25, of which waited for: 11 -> 12; matrix products, arithmetic and copies ran while one was open for 0% -> 0% of each run, Pallas kernels for 3% -> 28%
where the time goes in v2:
time: 93.6 us; the launch traced here: 93.4 us
  Pallas kernels  36.3 us (39%)
  starting transfers between devices  32.2 us (34%)
  waiting for transfers between devices  21.8 us (23%)
    pallas_call x3, Pallas kernels, one_round(): pl.pallas_call(functools.partial(near_kernel, step, layer, elements, unro...  18.5 us
    ppermute x12, starting transfers between devices, send_traces(): return lax.ppermute(value, 'xs', [(i, i ^ r) for i in range(count)])  16.2 us
    pallas_call x3, Pallas kernels, one_round(): pl.pallas_call(functools.partial(far_kernel, step, shards, elements, unro...  9.89 us
    ppermute x12, waiting for transfers between devices, send_traces(): return lax.ppermute(value, 'xs', [(i, i ^ r) for i in range(count)])  9.69 us
    ppermute x6, starting transfers between devices, rotate(): lax.ppermute(value, axis, [(i, (i + shift) % count) for i in range(count)])  8.02 us
    ppermute x7, starting transfers between devices, add_over(): lax.ppermute(value, axis, [(i, i ^ distance) for i in range(count)])  8.01 us
    ppermute x6, waiting for transfers between devices, rotate(): lax.ppermute(value, axis, [(i, (i + shift) % count) for i in range(count)])  6.24 us
    ppermute x7, waiting for transfers between devices, add_over(): lax.ppermute(value, axis, [(i, i ^ distance) for i in range(count)])  5.87 us
  transfers between devices with their start and end apart: 25, of which 12 were waited for; matrix products, arithmetic and copies ran while one was open for 0% of the time, Pallas kernels for 28%

profile of v2, /device:TPU:0, one launch (start us, length us, event | category | flops | bytes accessed | tf_op | source)
XLA Modules:
  0.0 93.4 jit_solution(14861935559224411573)
XLA Ops:
  0.6 0.7 add_select_fusion.3
  1.4 0.1 copy.20
  1.4 0.1 broadcast_in_dim.18
  1.5 0.1 broadcast_in_dim.19.refs_0_
  1.6 5.1 %collective-permute-start.47 = (s32[32,128]{1,0:T(8,128)S(1)}, s32[32,128]{1,0:T(8,128)S(1)}, u32[]{:S(2)}, u32[]{:S(2)}) collective-permute-start(s32[32,128]{1,0:T(8,128)S(1)} %broadcast_in_dim.19.refs_0_), channel_id=1, source_target_pairs={{0,3},{1,2},{2,1},{3,0},{4,7},{5,6},{6,5},{7,4},{8,11},{9,10},{10,... | collective-permute-start | bytes 49160 | tf_op jit(solution)/shard_map/ppermute | solution.py:352
  6.6 0.6 collective-permute-start.45
  7.3 0.1 fusion.12.selector_ref
  7.4 2.0 %opening.1 = (bf16[512,512]{1,0:T(8,128)(2,1)S(1)}, bf16[512,512]{1,0:T(8,128)(2,1)S(1)}, bf16[32,64,128]{2,1,0:T(8,128)(2,1)S(1)}) custom-call(bf16[1024,512]{1,0:T(8,128)(2,1)} %bitcast.14, bf16[512,256]{1,0:T(8,128)(2,1)S(1)} %fusion.12.selector_ref), custom_call_target="tpu_custom_call" | custom-call | tf_op jit(solution)/shard_map/opening/pallas_call | solution.py:400
  9.4 1.9 %collective-permute-done.46.refs_2_ = s32[32,128]{1,0:T(8,128)S(1)} collective-permute-done((s32[32,128]{1,0:T(8,128)S(1)}, s32[32,128]{1,0:T(8,128)S(1)}, u32[]{:S(2)}, u32[]{:S(2)}) %collective-permute-start.46) | collective-permute-done | bytes 16416 | tf_op jit(solution)/shard_map/ppermute | solution.py:352
  11.3 0.4 pattern.1
  11.8 67.1 %conditional.1 = (bf16[1024,512]{1,0:T(8,128)(2,1)}, f32[32,128]{1,0:T(8,128)S(1)}) conditional(s32[]{:T(128)} %bitcast.1, (bf16[1024,512]{1,0:T(8,128)(2,1)}, bf16[8,512,512]{2,1,0:T(8,128)(2,1)}, bf16[4096,512]{1,0:T(8,128)(2,1)}, bf16[512,512]{1,0:T(8,128)(2,1)S(1)}, bf16[512,512]{1,0:T(8,128)(2,1)S(1)}, ...), branch_computations={%region_0.1_spmd, %region_1.2_spmd, %region_2.3_spmd} | conditional | flops 16911433728 | bytes 167595312 | solution.py:475
  11.9 2.6 %collective-permute-start.1 = (bf16[512,512]{1,0:T(8,128)(2,1)S(1)}, bf16[512,512]{1,0:T(8,128)(2,1)S(1)}, u32[]{:S(2)}, u32[]{:S(2)}) collective-permute-start(bf16[512,512]{1,0:T(8,128)(2,1)S(1)} %get-tuple-element.69), channel_id=1, source_target_pairs={{0,28},{4,0},{8,4},{12,8},{16,12},{20,16},{24,20},{28,24},{1,29},{... | collective-permute-start | bytes 1572872 | tf_op jit(solution)/shard_map/cond/branch_0_fun/ppermute | solution.py:346
  14.5 0.9 picking.3
  15.3 2.1 %collective-permute-start.3 = (bf16[9,64,128]{2,1,0:T(8,128)(2,1)S(1)}, bf16[9,64,128]{2,1,0:T(8,128)(2,1)S(1)}, u32[]{:S(2)}, u32[]{:S(2)}) collective-permute-start(bf16[9,64,128]{2,1,0:T(8,128)(2,1)S(1)} %get-tuple-element.72), channel_id=1, source_target_pairs={{0,2},{1,3},{2,0},{3,1},{4,6},{5,7},{6,4},{7,5},{8,10},{9,11},{10,... | collective-permute-start | bytes 442376 | tf_op jit(solution)/shard_map/cond/branch_0_fun/ppermute | solution.py:352
  17.5 1.4 %collective-permute-start.2 = (bf16[18,64,128]{2,1,0:T(8,128)(2,1)S(1)}, bf16[18,64,128]{2,1,0:T(8,128)(2,1)S(1)}, u32[]{:S(2)}, u32[]{:S(2)}) collective-permute-start(bf16[18,64,128]{2,1,0:T(8,128)(2,1)S(1)} %get-tuple-element.71), channel_id=1, source_target_pairs={{0,1},{1,0},{2,3},{3,2},{4,5},{5,4},{6,7},{7,6},{8,9},{9,8},{10,11... | collective-permute-start | bytes 884744 | tf_op jit(solution)/shard_map/cond/branch_0_fun/ppermute | solution.py:352
  18.9 8.4 %near_1.3.near_ref = f32[4,1024,128]{2,1,0:T(8,128)S(1)} custom-call(bf16[1024,512]{1,0:T(8,128)(2,1)} %get-tuple-element.49.refs_0_.refs_3_, bf16[8,512,512]{2,1,0:T(8,128)(2,1)} %get-tuple-element.66.refs_1_, bf16[4096,512]{1,0:T(8,128)(2,1)} %get-tuple-element.67.refs_2_.axial_ref), custom_call_target="tpu_custom_call" | custom-call | flops 3758096384 | bytes 10000000 | tf_op jit(solution)/shard_map/cond/branch_0_fun/near_1/pallas_call | solution.py:418
  27.3 1.5 %middle_1.3.refs_2_ = f32[4,1024,128]{2,1,0:T(8,128)S(1)} custom-call(f32[4,1024,128]{2,1,0:T(8,128)S(1)} %near_1.3.near_ref, bf16[512,512]{1,0:T(8,128)(2,1)S(1)} %collective-permute-done.low_ref, bf16[512,512]{1,0:T(8,128)(2,1)S(1)} %collective-permute-done.1.high_ref, bf16[4096,512]{1,0:T(8,128)(2,1)S(1)} %copy-done), custom_call_target="tpu_custom_call", output_to_operand_aliasing={{}: (0, {})} | custom-call | flops 1342177280 | bytes 10000000 | tf_op jit(solution)/shard_map/cond/branch_0_fun/middle_1/pallas_call | solution.py:428
  28.9 2.4 %collective-permute-done.2.refs_4_ = bf16[18,64,128]{2,1,0:T(8,128)(2,1)S(1)} collective-permute-done((bf16[18,64,128]{2,1,0:T(8,128)(2,1)S(1)}, bf16[18,64,128]{2,1,0:T(8,128)(2,1)S(1)}, u32[]{:S(2)}, u32[]{:S(2)}) %collective-permute-start.2) | collective-permute-done | bytes 294944 | tf_op jit(solution)/shard_map/cond/branch_0_fun/ppermute | solution.py:352
  31.3 2.7 %far_1.3 = (bf16[1024,512]{1,0:T(8,128)(2,1)S(1)}, bf16[512,512]{1,0:T(8,128)(2,1)S(1)}, bf16[512,512]{1,0:T(8,128)(2,1)S(1)}, bf16[32,64,128]{2,1,0:T(8,128)(2,...) custom-call(s32[1,128]{1,0:T(1,128)S(1)} %get-tuple-element.47.refs_0_, ...), custom_call_target="tpu_custom_call" | custom-call | flops 536870912 | bytes 10000000 | tf_op jit(solution)/shard_map/cond/branch_0_fun/far_1/pallas_call | solution.py:448
  34.0 2.6 %collective-permute-start.6 = (bf16[512,512]{1,0:T(8,128)(2,1)S(1)}, bf16[512,512]{1,0:T(8,128)(2,1)S(1)}, u32[]{:S(2)}, u32[]{:S(2)}) collective-permute-start(bf16[512,512]{1,0:T(8,128)(2,1)S(1)} %get-tuple-element.78), channel_id=1, source_target_pairs={{0,28},{4,0},{8,4},{12,8},{16,12},{20,16},{24,20},{28,24},{1,29},{... | collective-permute-start | bytes 1572872 | tf_op jit(solution)/shard_map/cond/branch_0_fun/ppermute | solution.py:346
  36.6 0.6 collective-permute-start.8
  37.3 2.2 %collective-permute-start.9 = (bf16[9,64,128]{2,1,0:T(8,128)(2,1)S(1)}, bf16[9,64,128]{2,1,0:T(8,128)(2,1)S(1)}, u32[]{:S(2)}, u32[]{:S(2)}) collective-permute-start(bf16[9,64,128]{2,1,0:T(8,128)(2,1)S(1)} %get-tuple-element.82), channel_id=1, source_target_pairs={{0,3},{1,2},{2,1},{3,0},{4,7},{5,6},{6,5},{7,4},{8,11},{9,10},{10,... | collective-permute-start | bytes 442376 | tf_op jit(solution)/shard_map/cond/branch_0_fun/ppermute | solution.py:352
  39.4 0.7 collective-permute-start.7
  40.1 4.6 %near_2.3.near_ref = f32[4,1024,128]{2,1,0:T(8,128)S(1)} custom-call(bf16[1024,512]{1,0:T(8,128)(2,1)S(1)} %get-tuple-element.76.refs_0_, bf16[8,512,512]{2,1,0:T(8,128)(2,1)S(1)} %copy-done.9, bf16[4096,512]{1,0:T(8,128)(2,1)S(1)} %copy-done, bf16[1024,512]{1,0:T(8,128)(2,1)S(1)} %copy-done.6), custom_call_target="tpu_custom_call" | custom-call | flops 3758096384 | bytes 10000000 | tf_op jit(solution)/shard_map/cond/branch_0_fun/near_2/pallas_call | solution.py:418
  44.7 3.6 %collective-permute-done.5.low_ref = bf16[512,512]{1,0:T(8,128)(2,1)S(1)} collective-permute-done((bf16[512,512]{1,0:T(8,128)(2,1)S(1)}, bf16[512,512]{1,0:T(8,128)(2,1)S(1)}, u32[]{:S(2)}, u32[]{:S(2)}) %collective-permute-start.5) | collective-permute-done | bytes 524320 | tf_op jit(solution)/shard_map/cond/branch_0_fun/ppermute | solution.py:346
  48.3 1.5 %middle_2.3.refs_2_ = f32[4,1024,128]{2,1,0:T(8,128)S(1)} custom-call(f32[4,1024,128]{2,1,0:T(8,128)S(1)} %near_2.3.near_ref, bf16[512,512]{1,0:T(8,128)(2,1)S(1)} %collective-permute-done.5.low_ref, bf16[512,512]{1,0:T(8,128)(2,1)S(1)} %collective-permute-done.6.high_ref, bf16[4096,512]{1,0:T(8,128)(2,1)S(1)} %copy-done), custom_call_target="tpu_custom_call", output_to_operand_aliasing={{}: (0, {})} | custom-call | flops 1342177280 | bytes 10000000 | tf_op jit(solution)/shard_map/cond/branch_0_fun/middle_2/pallas_call | solution.py:428
  49.9 3.1 %collective-permute-done.7.refs_4_ = bf16[18,64,128]{2,1,0:T(8,128)(2,1)S(1)} collective-permute-done((bf16[18,64,128]{2,1,0:T(8,128)(2,1)S(1)}, bf16[18,64,128]{2,1,0:T(8,128)(2,1)S(1)}, u32[]{:S(2)}, u32[]{:S(2)}) %collective-permute-start.7) | collective-permute-done | bytes 294944 | tf_op jit(solution)/shard_map/cond/branch_0_fun/ppermute | solution.py:352
  53.0 3.6 %far_2.3 = (bf16[1024,512]{1,0:T(8,128)(2,1)}, bf16[512,512]{1,0:T(8,128)(2,1)S(1)}, bf16[512,512]{1,0:T(8,128)(2,1)S(1)}, bf16[32,64,128]{2,1,0:T(8,128)(2,1)S(...) custom-call(s32[1,128]{1,0:T(1,128)S(1)} %get-tuple-element.47.refs_0_, ...), custom_call_target="tpu_custom_call" | custom-call | flops 536870912 | bytes 10000000 | tf_op jit(solution)/shard_map/cond/branch_0_fun/far_2/pallas_call | solution.py:448
  56.5 2.6 %collective-permute-start.11 = (bf16[512,512]{1,0:T(8,128)(2,1)S(1)}, bf16[512,512]{1,0:T(8,128)(2,1)S(1)}, u32[]{:S(2)}, u32[]{:S(2)}) collective-permute-start(bf16[512,512]{1,0:T(8,128)(2,1)S(1)} %get-tuple-element.87), channel_id=1, source_target_pairs={{0,28},{4,0},{8,4},{12,8},{16,12},{20,16},{24,20},{28,24},{1,29},{... | collective-permute-start | bytes 1572872 | tf_op jit(solution)/shard_map/cond/branch_0_fun/ppermute | solution.py:346
  59.2 1.9 %collective-permute-start.14 = (bf16[9,64,128]{2,1,0:T(8,128)(2,1)S(1)}, bf16[9,64,128]{2,1,0:T(8,128)(2,1)S(1)}, u32[]{:S(2)}, u32[]{:S(2)}) collective-permute-start(bf16[9,64,128]{2,1,0:T(8,128)(2,1)S(1)} %get-tuple-element.91), channel_id=1, source_target_pairs={{0,3},{1,2},{2,1},{3,0},{4,7},{5,6},{6,5},{7,4},{8,11},{9,10},{10,... | collective-permute-start | bytes 442376 | tf_op jit(solution)/shard_map/cond/branch_0_fun/ppermute | solution.py:352
  61.1 1.6 %collective-permute-start.12 = (bf16[18,64,128]{2,1,0:T(8,128)(2,1)S(1)}, bf16[18,64,128]{2,1,0:T(8,128)(2,1)S(1)}, u32[]{:S(2)}, u32[]{:S(2)}) collective-permute-start(bf16[18,64,128]{2,1,0:T(8,128)(2,1)S(1)} %get-tuple-element.89), channel_id=1, source_target_pairs={{0,1},{1,0},{2,3},{3,2},{4,5},{5,4},{6,7},{7,6},{8,9},{9,8},{10,11... | collective-permute-start | bytes 884744 | tf_op jit(solution)/shard_map/cond/branch_0_fun/ppermute | solution.py:352
  62.7 5.5 %near_3.3 = (f32[4,1024,128]{2,1,0:T(8,128)S(1)}, f32[128,128]{1,0:T(8,128)S(1)}) custom-call(bf16[1024,512]{1,0:T(8,128)(2,1)} %get-tuple-element.180.refs_0_.refs_8_, bf16[8,512,512]{2,1,0:T(8,128)(2,1)S(1)} %copy-done.9, bf16[4096,512]{1,0:T(8,128)(2,1)S(1)} %copy-done), custom_call_target="tpu_custom_call" | custom-call | flops 3758096384 | bytes 10000000 | tf_op jit(solution)/shard_map/cond/branch_0_fun/near_3/pallas_call | solution.py:418
  68.2 2.6 %collective-permute-done.10.low_ref = bf16[512,512]{1,0:T(8,128)(2,1)S(1)} collective-permute-done((bf16[512,512]{1,0:T(8,128)(2,1)S(1)}, bf16[512,512]{1,0:T(8,128)(2,1)S(1)}, u32[]{:S(2)}, u32[]{:S(2)}) %collective-permute-start.10) | collective-permute-done | bytes 524320 | tf_op jit(solution)/shard_map/cond/branch_0_fun/ppermute | solution.py:346
  70.9 1.5 %middle_3.3.refs_2_ = f32[4,1024,128]{2,1,0:T(8,128)S(1)} custom-call(f32[4,1024,128]{2,1,0:T(8,128)S(1)} %get-tuple-element.85.near_ref, bf16[512,512]{1,0:T(8,128)(2,1)S(1)} %collective-permute-done.10.low_ref, bf16[512,512]{1,0:T(8,128)(2,1)S(1)} %collective-permute-done.11.high_ref, bf16[4096,512]{1,0:T(8,128)(2,1)S(1)} %copy-done), custom_call_target="tpu_custom_call", output_to_operand_aliasing={{}: (0, {})} | custom-call | flops 1342177280 | bytes 10000000 | tf_op jit(solution)/shard_map/cond/branch_0_fun/middle_3/pallas_call | solution.py:428
  72.4 2.3 %collective-permute-done.12.refs_4_ = bf16[18,64,128]{2,1,0:T(8,128)(2,1)S(1)} collective-permute-done((bf16[18,64,128]{2,1,0:T(8,128)(2,1)S(1)}, bf16[18,64,128]{2,1,0:T(8,128)(2,1)S(1)}, u32[]{:S(2)}, u32[]{:S(2)}) %collective-permute-start.12) | collective-permute-done | bytes 294944 | tf_op jit(solution)/shard_map/cond/branch_0_fun/ppermute | solution.py:352
  74.7 3.7 %far_3.3 = f32[32,128]{1,0:T(8,128)S(1)} custom-call(s32[1,128]{1,0:T(1,128)S(1)} %get-tuple-element.47.refs_0_, s32[8,128]{1,0:T(8,128)S(1)} %get-tuple-element.48.lists_ref.refs_1_, f32[4,1024,128]{2,1,0:T(8,128)S(1)} %middle_3.3.refs_2_, bf16[32,64,128]{2,1,0:T(8,128)(2,1)S(1)} %get-tuple-element.88.refs_3_, ...), custom_call_target="tpu_custom_call" | custom-call | flops 536870912 | bytes 10000000 | tf_op jit(solution)/shard_map/cond/branch_0_fun/far_3/pallas_call | solution.py:448
  78.9 1.2 %collective-permute-done.48 = f32[32,128]{1,0:T(8,128)S(1)} collective-permute-done((f32[32,128]{1,0:T(8,128)S(1)}, f32[32,128]{1,0:T(8,128)S(1)}, u32[]{:S(2)}, u32[]{:S(2)}) %collective-permute-start.48) | collective-permute-done | bytes 16416 | tf_op jit(solution)/shard_map/ppermute | solution.py:362
  80.1 1.4 %collective-permute-start.51 = (f32[32,128]{1,0:T(8,128)S(1)}, f32[32,128]{1,0:T(8,128)S(1)}, u32[]{:S(2)}, u32[]{:S(2)}) collective-permute-start(f32[32,128]{1,0:T(8,128)S(1)} %add.146), channel_id=1, source_target_pairs={{0,24},{4,28},{8,16},{12,20},{16,8},{20,12},{24,0},{28,4},{1,25},{... | collective-permute-start | bytes 49160 | tf_op jit(solution)/shard_map/ppermute | solution.py:362
  81.5 0.7 collective-permute-start.50
  82.2 1.4 %collective-permute-start.49 = (f32[32,128]{1,0:T(8,128)S(1)}, f32[32,128]{1,0:T(8,128)S(1)}, u32[]{:S(2)}, u32[]{:S(2)}) collective-permute-start(f32[32,128]{1,0:T(8,128)S(1)} %add.146), channel_id=1, source_target_pairs={{0,8},{4,12},{8,0},{12,4},{16,24},{20,28},{24,16},{28,20},{1,9},{5... | collective-permute-start | bytes 49160 | tf_op jit(solution)/shard_map/ppermute | solution.py:362
  83.6 1.1 %collective-permute-done.51 = f32[32,128]{1,0:T(8,128)S(1)} collective-permute-done((f32[32,128]{1,0:T(8,128)S(1)}, f32[32,128]{1,0:T(8,128)S(1)}, u32[]{:S(2)}, u32[]{:S(2)}) %collective-permute-start.51) | collective-permute-done | bytes 16416 | tf_op jit(solution)/shard_map/ppermute | solution.py:362
  84.7 0.5 collective-permute-done.50
  85.3 0.7 collective-permute-done.49
  85.9 2.2 %collective-permute-start.54 = (f32[32,128]{1,0:T(8,128)S(1)}, f32[32,128]{1,0:T(8,128)S(1)}, u32[]{:S(2)}, u32[]{:S(2)}) collective-permute-start(f32[32,128]{1,0:T(8,128)S(1)} %add_add_fusion), channel_id=1, source_target_pairs={{0,3},{1,2},{2,1},{3,0},{4,7},{5,6},{6,5},{7,4},{8,11},{9,10},{10,... | collective-permute-start | bytes 49160 | tf_op jit(solution)/shard_map/ppermute | solution.py:362
  88.1 2.3 %collective-permute-start.52 = (f32[32,128]{1,0:T(8,128)S(1)}, f32[32,128]{1,0:T(8,128)S(1)}, u32[]{:S(2)}, u32[]{:S(2)}) collective-permute-start(f32[32,128]{1,0:T(8,128)S(1)} %add_add_fusion), channel_id=1, source_target_pairs={{0,1},{1,0},{2,3},{3,2},{4,5},{5,4},{6,7},{7,6},{8,9},{9,8},{10,11... | collective-permute-start | bytes 49160 | tf_op jit(solution)/shard_map/ppermute | solution.py:362
  90.4 1.2 %collective-permute-done.54 = f32[32,128]{1,0:T(8,128)S(1)} collective-permute-done((f32[32,128]{1,0:T(8,128)S(1)}, f32[32,128]{1,0:T(8,128)S(1)}, u32[]{:S(2)}, u32[]{:S(2)}) %collective-permute-start.54) | collective-permute-done | bytes 16416 | tf_op jit(solution)/shard_map/ppermute | solution.py:362
  91.6 1.1 %collective-permute-done.53 = f32[32,128]{1,0:T(8,128)S(1)} collective-permute-done((f32[32,128]{1,0:T(8,128)S(1)}, f32[32,128]{1,0:T(8,128)S(1)}, u32[]{:S(2)}, u32[]{:S(2)}) %collective-permute-start.53) | collective-permute-done | bytes 16416 | tf_op jit(solution)/shard_map/ppermute | solution.py:362
  92.8 0.6 fusion.17
  (35 shorter events, 0.4 us)
Async XLA Ops:
  1.6 7.8 %collective-permute-start.47 = (s32[32,128]{1,0:T(8,128)S(1)}, s32[32,128]{1,0:T(8,128)S(1)}, u32[]{:S(2)}, u32[]{:S(2)}) collective-permute-start(s32[32,128]{1,0:T(8,128)S(1)} %broadcast_in_dim.19.refs_0_), channel_id=1, source_target_pairs={{0,3},{1,2},{2,1},{3,0},{4,7},{5,6},{6,5},{7,4},{8,11},{9,10},{10,... | collective-permute-start | bytes 49160 | tf_op jit(solution)/shard_map/ppermute | solution.py:352
  6.6 4.6 %collective-permute-start.46 = (s32[32,128]{1,0:T(8,128)S(1)}, s32[32,128]{1,0:T(8,128)S(1)}, u32[]{:S(2)}, u32[]{:S(2)}) collective-permute-start(s32[32,128]{1,0:T(8,128)S(1)} %broadcast_in_dim.19.refs_0_), channel_id=1, source_target_pairs={{0,2},{1,3},{2,0},{3,1},{4,6},{5,7},{6,4},{7,5},{8,10},{9,11},{10,... | collective-permute-start | bytes 49160 | tf_op jit(solution)/shard_map/ppermute | solution.py:352
  6.6 4.6 %collective-permute-start.45 = (s32[32,128]{1,0:T(8,128)S(1)}, s32[32,128]{1,0:T(8,128)S(1)}, u32[]{:S(2)}, u32[]{:S(2)}) collective-permute-start(s32[32,128]{1,0:T(8,128)S(1)} %broadcast_in_dim.19.refs_0_), channel_id=1, source_target_pairs={{0,1},{1,0},{2,3},{3,2},{4,5},{5,4},{6,7},{7,6},{8,9},{9,8},{10,11... | collective-permute-start | bytes 49160 | tf_op jit(solution)/shard_map/ppermute | solution.py:352
  11.8 15.5 %collective-permute-start = (bf16[512,512]{1,0:T(8,128)(2,1)S(1)}, bf16[512,512]{1,0:T(8,128)(2,1)S(1)}, u32[]{:S(2)}, u32[]{:S(2)}) collective-permute-start(bf16[512,512]{1,0:T(8,128)(2,1)S(1)} %get-tuple-element.68), channel_id=1, source_target_pairs={{0,4},{4,8},{8,12},{12,16},{16,20},{20,24},{24,28},{28,0},{1,5},{5... | collective-permute-start | bytes 1572872 | tf_op jit(solution)/shard_map/cond/branch_0_fun/ppermute | solution.py:346
  11.9 15.5 %collective-permute-start.1 = (bf16[512,512]{1,0:T(8,128)(2,1)S(1)}, bf16[512,512]{1,0:T(8,128)(2,1)S(1)}, u32[]{:S(2)}, u32[]{:S(2)}) collective-permute-start(bf16[512,512]{1,0:T(8,128)(2,1)S(1)} %get-tuple-element.69), channel_id=1, source_target_pairs={{0,28},{4,0},{8,4},{12,8},{16,12},{20,16},{24,20},{28,24},{1,29},{... | collective-permute-start | bytes 1572872 | tf_op jit(solution)/shard_map/cond/branch_0_fun/ppermute | solution.py:346
  15.3 13.5 %collective-permute-start.3 = (bf16[9,64,128]{2,1,0:T(8,128)(2,1)S(1)}, bf16[9,64,128]{2,1,0:T(8,128)(2,1)S(1)}, u32[]{:S(2)}, u32[]{:S(2)}) collective-permute-start(bf16[9,64,128]{2,1,0:T(8,128)(2,1)S(1)} %get-tuple-element.72), channel_id=1, source_target_pairs={{0,2},{1,3},{2,0},{3,1},{4,6},{5,7},{6,4},{7,5},{8,10},{9,11},{10,... | collective-permute-start | bytes 442376 | tf_op jit(solution)/shard_map/cond/branch_0_fun/ppermute | solution.py:352
  17.4 11.4 %collective-permute-start.4 = (bf16[9,64,128]{2,1,0:T(8,128)(2,1)S(1)}, bf16[9,64,128]{2,1,0:T(8,128)(2,1)S(1)}, u32[]{:S(2)}, u32[]{:S(2)}) collective-permute-start(bf16[9,64,128]{2,1,0:T(8,128)(2,1)S(1)} %get-tuple-element.73), channel_id=1, source_target_pairs={{0,3},{1,2},{2,1},{3,0},{4,7},{5,6},{6,5},{7,4},{8,11},{9,10},{10,... | collective-permute-start | bytes 442376 | tf_op jit(solution)/shard_map/cond/branch_0_fun/ppermute | solution.py:352
  17.5 13.8 %collective-permute-start.2 = (bf16[18,64,128]{2,1,0:T(8,128)(2,1)S(1)}, bf16[18,64,128]{2,1,0:T(8,128)(2,1)S(1)}, u32[]{:S(2)}, u32[]{:S(2)}) collective-permute-start(bf16[18,64,128]{2,1,0:T(8,128)(2,1)S(1)} %get-tuple-element.71), channel_id=1, source_target_pairs={{0,1},{1,0},{2,3},{3,2},{4,5},{5,4},{6,7},{7,6},{8,9},{9,8},{10,11... | collective-permute-start | bytes 884744 | tf_op jit(solution)/shard_map/cond/branch_0_fun/ppermute | solution.py:352
  18.9 8.4 %copy-start = (bf16[4096,512]{1,0:T(8,128)(2,1)S(1)}, bf16[4096,512]{1,0:T(8,128)(2,1)}, u32[]{:S(2)}) copy-start(bf16[4096,512]{1,0:T(8,128)(2,1)} %get-tuple-element.67.refs_2_.axial_ref) | copy-start | bytes 12582916 | tf_op jit(solution)/shard_map/cond
  27.3 4.0 %copy-start.3 = (bf16[8,256,512]{2,1,0:T(8,128)(2,1)S(1)}, bf16[8,256,512]{2,1,0:T(8,128)(2,1)}, u32[]{:S(2)}) copy-start(bf16[8,256,512]{2,1,0:T(8,128)(2,1)} %get-tuple-element.74.refs_7_) | copy-start | bytes 6291460 | tf_op jit(solution)/shard_map/cond
  31.3 8.9 %copy-start.6 = (bf16[1024,512]{1,0:T(8,128)(2,1)S(1)}, bf16[1024,512]{1,0:T(8,128)(2,1)}, u32[]{:S(2)}) copy-start(bf16[1024,512]{1,0:T(8,128)(2,1)} %get-tuple-element.49.refs_0_.refs_3_) | copy-start | bytes 3145732 | tf_op jit(solution)/shard_map/cond
  31.3 8.9 %copy-start.9 = (bf16[8,512,512]{2,1,0:T(8,128)(2,1)S(1)}, bf16[8,512,512]{2,1,0:T(8,128)(2,1)}, u32[]{:S(2)}) copy-start(bf16[8,512,512]{2,1,0:T(8,128)(2,1)} %get-tuple-element.66.refs_1_) | copy-start | bytes 12582916 | tf_op jit(solution)/shard_map/cond
  34.0 14.4 %collective-permute-start.5 = (bf16[512,512]{1,0:T(8,128)(2,1)S(1)}, bf16[512,512]{1,0:T(8,128)(2,1)S(1)}, u32[]{:S(2)}, u32[]{:S(2)}) collective-permute-start(bf16[512,512]{1,0:T(8,128)(2,1)S(1)} %get-tuple-element.77), channel_id=1, source_target_pairs={{0,4},{4,8},{8,12},{12,16},{16,20},{20,24},{24,28},{28,0},{1,5},{5... | collective-permute-start | bytes 1572872 | tf_op jit(solution)/shard_map/cond/branch_0_fun/ppermute | solution.py:346
  34.0 14.3 %collective-permute-start.6 = (bf16[512,512]{1,0:T(8,128)(2,1)S(1)}, bf16[512,512]{1,0:T(8,128)(2,1)S(1)}, u32[]{:S(2)}, u32[]{:S(2)}) collective-permute-start(bf16[512,512]{1,0:T(8,128)(2,1)S(1)} %get-tuple-element.78), channel_id=1, source_target_pairs={{0,28},{4,0},{8,4},{12,8},{16,12},{20,16},{24,20},{28,24},{1,29},{... | collective-permute-start | bytes 1572872 | tf_op jit(solution)/shard_map/cond/branch_0_fun/ppermute | solution.py:346
  36.6 13.2 %collective-permute-start.8 = (bf16[9,64,128]{2,1,0:T(8,128)(2,1)S(1)}, bf16[9,64,128]{2,1,0:T(8,128)(2,1)S(1)}, u32[]{:S(2)}, u32[]{:S(2)}) collective-permute-start(bf16[9,64,128]{2,1,0:T(8,128)(2,1)S(1)} %get-tuple-element.81), channel_id=1, source_target_pairs={{0,2},{1,3},{2,0},{3,1},{4,6},{5,7},{6,4},{7,5},{8,10},{9,11},{10,... | collective-permute-start | bytes 442376 | tf_op jit(solution)/shard_map/cond/branch_0_fun/ppermute | solution.py:352
  37.3 12.6 %collective-permute-start.9 = (bf16[9,64,128]{2,1,0:T(8,128)(2,1)S(1)}, bf16[9,64,128]{2,1,0:T(8,128)(2,1)S(1)}, u32[]{:S(2)}, u32[]{:S(2)}) collective-permute-start(bf16[9,64,128]{2,1,0:T(8,128)(2,1)S(1)} %get-tuple-element.82), channel_id=1, source_target_pairs={{0,3},{1,2},{2,1},{3,0},{4,7},{5,6},{6,5},{7,4},{8,11},{9,10},{10,... | collective-permute-start | bytes 442376 | tf_op jit(solution)/shard_map/cond/branch_0_fun/ppermute | solution.py:352
  39.4 13.6 %collective-permute-start.7 = (bf16[18,64,128]{2,1,0:T(8,128)(2,1)S(1)}, bf16[18,64,128]{2,1,0:T(8,128)(2,1)S(1)}, u32[]{:S(2)}, u32[]{:S(2)}) collective-permute-start(bf16[18,64,128]{2,1,0:T(8,128)(2,1)S(1)} %get-tuple-element.80), channel_id=1, source_target_pairs={{0,1},{1,0},{2,3},{3,2},{4,5},{5,4},{6,7},{7,6},{8,9},{9,8},{10,11... | collective-permute-start | bytes 884744 | tf_op jit(solution)/shard_map/cond/branch_0_fun/ppermute | solution.py:352
  56.5 14.3 %collective-permute-start.10 = (bf16[512,512]{1,0:T(8,128)(2,1)S(1)}, bf16[512,512]{1,0:T(8,128)(2,1)S(1)}, u32[]{:S(2)}, u32[]{:S(2)}) collective-permute-start(bf16[512,512]{1,0:T(8,128)(2,1)S(1)} %get-tuple-element.86), channel_id=1, source_target_pairs={{0,4},{4,8},{8,12},{12,16},{16,20},{20,24},{24,28},{28,0},{1,5},{5... | collective-permute-start | bytes 1572872 | tf_op jit(solution)/shard_map/cond/branch_0_fun/ppermute | solution.py:346
  56.5 14.3 %collective-permute-start.11 = (bf16[512,512]{1,0:T(8,128)(2,1)S(1)}, bf16[512,512]{1,0:T(8,128)(2,1)S(1)}, u32[]{:S(2)}, u32[]{:S(2)}) collective-permute-start(bf16[512,512]{1,0:T(8,128)(2,1)S(1)} %get-tuple-element.87), channel_id=1, source_target_pairs={{0,28},{4,0},{8,4},{12,8},{16,12},{20,16},{24,20},{28,24},{1,29},{... | collective-permute-start | bytes 1572872 | tf_op jit(solution)/shard_map/cond/branch_0_fun/ppermute | solution.py:346
  59.2 13.2 %collective-permute-start.13 = (bf16[9,64,128]{2,1,0:T(8,128)(2,1)S(1)}, bf16[9,64,128]{2,1,0:T(8,128)(2,1)S(1)}, u32[]{:S(2)}, u32[]{:S(2)}) collective-permute-start(bf16[9,64,128]{2,1,0:T(8,128)(2,1)S(1)} %get-tuple-element.90), channel_id=1, source_target_pairs={{0,2},{1,3},{2,0},{3,1},{4,6},{5,7},{6,4},{7,5},{8,10},{9,11},{10,... | collective-permute-start | bytes 442376 | tf_op jit(solution)/shard_map/cond/branch_0_fun/ppermute | solution.py:352
  59.2 13.2 %collective-permute-start.14 = (bf16[9,64,128]{2,1,0:T(8,128)(2,1)S(1)}, bf16[9,64,128]{2,1,0:T(8,128)(2,1)S(1)}, u32[]{:S(2)}, u32[]{:S(2)}) collective-permute-start(bf16[9,64,128]{2,1,0:T(8,128)(2,1)S(1)} %get-tuple-element.91), channel_id=1, source_target_pairs={{0,3},{1,2},{2,1},{3,0},{4,7},{5,6},{6,5},{7,4},{8,11},{9,10},{10,... | collective-permute-start | bytes 442376 | tf_op jit(solution)/shard_map/cond/branch_0_fun/ppermute | solution.py:352
  61.1 13.6 %collective-permute-start.12 = (bf16[18,64,128]{2,1,0:T(8,128)(2,1)S(1)}, bf16[18,64,128]{2,1,0:T(8,128)(2,1)S(1)}, u32[]{:S(2)}, u32[]{:S(2)}) collective-permute-start(bf16[18,64,128]{2,1,0:T(8,128)(2,1)S(1)} %get-tuple-element.89), channel_id=1, source_target_pairs={{0,1},{1,0},{2,3},{3,2},{4,5},{5,4},{6,7},{7,6},{8,9},{9,8},{10,11... | collective-permute-start | bytes 884744 | tf_op jit(solution)/shard_map/cond/branch_0_fun/ppermute | solution.py:352
  78.8 1.2 %collective-permute-start.48 = (f32[32,128]{1,0:T(8,128)S(1)}, f32[32,128]{1,0:T(8,128)S(1)}, u32[]{:S(2)}, u32[]{:S(2)}) collective-permute-start(f32[32,128]{1,0:T(8,128)S(1)} %get-tuple-element.171), channel_id=1, source_target_pairs={{0,4},{4,0},{8,12},{12,8},{16,20},{20,16},{24,28},{28,24},{1,5},{5... | collective-permute-start | bytes 49160 | tf_op jit(solution)/shard_map/ppermute | solution.py:362
  80.1 4.6 %collective-permute-start.51 = (f32[32,128]{1,0:T(8,128)S(1)}, f32[32,128]{1,0:T(8,128)S(1)}, u32[]{:S(2)}, u32[]{:S(2)}) collective-permute-start(f32[32,128]{1,0:T(8,128)S(1)} %add.146), channel_id=1, source_target_pairs={{0,24},{4,28},{8,16},{12,20},{16,8},{20,12},{24,0},{28,4},{1,25},{... | collective-permute-start | bytes 49160 | tf_op jit(solution)/shard_map/ppermute | solution.py:362
  81.5 3.7 %collective-permute-start.50 = (f32[32,128]{1,0:T(8,128)S(1)}, f32[32,128]{1,0:T(8,128)S(1)}, u32[]{:S(2)}, u32[]{:S(2)}) collective-permute-start(f32[32,128]{1,0:T(8,128)S(1)} %add.146), channel_id=1, source_target_pairs={{0,16},{4,20},{8,24},{12,28},{16,0},{20,4},{24,8},{28,12},{1,17},{... | collective-permute-start | bytes 49160 | tf_op jit(solution)/shard_map/ppermute | solution.py:362
  82.2 3.7 %collective-permute-start.49 = (f32[32,128]{1,0:T(8,128)S(1)}, f32[32,128]{1,0:T(8,128)S(1)}, u32[]{:S(2)}, u32[]{:S(2)}) collective-permute-start(f32[32,128]{1,0:T(8,128)S(1)} %add.146), channel_id=1, source_target_pairs={{0,8},{4,12},{8,0},{12,4},{16,24},{20,28},{24,16},{28,20},{1,9},{5... | collective-permute-start | bytes 49160 | tf_op jit(solution)/shard_map/ppermute | solution.py:362
  85.9 5.7 %collective-permute-start.54 = (f32[32,128]{1,0:T(8,128)S(1)}, f32[32,128]{1,0:T(8,128)S(1)}, u32[]{:S(2)}, u32[]{:S(2)}) collective-permute-start(f32[32,128]{1,0:T(8,128)S(1)} %add_add_fusion), channel_id=1, source_target_pairs={{0,3},{1,2},{2,1},{3,0},{4,7},{5,6},{6,5},{7,4},{8,11},{9,10},{10,... | collective-permute-start | bytes 49160 | tf_op jit(solution)/shard_map/ppermute | solution.py:362
  88.1 4.6 %collective-permute-start.53 = (f32[32,128]{1,0:T(8,128)S(1)}, f32[32,128]{1,0:T(8,128)S(1)}, u32[]{:S(2)}, u32[]{:S(2)}) collective-permute-start(f32[32,128]{1,0:T(8,128)S(1)} %add_add_fusion), channel_id=1, source_target_pairs={{0,2},{1,3},{2,0},{3,1},{4,6},{5,7},{6,4},{7,5},{8,10},{9,11},{10,... | collective-permute-start | bytes 49160 | tf_op jit(solution)/shard_map/ppermute | solution.py:362
  88.1 4.6 %collective-permute-start.52 = (f32[32,128]{1,0:T(8,128)S(1)}, f32[32,128]{1,0:T(8,128)S(1)}, u32[]{:S(2)}, u32[]{:S(2)}) collective-permute-start(f32[32,128]{1,0:T(8,128)S(1)} %add_add_fusion), channel_id=1, source_target_pairs={{0,1},{1,0},{2,3},{3,2},{4,5},{5,4},{6,7},{7,6},{8,9},{9,8},{10,11... | collective-permute-start | bytes 49160 | tf_op jit(solution)/shard_map/ppermute | solution.py:362

commit v3 on v2

--- a/solution.py
+++ b/solution.py
@@ -14,8 +14,8 @@
 LANES = 128
 CAPS = (9, 12)
 ROW_TILE = 256
-UNROLL = 8
-NEAR = 2
+UNROLL = 4
+MORE = 3
 
 shift_center = 0.3
 half_width = 1.2
@@ -122,19 +122,14 @@
 def opening_kernel(elements, unroll, start_ref, selector_ref, low_ref, high_ref, traces_ref, wide):
     rows = start_ref.shape[0]
     edge = low_ref.shape[0]
+
+    def chosen(index):
+        write_wide(wide, index, dot(start_ref[index, :], selector_ref[...]))
+
+    each_tile(rows, ROW_TILE, chosen)
+    each(elements, lambda e: store_traces(e, read_wide(wide, of_element(wide, e, elements)), traces_ref), unroll)
     low_ref[...] = start_ref[:edge]
     high_ref[...] = start_ref[rows - edge :]
-
-    def widen(index):
-        write_wide(wide, index, start_ref[index].astype(f32))
-
-    each_tile(rows, ROW_TILE, widen)
-
-    def element(e):
-        own = read_wide(wide, of_element(wide, e, elements)).astype(bf16)
-        store_traces(e, dot(own, selector_ref[...]), traces_ref)
-
-    each(elements, element, unroll)
 
 
 def picking_kernel(lists_ref, traces_ref, *sent_refs):
@@ -178,7 +173,7 @@
     owner = lax.broadcasted_iota(jnp.int32, total.shape, 1) // per
     number = lax.broadcasted_iota(jnp.int32, total.shape, 0)
     permute = permute_of(asker_of(me, number, shards), owner, shards)
-    weighed = jnp.where(permute == 1, total * (1.0 / NEAR), total)
+    weighed = jnp.where(permute == 1, total - MORE, total)
     weighed = jnp.where((permute == 0) | (number >= shards), 0.0, weighed)
     most = jnp.max(jnp.max(weighed, axis=1, keepdims=True), axis=0, keepdims=True)
     level = sum((most > cap).astype(jnp.int32) for cap in CAPS)
@@ -209,11 +204,12 @@
 
 def near_kernel(step, layer, elements, unroll, *refs):
     if step == 2:
-        here_ref, diag_ref, axial_ref, start_ref, acc_ref, wide = refs
+        here_ref, diag_ref, axial_ref, start_ref, acc_ref, wide, ext = refs
     elif step == 3:
-        here_ref, diag_ref, axial_ref, acc_ref, gram_ref, wide = refs
+        here_ref, diag_ref, axial_ref, acc_ref, gram_ref, own_ref, copy_ref, wide, ext = refs
+        copy_ref[...] = here_ref[...]
     else:
-        here_ref, diag_ref, axial_ref, acc_ref, wide = refs
+        here_ref, diag_ref, axial_ref, acc_ref, wide, ext = refs
     rows, block = here_ref.shape
     tile = 2 * layer
     if step == 3:
@@ -231,16 +227,36 @@
         write_wide(acc_ref, index, dot(own, diag_ref[e]))
         if step == 3:
             gram_ref[...] += across(own, own)
+            own_ref[e] = own
 
     each(elements, element, unroll)
 
-    layers = rows // layer
-    for offset in [*range(-HW, 0), *range(1, HW + 1)]:
-        if abs(offset) < layers:
-            begin, end = max(0, -offset) * layer, (layers - max(0, offset)) * layer
-            position = (offset + HW - (offset > 0)) * block
-            values = here_ref[begin + offset * layer : end + offset * layer]
-            add_to(acc_ref, slice(begin, end), dot(values, axial_ref[position : position + block]))
+    if unroll > 1:
+        layers = rows // layer
+        for offset in [*range(-HW, 0), *range(1, HW + 1)]:
+            if abs(offset) < layers:
+                begin, end = max(0, -offset) * layer, (layers - max(0, offset)) * layer
+                position = (offset + HW - (offset > 0)) * block
+                values = here_ref[begin + offset * layer : end + offset * layer]
+                add_to(acc_ref, slice(begin, end), dot(values, axial_ref[position : position + block]))
+    else:
+        edge = HW * layer
+        ext[:edge] = jnp.zeros((edge, block), bf16)
+        ext[edge : edge + rows] = here_ref[...]
+        ext[edge + rows :] = jnp.zeros((edge, block), bf16)
+
+        def offset(p):
+            begin = (p + jnp.where(p < HW, 0, 1)) * layer
+            weights = axial_ref[pl.ds(aligned(p * block, block), block), :]
+
+            def part(i):
+                base = aligned(i * tile, tile)
+                values = ext[pl.ds(aligned(begin + base, layer), tile), :]
+                add_to(acc_ref, pl.ds(base, tile), dot(values, weights))
+
+            each(rows // tile, part)
+
+        each(2 * HW, offset)
 
     if step != 3:
 
@@ -277,13 +293,8 @@
     arrived_refs = take(shards - 1)
     (face_ref,) = take(1)
     if step == 3:
-        here_ref, gram_ref, out_ref, wide, projected = take(5)
+        own_ref, gram_ref, out_ref, projected = take(4)
         projected[...] = jnp.zeros_like(projected)
-
-        def widen(index):
-            write_wide(wide, index, here_ref[index, :].astype(f32))
-
-        each_tile(here_ref.shape[0], ROW_TILE, widen)
     else:
         selector_ref, out_ref, out_low_ref, out_high_ref, out_traces_ref = take(5)
         sent_refs = take(shards - 1)
@@ -291,11 +302,11 @@
     scale = {1: 1.0 / half_width, 2: 2.0 / half_width, 3: 1.0}[step]
 
     def element(e):
-        index = of_element(wide, e, elements)
+        index = of_element(near_ref, e, elements)
         lifted = lifted_rows(e, places_ref, traces_ref, arrived_refs)
         total = (read_wide(near_ref, index) + dot(lifted, face_ref[e])) * scale
         if step == 3:
-            own = read_wide(wide, index).astype(bf16)
+            own = own_ref[e]
             upper = total.astype(bf16)
             lower = (total - upper.astype(f32)).astype(bf16)
             projected[...] += across(own, upper) + across(own, lower)
@@ -402,25 +413,31 @@
         out_shape=[shape((edge, block)), shape((edge, block)), shape((per, half, LANES))],
         in_specs=[VMEM] * 2,
         out_specs=[VMEM] * 3,
-        scratch_shapes=[pltpu.VMEM(wide_rows, f32)],
+        scratch_shapes=[pltpu.VMEM((F * TR // LANES, rows, LANES), f32)],
         compiler_params=params(rows),
         name="opening",
     )(start_flat, selector)
 
     def one_round(step, caps, here, low, high, traces, sent):
-        unroll = 1 if min(caps) == per else UNROLL
+        unroll = UNROLL if caps[-1] == CAPS[0] else 1
+        busy = 1 if caps[-1] == per else UNROLL
         arrived = [send_traces(s, r + 1) for r, s in enumerate(sent)]
         from_low = rotate(high, "pipe", 1)
         from_high = rotate(low, "pipe", -1)
         size = layers * vectors
         operands = [here, diag_blocks, axial_flat] + [start_flat] * (step == 2)
-        outs = [shape(wide_rows, f32)] + [shape((size, size), f32)] * (step == 3)
-        near, *gram = pl.pallas_call(
+        outs = [shape(wide_rows, f32)]
+        if step == 3:
+            outs += [shape((size, size), f32), shape((elements, size, block)), shape((rows, block))]
+        near, *extra = pl.pallas_call(
             functools.partial(near_kernel, step, layer, elements, unroll),
             out_shape=outs,
             in_specs=[VMEM] * len(operands),
             out_specs=[VMEM] * len(outs),
-            scratch_shapes=[pltpu.VMEM(wide_rows, f32)],
+            scratch_shapes=[
+                pltpu.VMEM(wide_rows, f32),
+                pltpu.VMEM((rows + 2 * edge if unroll == 1 else 16, block), bf16),
+            ],
             compiler_params=params(rows),
             cost_estimate=pl.CostEstimate(flops=14 * rows * block * block, bytes_accessed=10**7, transcendentals=0),
             name=f"near_{step}",
@@ -436,17 +453,17 @@
             name=f"middle_{step}",
         )(near, from_low, from_high, axial_flat)
         operands = [places, lists, near, traces, *arrived, face_flat]
-        scratch = [pltpu.VMEM(wide_rows, f32)]
         if step == 3:
-            operands += [here, *gram]
+            operands += [extra[1], extra[0]]
             outs = [shape((2 * vectors, LANES), f32)]
-            scratch += [pltpu.VMEM((size, size), f32)]
+            scratch = [pltpu.VMEM((size, size), f32)]
         else:
+            scratch = [pltpu.VMEM(wide_rows, f32)]
             operands += [selector]
             outs = [shape((rows, block)), shape((edge, block)), shape((edge, block)), shape((per, half, LANES))]
             outs += [shape((cap, half, LANES)) for cap in caps]
-        return pl.pallas_call(
-            functools.partial(far_kernel, step, shards, elements, unroll),
+        results = pl.pallas_call(
+            functools.partial(far_kernel, step, shards, elements, busy),
             out_shape=outs,
             in_specs=[SMEM] * 2 + [VMEM] * (len(operands) - 2),
             out_specs=[VMEM] * len(outs),
@@ -455,9 +472,10 @@
             cost_estimate=pl.CostEstimate(flops=2 * rows * block * block, bytes_accessed=10**7, transcendentals=0),
             name=f"far_{step}",
         )(*operands)
+        return [extra[2], *results] if step == 3 else results
 
     def run(cap):
-        caps = [min(per, cap * NEAR if r == 0 else cap) for r in range(shards - 1)]
+        caps = [min(per, cap + MORE if r == 0 else cap) for r in range(shards - 1)]
         sent = pl.pallas_call(
             picking_kernel,
             out_shape=[shape((cap, half, LANES)) for cap in caps],
@@ -467,8 +485,8 @@
             name="picking",
         )(lists, traces)
         first, *rest = one_round(1, caps, start_flat, low, high, traces, sent)
-        filtered, *rest = one_round(2, caps, first, rest[0], rest[1], rest[2], rest[3:])
-        (both,) = one_round(3, caps, filtered, rest[0], rest[1], rest[2], rest[3:])
+        second, *rest = one_round(2, caps, first, rest[0], rest[1], rest[2], rest[3:])
+        filtered, both = one_round(3, caps, second, rest[0], rest[1], rest[2], rest[3:])
         return filtered, both
 
     branches = [functools.partial(run, cap) for cap in (*CAPS, per)]

time: 93.6 us -> 88.2 us (0.942)
  waiting for transfers between devices: 21.8 us -> 16.7 us
    ppermute x12, waiting for transfers between devices: 9.69 us -> 4.06 us  [send_traces(): return lax.ppermute(value, 'xs', [(i, i ^ r) for i in range(count)])]
    pallas_call x3, Pallas kernels: 9.89 us -> 8.83 us  [one_round(): pl.pallas_call(functools.partial(far_kernel, step, shards, elements, busy...]
  transfers between devices with their start and end apart: 25 -> 25, of which waited for: 12 -> 12; matrix products, arithmetic and copies ran while one was open for 0% -> 0% of each run, Pallas kernels for 28% -> 30%
where the time goes in v3:
time: 88.2 us; the launch traced here: 88.1 us
  Pallas kernels  35.7 us (40%)
  starting transfers between devices  32.7 us (37%)
  waiting for transfers between devices  16.7 us (19%)
    pallas_call x3, Pallas kernels, one_round(): pl.pallas_call(functools.partial(near_kernel, step, layer, elements, unro...  18.4 us
    ppermute x12, starting transfers between devices, send_traces(): return lax.ppermute(value, 'xs', [(i, i ^ r) for i in range(count)])  16.6 us
    pallas_call x3, Pallas kernels, one_round(): pl.pallas_call(functools.partial(far_kernel, step, shards, elements, busy...  8.83 us
    ppermute x6, starting transfers between devices, rotate(): lax.ppermute(value, axis, [(i, (i + shift) % count) for i in range(count)])  8.07 us
    ppermute x7, starting transfers between devices, add_over(): lax.ppermute(value, axis, [(i, i ^ distance) for i in range(count)])  8.01 us
    ppermute x7, waiting for transfers between devices, add_over(): lax.ppermute(value, axis, [(i, i ^ distance) for i in range(count)])  6.36 us
    ppermute x6, waiting for transfers between devices, rotate(): lax.ppermute(value, axis, [(i, (i + shift) % count) for i in range(count)])  6.25 us
    pallas_call x3, Pallas kernels, one_round(): pl.pallas_call(functools.partial(middle_kernel, layer), out_shape=shape(w...  4.58 us
  transfers between devices with their start and end apart: 25, of which 12 were waited for; matrix products, arithmetic and copies ran while one was open for 0% of the time, Pallas kernels for 30%

profile of v3, /device:TPU:0, one launch (start us, length us, event | category | flops | bytes accessed | tf_op | source)
XLA Modules:
  0.0 88.1 jit_solution(12017461416032173440)
XLA Ops:
  0.6 0.7 add_select_fusion.3
  1.4 0.1 copy.20
  1.4 0.1 broadcast_in_dim.18
  1.6 5.1 %collective-permute-start.47 = (s32[32,128]{1,0:T(8,128)S(1)}, s32[32,128]{1,0:T(8,128)S(1)}, u32[]{:S(2)}, u32[]{:S(2)}) collective-permute-start(s32[32,128]{1,0:T(8,128)S(1)} %broadcast_in_dim.19.refs_0_), channel_id=1, source_target_pairs={{0,3},{1,2},{2,1},{3,0},{4,7},{5,6},{6,5},{7,4},{8,11},{9,10},{10,... | collective-permute-start | bytes 49160 | tf_op jit(solution)/shard_map/ppermute | solution.py:363
  6.6 0.6 collective-permute-start.45
  7.3 0.1 fusion.12.selector_ref
  7.4 2.6 %opening.1 = (bf16[512,512]{1,0:T(8,128)(2,1)S(1)}, bf16[512,512]{1,0:T(8,128)(2,1)S(1)}, bf16[32,64,128]{2,1,0:T(8,128)(2,1)S(1)}) custom-call(bf16[1024,512]{1,0:T(8,128)(2,1)} %bitcast.14, bf16[512,256]{1,0:T(8,128)(2,1)S(1)} %fusion.12.selector_ref), custom_call_target="tpu_custom_call" | custom-call | tf_op jit(solution)/shard_map/opening/pallas_call | solution.py:411
  10.0 1.3 %collective-permute-done.46.refs_2_ = s32[32,128]{1,0:T(8,128)S(1)} collective-permute-done((s32[32,128]{1,0:T(8,128)S(1)}, s32[32,128]{1,0:T(8,128)S(1)}, u32[]{:S(2)}, u32[]{:S(2)}) %collective-permute-start.46) | collective-permute-done | bytes 16416 | tf_op jit(solution)/shard_map/ppermute | solution.py:363
  11.3 0.4 pattern.1
  11.8 61.3 %conditional.1 = (bf16[1024,512]{1,0:T(8,128)(2,1)}, f32[32,128]{1,0:T(8,128)S(1)}) conditional(s32[]{:T(128)} %bitcast.1, (bf16[1024,512]{1,0:T(8,128)(2,1)}, bf16[8,512,512]{2,1,0:T(8,128)(2,1)}, bf16[4096,512]{1,0:T(8,128)(2,1)}, bf16[512,512]{1,0:T(8,128)(2,1)S(1)}, bf16[512,512]{1,0:T(8,128)(2,1)S(1)}, ...), branch_computations={%region_0.1_spmd, %region_1.2_spmd, %region_2.3_spmd} | conditional | flops 16911433728 | bytes 167595312 | solution.py:493
  11.9 2.6 %collective-permute-start.1 = (bf16[512,512]{1,0:T(8,128)(2,1)S(1)}, bf16[512,512]{1,0:T(8,128)(2,1)S(1)}, u32[]{:S(2)}, u32[]{:S(2)}) collective-permute-start(bf16[512,512]{1,0:T(8,128)(2,1)S(1)} %get-tuple-element.69), channel_id=1, source_target_pairs={{0,28},{4,0},{8,4},{12,8},{16,12},{20,16},{24,20},{28,24},{1,29},{... | collective-permute-start | bytes 1572872 | tf_op jit(solution)/shard_map/cond/branch_0_fun/ppermute | solution.py:357
  14.5 0.8 picking.3
  15.3 2.1 %collective-permute-start.3 = (bf16[9,64,128]{2,1,0:T(8,128)(2,1)S(1)}, bf16[9,64,128]{2,1,0:T(8,128)(2,1)S(1)}, u32[]{:S(2)}, u32[]{:S(2)}) collective-permute-start(bf16[9,64,128]{2,1,0:T(8,128)(2,1)S(1)} %get-tuple-element.72), channel_id=1, source_target_pairs={{0,2},{1,3},{2,0},{3,1},{4,6},{5,7},{6,4},{7,5},{8,10},{9,11},{10,... | collective-permute-start | bytes 442376 | tf_op jit(solution)/shard_map/cond/branch_0_fun/ppermute | solution.py:363
  17.4 0.5 collective-permute-start.4
  17.9 0.9 %collective-permute-start.2 = (bf16[12,64,128]{2,1,0:T(8,128)(2,1)S(1)}, bf16[12,64,128]{2,1,0:T(8,128)(2,1)S(1)}, u32[]{:S(2)}, u32[]{:S(2)}) collective-permute-start(bf16[12,64,128]{2,1,0:T(8,128)(2,1)S(1)} %get-tuple-element.71), channel_id=1, source_target_pairs={{0,1},{1,0},{2,3},{3,2},{4,5},{5,4},{6,7},{7,6},{8,9},{9,8},{10,11... | collective-permute-start | bytes 589832 | tf_op jit(solution)/shard_map/cond/branch_0_fun/ppermute | solution.py:363
  18.9 8.7 %near_1.3.near_ref = f32[4,1024,128]{2,1,0:T(8,128)S(1)} custom-call(bf16[1024,512]{1,0:T(8,128)(2,1)} %get-tuple-element.49.refs_0_.refs_3_, bf16[8,512,512]{2,1,0:T(8,128)(2,1)} %get-tuple-element.66.refs_1_, bf16[4096,512]{1,0:T(8,128)(2,1)} %get-tuple-element.67.refs_2_.axial_ref), custom_call_target="tpu_custom_call" | custom-call | flops 3758096384 | bytes 10000000 | tf_op jit(solution)/shard_map/cond/branch_0_fun/near_1/pallas_call | solution.py:432
  27.6 1.5 %middle_1.3.refs_2_ = f32[4,1024,128]{2,1,0:T(8,128)S(1)} custom-call(f32[4,1024,128]{2,1,0:T(8,128)S(1)} %near_1.3.near_ref, bf16[512,512]{1,0:T(8,128)(2,1)S(1)} %collective-permute-done.low_ref, bf16[512,512]{1,0:T(8,128)(2,1)S(1)} %collective-permute-done.1.high_ref, bf16[4096,512]{1,0:T(8,128)(2,1)S(1)} %copy-done), custom_call_target="tpu_custom_call", output_to_operand_aliasing={{}: (0, {})} | custom-call | flops 1342177280 | bytes 10000000 | tf_op jit(solution)/shard_map/cond/branch_0_fun/middle_1/pallas_call | solution.py:445
  29.2 0.5 collective-permute-done.2.refs_4_
  29.7 2.8 %far_1.3 = (bf16[1024,512]{1,0:T(8,128)(2,1)S(1)}, bf16[512,512]{1,0:T(8,128)(2,1)S(1)}, bf16[512,512]{1,0:T(8,128)(2,1)S(1)}, bf16[32,64,128]{2,1,0:T(8,128)(2,...) custom-call(s32[1,128]{1,0:T(1,128)S(1)} %get-tuple-element.47.refs_0_, ...), custom_call_target="tpu_custom_call" | custom-call | flops 536870912 | bytes 10000000 | tf_op jit(solution)/shard_map/cond/branch_0_fun/far_1/pallas_call | solution.py:465
  32.6 2.6 %collective-permute-start.6 = (bf16[512,512]{1,0:T(8,128)(2,1)S(1)}, bf16[512,512]{1,0:T(8,128)(2,1)S(1)}, u32[]{:S(2)}, u32[]{:S(2)}) collective-permute-start(bf16[512,512]{1,0:T(8,128)(2,1)S(1)} %get-tuple-element.78), channel_id=1, source_target_pairs={{0,28},{4,0},{8,4},{12,8},{16,12},{20,16},{24,20},{28,24},{1,29},{... | collective-permute-start | bytes 1572872 | tf_op jit(solution)/shard_map/cond/branch_0_fun/ppermute | solution.py:357
  35.2 2.5 %collective-permute-start.8 = (bf16[9,64,128]{2,1,0:T(8,128)(2,1)S(1)}, bf16[9,64,128]{2,1,0:T(8,128)(2,1)S(1)}, u32[]{:S(2)}, u32[]{:S(2)}) collective-permute-start(bf16[9,64,128]{2,1,0:T(8,128)(2,1)S(1)} %get-tuple-element.81), channel_id=1, source_target_pairs={{0,2},{1,3},{2,0},{3,1},{4,6},{5,7},{6,4},{7,5},{8,10},{9,11},{10,... | collective-permute-start | bytes 442376 | tf_op jit(solution)/shard_map/cond/branch_0_fun/ppermute | solution.py:363
  37.7 1.2 %collective-permute-start.9 = (bf16[9,64,128]{2,1,0:T(8,128)(2,1)S(1)}, bf16[9,64,128]{2,1,0:T(8,128)(2,1)S(1)}, u32[]{:S(2)}, u32[]{:S(2)}) collective-permute-start(bf16[9,64,128]{2,1,0:T(8,128)(2,1)S(1)} %get-tuple-element.82), channel_id=1, source_target_pairs={{0,3},{1,2},{2,1},{3,0},{4,7},{5,6},{6,5},{7,4},{8,11},{9,10},{10,... | collective-permute-start | bytes 442376 | tf_op jit(solution)/shard_map/cond/branch_0_fun/ppermute | solution.py:363
  38.9 4.9 %near_2.3.near_ref = f32[4,1024,128]{2,1,0:T(8,128)S(1)} custom-call(bf16[1024,512]{1,0:T(8,128)(2,1)S(1)} %get-tuple-element.76.refs_0_, bf16[8,512,512]{2,1,0:T(8,128)(2,1)S(1)} %copy-done.9, bf16[4096,512]{1,0:T(8,128)(2,1)S(1)} %copy-done, bf16[1024,512]{1,0:T(8,128)(2,1)S(1)} %copy-done.6), custom_call_target="tpu_custom_call" | custom-call | flops 3758096384 | bytes 10000000 | tf_op jit(solution)/shard_map/cond/branch_0_fun/near_2/pallas_call | solution.py:432
  43.8 3.1 %collective-permute-done.5.low_ref = bf16[512,512]{1,0:T(8,128)(2,1)S(1)} collective-permute-done((bf16[512,512]{1,0:T(8,128)(2,1)S(1)}, bf16[512,512]{1,0:T(8,128)(2,1)S(1)}, u32[]{:S(2)}, u32[]{:S(2)}) %collective-permute-start.5) | collective-permute-done | bytes 524320 | tf_op jit(solution)/shard_map/cond/branch_0_fun/ppermute | solution.py:357
  46.9 1.5 %middle_2.3.refs_2_ = f32[4,1024,128]{2,1,0:T(8,128)S(1)} custom-call(f32[4,1024,128]{2,1,0:T(8,128)S(1)} %near_2.3.near_ref, bf16[512,512]{1,0:T(8,128)(2,1)S(1)} %collective-permute-done.5.low_ref, bf16[512,512]{1,0:T(8,128)(2,1)S(1)} %collective-permute-done.6.high_ref, bf16[4096,512]{1,0:T(8,128)(2,1)S(1)} %copy-done), custom_call_target="tpu_custom_call", output_to_operand_aliasing={{}: (0, {})} | custom-call | flops 1342177280 | bytes 10000000 | tf_op jit(solution)/shard_map/cond/branch_0_fun/middle_2/pallas_call | solution.py:445
  48.4 1.1 %collective-permute-done.7.refs_4_ = bf16[12,64,128]{2,1,0:T(8,128)(2,1)S(1)} collective-permute-done((bf16[12,64,128]{2,1,0:T(8,128)(2,1)S(1)}, bf16[12,64,128]{2,1,0:T(8,128)(2,1)S(1)}, u32[]{:S(2)}, u32[]{:S(2)}) %collective-permute-start.7) | collective-permute-done | bytes 196640 | tf_op jit(solution)/shard_map/cond/branch_0_fun/ppermute | solution.py:363
  49.6 2.8 %far_2.3 = (bf16[1024,512]{1,0:T(8,128)(2,1)S(1)}, bf16[512,512]{1,0:T(8,128)(2,1)S(1)}, bf16[512,512]{1,0:T(8,128)(2,1)S(1)}, bf16[32,64,128]{2,1,0:T(8,128)(2,...) custom-call(s32[1,128]{1,0:T(1,128)S(1)} %get-tuple-element.47.refs_0_, ...), custom_call_target="tpu_custom_call" | custom-call | flops 536870912 | bytes 10000000 | tf_op jit(solution)/shard_map/cond/branch_0_fun/far_2/pallas_call | solution.py:465
  52.5 2.6 %collective-permute-start.11 = (bf16[512,512]{1,0:T(8,128)(2,1)S(1)}, bf16[512,512]{1,0:T(8,128)(2,1)S(1)}, u32[]{:S(2)}, u32[]{:S(2)}) collective-permute-start(bf16[512,512]{1,0:T(8,128)(2,1)S(1)} %get-tuple-element.88), channel_id=1, source_target_pairs={{0,28},{4,0},{8,4},{12,8},{16,12},{20,16},{24,20},{28,24},{1,29},{... | collective-permute-start | bytes 1572872 | tf_op jit(solution)/shard_map/cond/branch_0_fun/ppermute | solution.py:357
  55.1 2.4 %collective-permute-start.13 = (bf16[9,64,128]{2,1,0:T(8,128)(2,1)S(1)}, bf16[9,64,128]{2,1,0:T(8,128)(2,1)S(1)}, u32[]{:S(2)}, u32[]{:S(2)}) collective-permute-start(bf16[9,64,128]{2,1,0:T(8,128)(2,1)S(1)} %get-tuple-element.91), channel_id=1, source_target_pairs={{0,2},{1,3},{2,0},{3,1},{4,6},{5,7},{6,4},{7,5},{8,10},{9,11},{10,... | collective-permute-start | bytes 442376 | tf_op jit(solution)/shard_map/cond/branch_0_fun/ppermute | solution.py:363
  57.5 1.3 %collective-permute-start.14 = (bf16[9,64,128]{2,1,0:T(8,128)(2,1)S(1)}, bf16[9,64,128]{2,1,0:T(8,128)(2,1)S(1)}, u32[]{:S(2)}, u32[]{:S(2)}) collective-permute-start(bf16[9,64,128]{2,1,0:T(8,128)(2,1)S(1)} %get-tuple-element.92), channel_id=1, source_target_pairs={{0,3},{1,2},{2,1},{3,0},{4,7},{5,6},{6,5},{7,4},{8,11},{9,10},{10,... | collective-permute-start | bytes 442376 | tf_op jit(solution)/shard_map/cond/branch_0_fun/ppermute | solution.py:363
  58.8 4.9 %near_3.3 = (f32[4,1024,128]{2,1,0:T(8,128)S(1)}, f32[128,128]{1,0:T(8,128)S(1)}, bf16[8,128,512]{2,1,0:T(8,128)(2,1)S(1)}, bf16[1024,512]{1,0:T(8,128)(2,1)}) custom-call(bf16[1024,512]{1,0:T(8,128)(2,1)S(1)} %get-tuple-element.84.refs_0_, bf16[8,512,512]{2,1,0:T(8,128)(2,1)S(1)} %copy-done.9, bf16[4096,512]{1,0:T(8,128)(2,1)S(1)} %copy-done), custom_call_target="tpu_custom_call" | custom-call | flops 3758096384 | bytes 10000000 | tf_op jit(solution)/shard_map/cond/branch_0_fun/near_3/pallas_call | solution.py:432
  63.6 3.1 %collective-permute-done.10.low_ref = bf16[512,512]{1,0:T(8,128)(2,1)S(1)} collective-permute-done((bf16[512,512]{1,0:T(8,128)(2,1)S(1)}, bf16[512,512]{1,0:T(8,128)(2,1)S(1)}, u32[]{:S(2)}, u32[]{:S(2)}) %collective-permute-start.10) | collective-permute-done | bytes 524320 | tf_op jit(solution)/shard_map/cond/branch_0_fun/ppermute | solution.py:357
  66.8 1.5 %middle_3.3.refs_2_ = f32[4,1024,128]{2,1,0:T(8,128)S(1)} custom-call(f32[4,1024,128]{2,1,0:T(8,128)S(1)} %get-tuple-element.86.near_ref, bf16[512,512]{1,0:T(8,128)(2,1)S(1)} %collective-permute-done.10.low_ref, bf16[512,512]{1,0:T(8,128)(2,1)S(1)} %collective-permute-done.11.high_ref, bf16[4096,512]{1,0:T(8,128)(2,1)S(1)} %copy-done), custom_call_target="tpu_custom_call", output_to_operand_aliasing={{}: (0, {})} | custom-call | flops 1342177280 | bytes 10000000 | tf_op jit(solution)/shard_map/cond/branch_0_fun/middle_3/pallas_call | solution.py:445
  68.3 1.1 %collective-permute-done.12.refs_4_ = bf16[12,64,128]{2,1,0:T(8,128)(2,1)S(1)} collective-permute-done((bf16[12,64,128]{2,1,0:T(8,128)(2,1)S(1)}, bf16[12,64,128]{2,1,0:T(8,128)(2,1)S(1)}, u32[]{:S(2)}, u32[]{:S(2)}) %collective-permute-start.12) | collective-permute-done | bytes 196640 | tf_op jit(solution)/shard_map/cond/branch_0_fun/ppermute | solution.py:363
  69.4 3.2 %far_3.3 = f32[32,128]{1,0:T(8,128)S(1)} custom-call(s32[1,128]{1,0:T(1,128)S(1)} %get-tuple-element.47.refs_0_, s32[8,128]{1,0:T(8,128)S(1)} %get-tuple-element.48.lists_ref.refs_1_, f32[4,1024,128]{2,1,0:T(8,128)S(1)} %middle_3.3.refs_2_, bf16[32,64,128]{2,1,0:T(8,128)(2,1)S(1)} %get-tuple-element.89.refs_3_, ...), custom_call_target="tpu_custom_call" | custom-call | flops 536870912 | bytes 10000000 | tf_op jit(solution)/shard_map/cond/branch_0_fun/far_3/pallas_call | solution.py:465
  73.1 1.2 %collective-permute-done.48 = f32[32,128]{1,0:T(8,128)S(1)} collective-permute-done((f32[32,128]{1,0:T(8,128)S(1)}, f32[32,128]{1,0:T(8,128)S(1)}, u32[]{:S(2)}, u32[]{:S(2)}) %collective-permute-start.48) | collective-permute-done | bytes 16416 | tf_op jit(solution)/shard_map/ppermute | solution.py:373
  74.3 1.4 %collective-permute-start.51 = (f32[32,128]{1,0:T(8,128)S(1)}, f32[32,128]{1,0:T(8,128)S(1)}, u32[]{:S(2)}, u32[]{:S(2)}) collective-permute-start(f32[32,128]{1,0:T(8,128)S(1)} %add.146), channel_id=1, source_target_pairs={{0,24},{4,28},{8,16},{12,20},{16,8},{20,12},{24,0},{28,4},{1,25},{... | collective-permute-start | bytes 49160 | tf_op jit(solution)/shard_map/ppermute | solution.py:373
  75.7 0.7 collective-permute-start.50
  76.4 1.4 %collective-permute-start.49 = (f32[32,128]{1,0:T(8,128)S(1)}, f32[32,128]{1,0:T(8,128)S(1)}, u32[]{:S(2)}, u32[]{:S(2)}) collective-permute-start(f32[32,128]{1,0:T(8,128)S(1)} %add.146), channel_id=1, source_target_pairs={{0,8},{4,12},{8,0},{12,4},{16,24},{20,28},{24,16},{28,20},{1,9},{5... | collective-permute-start | bytes 49160 | tf_op jit(solution)/shard_map/ppermute | solution.py:373
  77.8 1.1 %collective-permute-done.51 = f32[32,128]{1,0:T(8,128)S(1)} collective-permute-done((f32[32,128]{1,0:T(8,128)S(1)}, f32[32,128]{1,0:T(8,128)S(1)}, u32[]{:S(2)}, u32[]{:S(2)}) %collective-permute-start.51) | collective-permute-done | bytes 16416 | tf_op jit(solution)/shard_map/ppermute | solution.py:373
  78.9 0.5 collective-permute-done.50
  79.5 0.7 collective-permute-done.49
  80.1 2.6 %collective-permute-start.54 = (f32[32,128]{1,0:T(8,128)S(1)}, f32[32,128]{1,0:T(8,128)S(1)}, u32[]{:S(2)}, u32[]{:S(2)}) collective-permute-start(f32[32,128]{1,0:T(8,128)S(1)} %add_add_fusion), channel_id=1, source_target_pairs={{0,3},{1,2},{2,1},{3,0},{4,7},{5,6},{6,5},{7,4},{8,11},{9,10},{10,... | collective-permute-start | bytes 49160 | tf_op jit(solution)/shard_map/ppermute | solution.py:373
  82.8 0.2 collective-permute-start.53
  83.0 1.6 %collective-permute-start.52 = (f32[32,128]{1,0:T(8,128)S(1)}, f32[32,128]{1,0:T(8,128)S(1)}, u32[]{:S(2)}, u32[]{:S(2)}) collective-permute-start(f32[32,128]{1,0:T(8,128)S(1)} %add_add_fusion), channel_id=1, source_target_pairs={{0,1},{1,0},{2,3},{3,2},{4,5},{5,4},{6,7},{7,6},{8,9},{9,8},{10,11... | collective-permute-start | bytes 49160 | tf_op jit(solution)/shard_map/ppermute | solution.py:373
  84.6 1.1 %collective-permute-done.54 = f32[32,128]{1,0:T(8,128)S(1)} collective-permute-done((f32[32,128]{1,0:T(8,128)S(1)}, f32[32,128]{1,0:T(8,128)S(1)}, u32[]{:S(2)}, u32[]{:S(2)}) %collective-permute-start.54) | collective-permute-done | bytes 16416 | tf_op jit(solution)/shard_map/ppermute | solution.py:373
  85.7 1.7 %collective-permute-done.53 = f32[32,128]{1,0:T(8,128)S(1)} collective-permute-done((f32[32,128]{1,0:T(8,128)S(1)}, f32[32,128]{1,0:T(8,128)S(1)}, u32[]{:S(2)}, u32[]{:S(2)}) %collective-permute-start.53) | collective-permute-done | bytes 16416 | tf_op jit(solution)/shard_map/ppermute | solution.py:373
  87.5 0.6 fusion.17
  (35 shorter events, 0.4 us)
Async XLA Ops:
  1.6 8.4 %collective-permute-start.47 = (s32[32,128]{1,0:T(8,128)S(1)}, s32[32,128]{1,0:T(8,128)S(1)}, u32[]{:S(2)}, u32[]{:S(2)}) collective-permute-start(s32[32,128]{1,0:T(8,128)S(1)} %broadcast_in_dim.19.refs_0_), channel_id=1, source_target_pairs={{0,3},{1,2},{2,1},{3,0},{4,7},{5,6},{6,5},{7,4},{8,11},{9,10},{10,... | collective-permute-start | bytes 49160 | tf_op jit(solution)/shard_map/ppermute | solution.py:363
  6.6 4.6 %collective-permute-start.46 = (s32[32,128]{1,0:T(8,128)S(1)}, s32[32,128]{1,0:T(8,128)S(1)}, u32[]{:S(2)}, u32[]{:S(2)}) collective-permute-start(s32[32,128]{1,0:T(8,128)S(1)} %broadcast_in_dim.19.refs_0_), channel_id=1, source_target_pairs={{0,2},{1,3},{2,0},{3,1},{4,6},{5,7},{6,4},{7,5},{8,10},{9,11},{10,... | collective-permute-start | bytes 49160 | tf_op jit(solution)/shard_map/ppermute | solution.py:363
  6.6 4.6 %collective-permute-start.45 = (s32[32,128]{1,0:T(8,128)S(1)}, s32[32,128]{1,0:T(8,128)S(1)}, u32[]{:S(2)}, u32[]{:S(2)}) collective-permute-start(s32[32,128]{1,0:T(8,128)S(1)} %broadcast_in_dim.19.refs_0_), channel_id=1, source_target_pairs={{0,1},{1,0},{2,3},{3,2},{4,5},{5,4},{6,7},{7,6},{8,9},{9,8},{10,11... | collective-permute-start | bytes 49160 | tf_op jit(solution)/shard_map/ppermute | solution.py:363
  11.8 15.8 %collective-permute-start = (bf16[512,512]{1,0:T(8,128)(2,1)S(1)}, bf16[512,512]{1,0:T(8,128)(2,1)S(1)}, u32[]{:S(2)}, u32[]{:S(2)}) collective-permute-start(bf16[512,512]{1,0:T(8,128)(2,1)S(1)} %get-tuple-element.68), channel_id=1, source_target_pairs={{0,4},{4,8},{8,12},{12,16},{16,20},{20,24},{24,28},{28,0},{1,5},{5... | collective-permute-start | bytes 1572872 | tf_op jit(solution)/shard_map/cond/branch_0_fun/ppermute | solution.py:357
  11.9 15.7 %collective-permute-start.1 = (bf16[512,512]{1,0:T(8,128)(2,1)S(1)}, bf16[512,512]{1,0:T(8,128)(2,1)S(1)}, u32[]{:S(2)}, u32[]{:S(2)}) collective-permute-start(bf16[512,512]{1,0:T(8,128)(2,1)S(1)} %get-tuple-element.69), channel_id=1, source_target_pairs={{0,28},{4,0},{8,4},{12,8},{16,12},{20,16},{24,20},{28,24},{1,29},{... | collective-permute-start | bytes 1572872 | tf_op jit(solution)/shard_map/cond/branch_0_fun/ppermute | solution.py:357
  15.3 13.8 %collective-permute-start.3 = (bf16[9,64,128]{2,1,0:T(8,128)(2,1)S(1)}, bf16[9,64,128]{2,1,0:T(8,128)(2,1)S(1)}, u32[]{:S(2)}, u32[]{:S(2)}) collective-permute-start(bf16[9,64,128]{2,1,0:T(8,128)(2,1)S(1)} %get-tuple-element.72), channel_id=1, source_target_pairs={{0,2},{1,3},{2,0},{3,1},{4,6},{5,7},{6,4},{7,5},{8,10},{9,11},{10,... | collective-permute-start | bytes 442376 | tf_op jit(solution)/shard_map/cond/branch_0_fun/ppermute | solution.py:363
  17.4 11.7 %collective-permute-start.4 = (bf16[9,64,128]{2,1,0:T(8,128)(2,1)S(1)}, bf16[9,64,128]{2,1,0:T(8,128)(2,1)S(1)}, u32[]{:S(2)}, u32[]{:S(2)}) collective-permute-start(bf16[9,64,128]{2,1,0:T(8,128)(2,1)S(1)} %get-tuple-element.73), channel_id=1, source_target_pairs={{0,3},{1,2},{2,1},{3,0},{4,7},{5,6},{6,5},{7,4},{8,11},{9,10},{10,... | collective-permute-start | bytes 442376 | tf_op jit(solution)/shard_map/cond/branch_0_fun/ppermute | solution.py:363
  17.9 11.7 %collective-permute-start.2 = (bf16[12,64,128]{2,1,0:T(8,128)(2,1)S(1)}, bf16[12,64,128]{2,1,0:T(8,128)(2,1)S(1)}, u32[]{:S(2)}, u32[]{:S(2)}) collective-permute-start(bf16[12,64,128]{2,1,0:T(8,128)(2,1)S(1)} %get-tuple-element.71), channel_id=1, source_target_pairs={{0,1},{1,0},{2,3},{3,2},{4,5},{5,4},{6,7},{7,6},{8,9},{9,8},{10,11... | collective-permute-start | bytes 589832 | tf_op jit(solution)/shard_map/cond/branch_0_fun/ppermute | solution.py:363
  18.9 8.7 %copy-start = (bf16[4096,512]{1,0:T(8,128)(2,1)S(1)}, bf16[4096,512]{1,0:T(8,128)(2,1)}, u32[]{:S(2)}) copy-start(bf16[4096,512]{1,0:T(8,128)(2,1)} %get-tuple-element.67.refs_2_.axial_ref) | copy-start | bytes 12582916 | tf_op jit(solution)/shard_map/cond
  27.6 2.1 %copy-start.3 = (bf16[8,256,512]{2,1,0:T(8,128)(2,1)S(1)}, bf16[8,256,512]{2,1,0:T(8,128)(2,1)}, u32[]{:S(2)}) copy-start(bf16[8,256,512]{2,1,0:T(8,128)(2,1)} %get-tuple-element.74.refs_7_) | copy-start | bytes 6291460 | tf_op jit(solution)/shard_map/cond
  29.7 9.2 %copy-start.6 = (bf16[1024,512]{1,0:T(8,128)(2,1)S(1)}, bf16[1024,512]{1,0:T(8,128)(2,1)}, u32[]{:S(2)}) copy-start(bf16[1024,512]{1,0:T(8,128)(2,1)} %get-tuple-element.49.refs_0_.refs_3_) | copy-start | bytes 3145732 | tf_op jit(solution)/shard_map/cond
  29.7 9.2 %copy-start.9 = (bf16[8,512,512]{2,1,0:T(8,128)(2,1)S(1)}, bf16[8,512,512]{2,1,0:T(8,128)(2,1)}, u32[]{:S(2)}) copy-start(bf16[8,512,512]{2,1,0:T(8,128)(2,1)} %get-tuple-element.66.refs_1_) | copy-start | bytes 12582916 | tf_op jit(solution)/shard_map/cond
  32.5 14.4 %collective-permute-start.5 = (bf16[512,512]{1,0:T(8,128)(2,1)S(1)}, bf16[512,512]{1,0:T(8,128)(2,1)S(1)}, u32[]{:S(2)}, u32[]{:S(2)}) collective-permute-start(bf16[512,512]{1,0:T(8,128)(2,1)S(1)} %get-tuple-element.77), channel_id=1, source_target_pairs={{0,4},{4,8},{8,12},{12,16},{16,20},{20,24},{24,28},{28,0},{1,5},{5... | collective-permute-start | bytes 1572872 | tf_op jit(solution)/shard_map/cond/branch_0_fun/ppermute | solution.py:357
  32.6 14.3 %collective-permute-start.6 = (bf16[512,512]{1,0:T(8,128)(2,1)S(1)}, bf16[512,512]{1,0:T(8,128)(2,1)S(1)}, u32[]{:S(2)}, u32[]{:S(2)}) collective-permute-start(bf16[512,512]{1,0:T(8,128)(2,1)S(1)} %get-tuple-element.78), channel_id=1, source_target_pairs={{0,28},{4,0},{8,4},{12,8},{16,12},{20,16},{24,20},{28,24},{1,29},{... | collective-permute-start | bytes 1572872 | tf_op jit(solution)/shard_map/cond/branch_0_fun/ppermute | solution.py:357
  35.2 13.2 %collective-permute-start.8 = (bf16[9,64,128]{2,1,0:T(8,128)(2,1)S(1)}, bf16[9,64,128]{2,1,0:T(8,128)(2,1)S(1)}, u32[]{:S(2)}, u32[]{:S(2)}) collective-permute-start(bf16[9,64,128]{2,1,0:T(8,128)(2,1)S(1)} %get-tuple-element.81), channel_id=1, source_target_pairs={{0,2},{1,3},{2,0},{3,1},{4,6},{5,7},{6,4},{7,5},{8,10},{9,11},{10,... | collective-permute-start | bytes 442376 | tf_op jit(solution)/shard_map/cond/branch_0_fun/ppermute | solution.py:363
  37.7 10.8 %collective-permute-start.9 = (bf16[9,64,128]{2,1,0:T(8,128)(2,1)S(1)}, bf16[9,64,128]{2,1,0:T(8,128)(2,1)S(1)}, u32[]{:S(2)}, u32[]{:S(2)}) collective-permute-start(bf16[9,64,128]{2,1,0:T(8,128)(2,1)S(1)} %get-tuple-element.82), channel_id=1, source_target_pairs={{0,3},{1,2},{2,1},{3,0},{4,7},{5,6},{6,5},{7,4},{8,11},{9,10},{10,... | collective-permute-start | bytes 442376 | tf_op jit(solution)/shard_map/cond/branch_0_fun/ppermute | solution.py:363
  38.9 10.7 %collective-permute-start.7 = (bf16[12,64,128]{2,1,0:T(8,128)(2,1)S(1)}, bf16[12,64,128]{2,1,0:T(8,128)(2,1)S(1)}, u32[]{:S(2)}, u32[]{:S(2)}) collective-permute-start(bf16[12,64,128]{2,1,0:T(8,128)(2,1)S(1)} %get-tuple-element.80), channel_id=1, source_target_pairs={{0,1},{1,0},{2,3},{3,2},{4,5},{5,4},{6,7},{7,6},{8,9},{9,8},{10,11... | collective-permute-start | bytes 589832 | tf_op jit(solution)/shard_map/cond/branch_0_fun/ppermute | solution.py:363
  52.4 14.4 %collective-permute-start.10 = (bf16[512,512]{1,0:T(8,128)(2,1)S(1)}, bf16[512,512]{1,0:T(8,128)(2,1)S(1)}, u32[]{:S(2)}, u32[]{:S(2)}) collective-permute-start(bf16[512,512]{1,0:T(8,128)(2,1)S(1)} %get-tuple-element.87), channel_id=1, source_target_pairs={{0,4},{4,8},{8,12},{12,16},{16,20},{20,24},{24,28},{28,0},{1,5},{5... | collective-permute-start | bytes 1572872 | tf_op jit(solution)/shard_map/cond/branch_0_fun/ppermute | solution.py:357
  52.5 14.3 %collective-permute-start.11 = (bf16[512,512]{1,0:T(8,128)(2,1)S(1)}, bf16[512,512]{1,0:T(8,128)(2,1)S(1)}, u32[]{:S(2)}, u32[]{:S(2)}) collective-permute-start(bf16[512,512]{1,0:T(8,128)(2,1)S(1)} %get-tuple-element.88), channel_id=1, source_target_pairs={{0,28},{4,0},{8,4},{12,8},{16,12},{20,16},{24,20},{28,24},{1,29},{... | collective-permute-start | bytes 1572872 | tf_op jit(solution)/shard_map/cond/branch_0_fun/ppermute | solution.py:357
  55.1 13.2 %collective-permute-start.13 = (bf16[9,64,128]{2,1,0:T(8,128)(2,1)S(1)}, bf16[9,64,128]{2,1,0:T(8,128)(2,1)S(1)}, u32[]{:S(2)}, u32[]{:S(2)}) collective-permute-start(bf16[9,64,128]{2,1,0:T(8,128)(2,1)S(1)} %get-tuple-element.91), channel_id=1, source_target_pairs={{0,2},{1,3},{2,0},{3,1},{4,6},{5,7},{6,4},{7,5},{8,10},{9,11},{10,... | collective-permute-start | bytes 442376 | tf_op jit(solution)/shard_map/cond/branch_0_fun/ppermute | solution.py:363
  57.5 10.8 %collective-permute-start.14 = (bf16[9,64,128]{2,1,0:T(8,128)(2,1)S(1)}, bf16[9,64,128]{2,1,0:T(8,128)(2,1)S(1)}, u32[]{:S(2)}, u32[]{:S(2)}) collective-permute-start(bf16[9,64,128]{2,1,0:T(8,128)(2,1)S(1)} %get-tuple-element.92), channel_id=1, source_target_pairs={{0,3},{1,2},{2,1},{3,0},{4,7},{5,6},{6,5},{7,4},{8,11},{9,10},{10,... | collective-permute-start | bytes 442376 | tf_op jit(solution)/shard_map/cond/branch_0_fun/ppermute | solution.py:363
  58.8 10.7 %collective-permute-start.12 = (bf16[12,64,128]{2,1,0:T(8,128)(2,1)S(1)}, bf16[12,64,128]{2,1,0:T(8,128)(2,1)S(1)}, u32[]{:S(2)}, u32[]{:S(2)}) collective-permute-start(bf16[12,64,128]{2,1,0:T(8,128)(2,1)S(1)} %get-tuple-element.90), channel_id=1, source_target_pairs={{0,1},{1,0},{2,3},{3,2},{4,5},{5,4},{6,7},{7,6},{8,9},{9,8},{10,11... | collective-permute-start | bytes 589832 | tf_op jit(solution)/shard_map/cond/branch_0_fun/ppermute | solution.py:363
  73.0 1.2 %collective-permute-start.48 = (f32[32,128]{1,0:T(8,128)S(1)}, f32[32,128]{1,0:T(8,128)S(1)}, u32[]{:S(2)}, u32[]{:S(2)}) collective-permute-start(f32[32,128]{1,0:T(8,128)S(1)} %get-tuple-element.177), channel_id=1, source_target_pairs={{0,4},{4,0},{8,12},{12,8},{16,20},{20,16},{24,28},{28,24},{1,5},{5... | collective-permute-start | bytes 49160 | tf_op jit(solution)/shard_map/ppermute | solution.py:373
  74.3 4.6 %collective-permute-start.51 = (f32[32,128]{1,0:T(8,128)S(1)}, f32[32,128]{1,0:T(8,128)S(1)}, u32[]{:S(2)}, u32[]{:S(2)}) collective-permute-start(f32[32,128]{1,0:T(8,128)S(1)} %add.146), channel_id=1, source_target_pairs={{0,24},{4,28},{8,16},{12,20},{16,8},{20,12},{24,0},{28,4},{1,25},{... | collective-permute-start | bytes 49160 | tf_op jit(solution)/shard_map/ppermute | solution.py:373
  75.7 3.7 %collective-permute-start.50 = (f32[32,128]{1,0:T(8,128)S(1)}, f32[32,128]{1,0:T(8,128)S(1)}, u32[]{:S(2)}, u32[]{:S(2)}) collective-permute-start(f32[32,128]{1,0:T(8,128)S(1)} %add.146), channel_id=1, source_target_pairs={{0,16},{4,20},{8,24},{12,28},{16,0},{20,4},{24,8},{28,12},{1,17},{... | collective-permute-start | bytes 49160 | tf_op jit(solution)/shard_map/ppermute | solution.py:373
  76.4 3.7 %collective-permute-start.49 = (f32[32,128]{1,0:T(8,128)S(1)}, f32[32,128]{1,0:T(8,128)S(1)}, u32[]{:S(2)}, u32[]{:S(2)}) collective-permute-start(f32[32,128]{1,0:T(8,128)S(1)} %add.146), channel_id=1, source_target_pairs={{0,8},{4,12},{8,0},{12,4},{16,24},{20,28},{24,16},{28,20},{1,9},{5... | collective-permute-start | bytes 49160 | tf_op jit(solution)/shard_map/ppermute | solution.py:373
  80.1 5.6 %collective-permute-start.54 = (f32[32,128]{1,0:T(8,128)S(1)}, f32[32,128]{1,0:T(8,128)S(1)}, u32[]{:S(2)}, u32[]{:S(2)}) collective-permute-start(f32[32,128]{1,0:T(8,128)S(1)} %add_add_fusion), channel_id=1, source_target_pairs={{0,3},{1,2},{2,1},{3,0},{4,7},{5,6},{6,5},{7,4},{8,11},{9,10},{10,... | collective-permute-start | bytes 49160 | tf_op jit(solution)/shard_map/ppermute | solution.py:373
  82.8 4.7 %collective-permute-start.53 = (f32[32,128]{1,0:T(8,128)S(1)}, f32[32,128]{1,0:T(8,128)S(1)}, u32[]{:S(2)}, u32[]{:S(2)}) collective-permute-start(f32[32,128]{1,0:T(8,128)S(1)} %add_add_fusion), channel_id=1, source_target_pairs={{0,2},{1,3},{2,0},{3,1},{4,6},{5,7},{6,4},{7,5},{8,10},{9,11},{10,... | collective-permute-start | bytes 49160 | tf_op jit(solution)/shard_map/ppermute | solution.py:373
  83.0 4.5 %collective-permute-start.52 = (f32[32,128]{1,0:T(8,128)S(1)}, f32[32,128]{1,0:T(8,128)S(1)}, u32[]{:S(2)}, u32[]{:S(2)}) collective-permute-start(f32[32,128]{1,0:T(8,128)S(1)} %add_add_fusion), channel_id=1, source_target_pairs={{0,1},{1,0},{2,3},{3,2},{4,5},{5,4},{6,7},{7,6},{8,9},{9,8},{10,11... | collective-permute-start | bytes 49160 | tf_op jit(solution)/shard_map/ppermute | solution.py:373

commit v4 on v2

--- a/solution.py
+++ b/solution.py
@@ -15,7 +15,7 @@
 CAPS = (9, 12)
 ROW_TILE = 256
 UNROLL = 8
-NEAR = 2
+MORE = 3
 
 shift_center = 0.3
 half_width = 1.2
@@ -89,13 +89,13 @@
     each(rows // tile, lambda i: body(pl.ds(aligned(i * tile, tile), tile)))
 
 
-def pick_traces(lists_ref, traces_ref, sent_refs):
+def pick_traces(lists_ref, traces_ref, sent_refs, unroll):
     for r, sent in enumerate(sent_refs):
 
         def body(j, r=r, sent=sent):
             sent[j] = traces_ref[lists_ref[r, j]]
 
-        each(sent.shape[0], body)
+        each(sent.shape[0], body, sent.shape[0] if unroll > 1 else 1)
 
 
 def lifted_rows(e, refs_ref, traces_ref, arrived_refs):
@@ -119,26 +119,36 @@
     return both.astype(bf16)
 
 
-def opening_kernel(elements, unroll, start_ref, selector_ref, low_ref, high_ref, traces_ref, wide):
-    rows = start_ref.shape[0]
-    edge = low_ref.shape[0]
-    low_ref[...] = start_ref[:edge]
-    high_ref[...] = start_ref[rows - edge :]
-
-    def widen(index):
-        write_wide(wide, index, start_ref[index].astype(f32))
-
-    each_tile(rows, ROW_TILE, widen)
+def keep_rows(e, new, out_ref, low_ref, high_ref):
+    edge = low_ref.shape[1]
+    out_ref[e] = new
+    low_ref[e] = new[:edge]
+    high_ref[e] = new[new.shape[0] - edge :]
+
+
+def opening_kernel(elements, start_hbm, selector_ref, out_ref, low_ref, high_ref, traces_ref, begun, wide, sems):
+    parts = sems.shape[0]
+    tile = begun.shape[0] // parts
+    loads = []
+    for i in range(parts):
+        index = pl.ds(i * tile, tile)
+        loads.append(pltpu.make_async_copy(start_hbm.at[index], begun.at[index], sems.at[i]))
+        loads[-1].start()
+    for i, load in enumerate(loads):
+        load.wait()
+        index = pl.ds(i * tile, tile)
+        write_wide(wide, index, begun[index, :].astype(f32))
 
     def element(e):
         own = read_wide(wide, of_element(wide, e, elements)).astype(bf16)
+        keep_rows(e, own, out_ref, low_ref, high_ref)
         store_traces(e, dot(own, selector_ref[...]), traces_ref)
 
-    each(elements, element, unroll)
-
-
-def picking_kernel(lists_ref, traces_ref, *sent_refs):
-    pick_traces(lists_ref, traces_ref, sent_refs)
+    each(elements, element, elements)
+
+
+def picking_kernel(unroll, lists_ref, traces_ref, *sent_refs):
+    pick_traces(lists_ref, traces_ref, sent_refs, unroll)
 
 
 def paired(shards):
@@ -178,7 +188,7 @@
     owner = lax.broadcasted_iota(jnp.int32, total.shape, 1) // per
     number = lax.broadcasted_iota(jnp.int32, total.shape, 0)
     permute = permute_of(asker_of(me, number, shards), owner, shards)
-    weighed = jnp.where(permute == 1, total * (1.0 / NEAR), total)
+    weighed = jnp.where(permute == 1, total - MORE, total)
     weighed = jnp.where((permute == 0) | (number >= shards), 0.0, weighed)
     most = jnp.max(jnp.max(weighed, axis=1, keepdims=True), axis=0, keepdims=True)
     level = sum((most > cap).astype(jnp.int32) for cap in CAPS)
@@ -203,67 +213,83 @@
     places_ref[...] = turned.astype(jnp.int32)
 
 
-def add_to(acc_ref, index, value):
-    write_wide(acc_ref, index, read_wide(acc_ref, index) + value)
-
-
-def near_kernel(step, layer, elements, unroll, *refs):
+def add_offset(reach, position, begin, source, values_ref, axial_ref, acc_ref):
+    elements, _, block = acc_ref.shape
+    values = values_ref[:, source : source + reach].reshape(elements * reach, block)
+    product = dot(values, axial_ref[position * block : (position + 1) * block])
+    acc_ref[:, begin : begin + reach] += product.reshape(elements, reach, block)
+
+
+def near_kernel(step, vectors, unroll, *refs):
+    refs = list(refs)
+    here_ref, diag_ref, axial_ref = refs[:3]
     if step == 2:
-        here_ref, diag_ref, axial_ref, start_ref, acc_ref, wide = refs
+        start_ref, acc_ref, ext = refs[3:]
     elif step == 3:
-        here_ref, diag_ref, axial_ref, acc_ref, gram_ref, wide = refs
+        acc_ref, gram_ref, copy_ref, ext, wide = refs[3:]
+        gram_ref[...] = jnp.zeros_like(gram_ref)
     else:
-        here_ref, diag_ref, axial_ref, acc_ref, wide = refs
-    rows, block = here_ref.shape
-    tile = 2 * layer
-    if step == 3:
-        gram_ref[...] = jnp.zeros_like(gram_ref)
-
-    def widen(i):
-        index = pl.ds(aligned(i * tile, tile), tile)
-        write_wide(wide, index, here_ref[index, :].astype(f32))
-
-    each(rows // tile, widen)
+        acc_ref, ext = refs[3:]
+    elements, size, block = here_ref.shape
 
     def element(e):
-        index = of_element(wide, e, elements)
-        own = read_wide(wide, index).astype(bf16)
-        write_wide(acc_ref, index, dot(own, diag_ref[e]))
+        own = here_ref[e]
+        total = dot(own, diag_ref[e])
         if step == 3:
             gram_ref[...] += across(own, own)
+            write_wide(wide, of_element(wide, e, elements), own.astype(f32))
+        else:
+            total -= shift_center * own.astype(f32)
+        if step == 2:
+            total -= (half_width / 2.0) * start_ref[e].astype(f32)
+        acc_ref[e] = total
 
     each(elements, element, unroll)
-
-    layers = rows // layer
-    for offset in [*range(-HW, 0), *range(1, HW + 1)]:
-        if abs(offset) < layers:
-            begin, end = max(0, -offset) * layer, (layers - max(0, offset)) * layer
-            position = (offset + HW - (offset > 0)) * block
-            values = here_ref[begin + offset * layer : end + offset * layer]
-            add_to(acc_ref, slice(begin, end), dot(values, axial_ref[position : position + block]))
-
-    if step != 3:
-
-        def along(i):
-            index = pl.ds(aligned(i * tile, tile), tile)
-            total = read_wide(acc_ref, index) - shift_center * read_wide(wide, index)
-            if step == 2:
-                total -= (half_width / 2.0) * start_ref[index, :].astype(f32)
-            write_wide(acc_ref, index, total)
-
-        each(rows // tile, along)
-
-
-def middle_kernel(layer, near_ref, low_ref, high_ref, axial_ref, acc_ref):
+    if unroll > 1:
+        for offset in [*range(-HW, 0), *range(1, HW + 1)]:
+            shift = abs(offset) * vectors
+            if shift < size:
+                begin, source = (shift, 0) if offset < 0 else (0, shift)
+                position = offset + HW - (offset > 0)
+                add_offset(size - shift, position, begin, source, here_ref, axial_ref, acc_ref)
+    else:
+        edge = HW * vectors
+
+        def wider(e):
+            ext[e, :edge] = jnp.zeros((edge, block), bf16)
+            ext[e, edge : edge + size] = here_ref[e]
+            ext[e, edge + size :] = jnp.zeros((edge, block), bf16)
+
+        each(elements, wider)
+
+        def offset(p):
+            begin = aligned((p + jnp.where(p < HW, 0, 1)) * vectors, vectors)
+            weights = axial_ref[pl.ds(aligned(p * block, block), block), :]
+
+            def along(e):
+                acc_ref[e] += dot(ext[e, pl.ds(begin, size), :], weights)
+
+            each(elements, along)
+
+        each(2 * HW, offset)
+    if step == 3:
+
+        def narrow(index):
+            copy_ref[index, :] = read_wide(wide, index).astype(bf16)
+
+        each_tile(copy_ref.shape[0], ROW_TILE, narrow)
+
+
+def middle_kernel(side, vectors, near_ref, edge_ref, axial_ref, acc_ref):
     del near_ref
-    edge, block = low_ref.shape
-    rows = acc_ref.shape[1]
-    for reach in range(1, HW + 1):
-        far = reach * layer
-        below = dot(low_ref[edge - far :], axial_ref[(HW - reach) * block : (HW - reach + 1) * block])
-        add_to(acc_ref, slice(0, far), below)
-        above = dot(high_ref[:far], axial_ref[(HW + reach - 1) * block : (HW + reach) * block])
-        add_to(acc_ref, slice(rows - far, rows), above)
+    size = acc_ref.shape[1]
+    edge = edge_ref.shape[1]
+    for layers in range(1, HW + 1):
+        reach = layers * vectors
+        if side == 0:
+            add_offset(reach, HW - layers, 0, edge - reach, edge_ref, axial_ref, acc_ref)
+        else:
+            add_offset(reach, HW + layers - 1, size - reach, 0, edge_ref, axial_ref, acc_ref)
 
 
 def across(a, b):
@@ -277,45 +303,29 @@
     arrived_refs = take(shards - 1)
     (face_ref,) = take(1)
     if step == 3:
-        here_ref, gram_ref, out_ref, wide, projected = take(5)
+        here_ref, gram_ref, out_ref, projected = take(4)
         projected[...] = jnp.zeros_like(projected)
-
-        def widen(index):
-            write_wide(wide, index, here_ref[index, :].astype(f32))
-
-        each_tile(here_ref.shape[0], ROW_TILE, widen)
     else:
         selector_ref, out_ref, out_low_ref, out_high_ref, out_traces_ref = take(5)
         sent_refs = take(shards - 1)
-        (wide,) = take(1)
     scale = {1: 1.0 / half_width, 2: 2.0 / half_width, 3: 1.0}[step]
 
     def element(e):
-        index = of_element(wide, e, elements)
         lifted = lifted_rows(e, places_ref, traces_ref, arrived_refs)
-        total = (read_wide(near_ref, index) + dot(lifted, face_ref[e])) * scale
+        total = (near_ref[e] + dot(lifted, face_ref[e])) * scale
         if step == 3:
-            own = read_wide(wide, index).astype(bf16)
+            own = here_ref[e]
             upper = total.astype(bf16)
             lower = (total - upper.astype(f32)).astype(bf16)
             projected[...] += across(own, upper) + across(own, lower)
             return
         new = total.astype(bf16)
-        write_wide(wide, index, new.astype(f32))
+        keep_rows(e, new, out_ref, out_low_ref, out_high_ref)
         store_traces(e, dot(new, selector_ref[...]), out_traces_ref)
 
     each(elements, element, unroll)
     if step != 3:
-        rows = out_ref.shape[0]
-        edge = out_low_ref.shape[0]
-        pick_traces(lists_ref, out_traces_ref, sent_refs)
-
-        def narrow(index):
-            out_ref[index, :] = read_wide(wide, index).astype(bf16)
-
-        each_tile(rows, ROW_TILE, narrow)
-        out_low_ref[...] = out_ref[:edge]
-        out_high_ref[...] = out_ref[rows - edge :]
+        pick_traces(lists_ref, out_traces_ref, sent_refs, unroll)
         return
 
     size = projected.shape[0]
@@ -374,11 +384,7 @@
     shards = lax.axis_size("xs")
     me = lax.axis_index("xs").astype(jnp.int32)
     per = elements * F
-    layer = vectors * elements
-    rows = layers * layer
-    edge = HW * layer
-    half = layers * vectors // 2
-    wide_rows = (block // LANES, rows, LANES)
+    rows = layers * vectors * elements
     face_flat = face_blocks.reshape(elements, F * TR, block)
     axial_flat = axial_blocks.reshape(2 * HW * block, block)
     selector = trace_selector(block)
@@ -397,55 +403,70 @@
     )(*all_codes, me.reshape(1))
 
     start_flat = start_vectors.reshape(rows, block)
-    low, high, traces = pl.pallas_call(
-        functools.partial(opening_kernel, elements, UNROLL),
-        out_shape=[shape((edge, block)), shape((edge, block)), shape((per, half, LANES))],
-        in_specs=[VMEM] * 2,
-        out_specs=[VMEM] * 3,
-        scratch_shapes=[pltpu.VMEM(wide_rows, f32)],
+    size, edge = layers * vectors, HW * vectors
+    field, side = shape((elements, size, block)), shape((elements, edge, block))
+    start, low, high, traces = pl.pallas_call(
+        functools.partial(opening_kernel, elements),
+        out_shape=[field, side, side, shape((per, size // 2, LANES))],
+        in_specs=[ANY, VMEM],
+        out_specs=[VMEM] * 4,
+        scratch_shapes=[
+            pltpu.VMEM((rows, block), bf16),
+            pltpu.VMEM((block // LANES, rows, LANES), f32),
+            pltpu.SemaphoreType.DMA((4,)),
+        ],
         compiler_params=params(rows),
         name="opening",
-    )(start_flat, selector)
+    )(start_vectors.reshape(rows, block), selector)
+
+    def unroll_of(caps):
+        return 1 if caps[-1] == per else UNROLL if caps[-1] == CAPS[0] else UNROLL // 4
 
     def one_round(step, caps, here, low, high, traces, sent):
-        unroll = 1 if min(caps) == per else UNROLL
+        unroll = unroll_of(caps)
         arrived = [send_traces(s, r + 1) for r, s in enumerate(sent)]
         from_low = rotate(high, "pipe", 1)
         from_high = rotate(low, "pipe", -1)
-        size = layers * vectors
-        operands = [here, diag_blocks, axial_flat] + [start_flat] * (step == 2)
-        outs = [shape(wide_rows, f32)] + [shape((size, size), f32)] * (step == 3)
-        near, *gram = pl.pallas_call(
-            functools.partial(near_kernel, step, layer, elements, unroll),
+        operands = [here, diag_blocks, axial_flat] + [start] * (step == 2)
+        outs = [shape((elements, size, block), f32)]
+        scratch = [pltpu.VMEM((elements, size + 2 * edge, block) if unroll == 1 else (16, LANES), bf16)]
+        if step == 3:
+            outs += [shape((size, size), f32), shape((rows, block))]
+            scratch += [pltpu.VMEM((block // LANES, rows, LANES), f32)]
+        near, *more = pl.pallas_call(
+            functools.partial(near_kernel, step, vectors, unroll),
             out_shape=outs,
             in_specs=[VMEM] * len(operands),
             out_specs=[VMEM] * len(outs),
-            scratch_shapes=[pltpu.VMEM(wide_rows, f32)],
+            scratch_shapes=scratch,
             compiler_params=params(rows),
             cost_estimate=pl.CostEstimate(flops=14 * rows * block * block, bytes_accessed=10**7, transcendentals=0),
             name=f"near_{step}",
         )(*operands)
-        near = pl.pallas_call(
-            functools.partial(middle_kernel, layer),
-            out_shape=shape(wide_rows, f32),
-            in_specs=[VMEM] * 4,
-            out_specs=VMEM,
-            input_output_aliases={0: 0},
-            compiler_params=params(rows),
-            cost_estimate=pl.CostEstimate(flops=5 * rows * block * block, bytes_accessed=10**7, transcendentals=0),
-            name=f"middle_{step}",
-        )(near, from_low, from_high, axial_flat)
+        for which, arriving in enumerate((from_low, from_high)):
+            near = pl.pallas_call(
+                functools.partial(middle_kernel, which, vectors),
+                out_shape=shape((elements, size, block), f32),
+                in_specs=[VMEM] * 3,
+                out_specs=VMEM,
+                input_output_aliases={0: 0},
+                compiler_params=params(rows),
+                cost_estimate=pl.CostEstimate(
+                    flops=5 * rows * block * block // 2, bytes_accessed=10**7, transcendentals=0
+                ),
+                name=f"middle_{step}",
+            )(near, arriving, axial_flat)
         operands = [places, lists, near, traces, *arrived, face_flat]
-        scratch = [pltpu.VMEM(wide_rows, f32)]
+        scratch = []
         if step == 3:
-            operands += [here, *gram]
+            operands += [here, more[0]]
             outs = [shape((2 * vectors, LANES), f32)]
-            scratch += [pltpu.VMEM((size, size), f32)]
+            scratch = [pltpu.VMEM((size, size), f32)]
         else:
             operands += [selector]
-            outs = [shape((rows, block)), shape((edge, block)), shape((edge, block)), shape((per, half, LANES))]
-            outs += [shape((cap, half, LANES)) for cap in caps]
-        return pl.pallas_call(
+            outs = [field, side, side, shape((per, size // 2, LANES))]
+            outs += [shape((cap, size // 2, LANES)) for cap in caps]
+        results = pl.pallas_call(
             functools.partial(far_kernel, step, shards, elements, unroll),
             out_shape=outs,
             in_specs=[SMEM] * 2 + [VMEM] * (len(operands) - 2),
@@ -455,20 +476,22 @@
             cost_estimate=pl.CostEstimate(flops=2 * rows * block * block, bytes_accessed=10**7, transcendentals=0),
             name=f"far_{step}",
         )(*operands)
+        return [more[1], *results] if step == 3 else results
 
     def run(cap):
-        caps = [min(per, cap * NEAR if r == 0 else cap) for r in range(shards - 1)]
+        caps = [min(per, cap + MORE if r == 0 else cap) for r in range(shards - 1)]
+        unroll = unroll_of(caps)
         sent = pl.pallas_call(
-            picking_kernel,
-            out_shape=[shape((cap, half, LANES)) for cap in caps],
+            functools.partial(picking_kernel, unroll),
+            out_shape=[shape((cap, size // 2, LANES)) for cap in caps],
             in_specs=[SMEM, VMEM],
             out_specs=[VMEM] * (shards - 1),
             compiler_params=params(rows),
             name="picking",
         )(lists, traces)
-        first, *rest = one_round(1, caps, start_flat, low, high, traces, sent)
-        filtered, *rest = one_round(2, caps, first, rest[0], rest[1], rest[2], rest[3:])
-        (both,) = one_round(3, caps, filtered, rest[0], rest[1], rest[2], rest[3:])
+        first, *rest = one_round(1, caps, start, low, high, traces, sent)
+        second, *rest = one_round(2, caps, first, rest[0], rest[1], rest[2], rest[3:])
+        filtered, both = one_round(3, caps, second, rest[0], rest[1], rest[2], rest[3:])
         return filtered, both
 
     branches = [functools.partial(run, cap) for cap in (*CAPS, per)]

time: 93.6 us -> 85 us (0.908)
  Pallas kernels: 36.3 us -> 29.6 us
  waiting for transfers between devices: 21.8 us -> 18.3 us
  local copies, waits for them, and re-layouts: 0.86 us -> 2.08 us
    ppermute x12, waiting for transfers between devices: 9.69 us -> 4.92 us  [send_traces(): return lax.ppermute(value, 'xs', [(i, i ^ r) for i in range(count)])]
    pallas_call x3, Pallas kernels: 9.89 us -> 6.23 us  [one_round(): pl.pallas_call(functools.partial(far_kernel, step, shards, elements, unro...]
    pallas_call x8 -> x11, Pallas kernels: 25.9 us -> 22.9 us  [the longest x3 16.3 us: one_round(): pl.pallas_call(functools.partial(near_kernel, step, vectors, unroll), out...]
    unnamed x0 -> x2, local copies, waits for them, and re-layouts: none -> 1.22 us
  transfers between devices with their start and end apart: 25 -> 25, of which waited for: 12 -> 12; matrix products, arithmetic and copies ran while one was open for 0% -> 0% of each run, Pallas kernels for 28% -> 27%
where the time goes in v4:
time: 85 us; the launch traced here: 84.8 us
  starting transfers between devices  32.6 us (38%)
  Pallas kernels  29.6 us (35%)
  waiting for transfers between devices  18.3 us (22%)
  local copies, waits for them, and re-layouts  2.08 us (2%)
    ppermute x12, starting transfers between devices, send_traces(): return lax.ppermute(value, 'xs', [(i, i ^ r) for i in range(count)])  16.6 us
    pallas_call x3, Pallas kernels, one_round(): pl.pallas_call(functools.partial(near_kernel, step, vectors, unroll), out...  16.3 us
    ppermute x6, starting transfers between devices, rotate(): lax.ppermute(value, axis, [(i, (i + shift) % count) for i in range(count)])  8.07 us
    ppermute x7, starting transfers between devices, add_over(): lax.ppermute(value, axis, [(i, i ^ distance) for i in range(count)])  8.01 us
    ppermute x6, waiting for transfers between devices, rotate(): lax.ppermute(value, axis, [(i, (i + shift) % count) for i in range(count)])  7 us
    ppermute x7, waiting for transfers between devices, add_over(): lax.ppermute(value, axis, [(i, i ^ distance) for i in range(count)])  6.34 us
    pallas_call x3, Pallas kernels, one_round(): pl.pallas_call(functools.partial(far_kernel, step, shards, elements, unro...  6.23 us
    pallas_call x6, Pallas kernels, one_round(): pl.pallas_call(functools.partial(middle_kernel, which, vectors), out_shap...  5.08 us
  transfers between devices with their start and end apart: 25, of which 12 were waited for; matrix products, arithmetic and copies ran while one was open for 0% of the time, Pallas kernels for 27%

profile of v4, /device:TPU:0, one launch (start us, length us, event | category | flops | bytes accessed | tf_op | source)
XLA Modules:
  0.0 84.8 jit_solution(5052592764063652252)
XLA Ops:
  0.6 0.7 add_select_fusion.3
  1.6 5.1 %collective-permute-start.47 = (s32[32,128]{1,0:T(8,128)S(1)}, s32[32,128]{1,0:T(8,128)S(1)}, u32[]{:S(2)}, u32[]{:S(2)}) collective-permute-start(s32[32,128]{1,0:T(8,128)S(1)} %broadcast_in_dim.19.refs_0_), channel_id=1, source_target_pairs={{0,3},{1,2},{2,1},{3,0},{4,7},{5,6},{6,5},{7,4},{8,11},{9,10},{10,... | collective-permute-start | bytes 49160 | tf_op jit(solution)/shard_map/ppermute | solution.py:362
  6.6 0.6 collective-permute-start.45
  7.4 1.2 %copy-done = bf16[8,16,8,512]{3,2,1,0:T(8,128)(2,1)S(1)} copy-done((bf16[8,16,8,512]{3,2,1,0:T(8,128)(2,1)S(1)}, bf16[8,16,8,512]{3,2,1,0:T(8,128)(2,1)}, u32[]{:S(2)}) %copy-start) | copy-done | bytes 1048600
  8.6 0.9 %opening.1 = (bf16[8,128,512]{2,1,0:T(8,128)(2,1)S(1)}, bf16[8,64,512]{2,1,0:T(8,128)(2,1)S(1)}, bf16[8,64,512]{2,1,0:T(8,128)(2,1)S(1)}, bf16[32,64,128]{2,1,0:T(8,128)(2,1)S(1)}) custom-call(bf16[1024,512]{1,0:T(8,128)(2,1)S(1)} %bitcast.7, bf16[512,256]{1,0:T(8,128)(2,1)S(1)} %fusion.12.selector_ref), custom_call_target="tpu_custom_call" | custom-call | tf_op jit(solution)/shard_map/opening/pallas_call | solution.py:408
  9.5 1.7 %collective-permute-done.46.refs_2_ = s32[32,128]{1,0:T(8,128)S(1)} collective-permute-done((s32[32,128]{1,0:T(8,128)S(1)}, s32[32,128]{1,0:T(8,128)S(1)}, u32[]{:S(2)}, u32[]{:S(2)}) %collective-permute-start.46) | collective-permute-done | bytes 16416 | tf_op jit(solution)/shard_map/ppermute | solution.py:362
  11.3 0.4 pattern.1
  11.8 58.0 %conditional.1 = (bf16[1024,512]{1,0:T(8,128)(2,1)}, f32[32,128]{1,0:T(8,128)S(1)}) conditional(s32[]{:T(128)} %bitcast.1, (bf16[8,128,512]{2,1,0:T(8,128)(2,1)S(1)}, bf16[8,512,512]{2,1,0:T(8,128)(2,1)}, bf16[4096,512]{1,0:T(8,128)(2,1)}, bf16[8,64,512]{2,1,0:T(8,128)(2,1)S(1)}, bf16[8,64,512]{2,1,0:T(8,128)(2,1)S(1)}, ...), branch_computations={%region_0.1_spmd, %region_1.2_spmd, %region_2.3_spmd} | conditional | flops 16911433728 | bytes 193400976 | solution.py:498
  11.9 2.6 %collective-permute-start.1 = (bf16[8,64,512]{2,1,0:T(8,128)(2,1)S(1)}, bf16[8,64,512]{2,1,0:T(8,128)(2,1)S(1)}, u32[]{:S(2)}, u32[]{:S(2)}) collective-permute-start(bf16[8,64,512]{2,1,0:T(8,128)(2,1)S(1)} %get-tuple-element.69), channel_id=1, source_target_pairs={{0,28},{4,0},{8,4},{12,8},{16,12},{20,16},{24,20},{28,24},{1,29},{... | collective-permute-start | bytes 1572872 | tf_op jit(solution)/shard_map/cond/branch_0_fun/ppermute | solution.py:356
  14.5 0.6 picking.3
  15.1 2.1 %collective-permute-start.3 = (bf16[9,64,128]{2,1,0:T(8,128)(2,1)S(1)}, bf16[9,64,128]{2,1,0:T(8,128)(2,1)S(1)}, u32[]{:S(2)}, u32[]{:S(2)}) collective-permute-start(bf16[9,64,128]{2,1,0:T(8,128)(2,1)S(1)} %get-tuple-element.72), channel_id=1, source_target_pairs={{0,2},{1,3},{2,0},{3,1},{4,6},{5,7},{6,4},{7,5},{8,10},{9,11},{10,... | collective-permute-start | bytes 442376 | tf_op jit(solution)/shard_map/cond/branch_0_fun/ppermute | solution.py:362
  17.3 1.4 %collective-permute-start.2 = (bf16[12,64,128]{2,1,0:T(8,128)(2,1)S(1)}, bf16[12,64,128]{2,1,0:T(8,128)(2,1)S(1)}, u32[]{:S(2)}, u32[]{:S(2)}) collective-permute-start(bf16[12,64,128]{2,1,0:T(8,128)(2,1)S(1)} %get-tuple-element.71), channel_id=1, source_target_pairs={{0,1},{1,0},{2,3},{3,2},{4,5},{5,4},{6,7},{7,6},{8,9},{9,8},{10,11... | collective-permute-start | bytes 589832 | tf_op jit(solution)/shard_map/cond/branch_0_fun/ppermute | solution.py:362
  18.7 7.3 %near_1.3.near_ref = f32[8,128,512]{2,1,0:T(8,128)S(1)} custom-call(bf16[8,128,512]{2,1,0:T(8,128)(2,1)S(1)} %get-tuple-element.49.refs_0_.refs_3_, bf16[8,512,512]{2,1,0:T(8,128)(2,1)} %get-tuple-element.66.refs_1_, bf16[4096,512]{1,0:T(8,128)(2,1)} %get-tuple-element.67.refs_2_.axial_ref), custom_call_target="tpu_custom_call" | custom-call | flops 3758096384 | bytes 10000000 | tf_op jit(solution)/shard_map/cond/branch_0_fun/near_1/pallas_call | solution.py:436
  26.0 0.8 middle_1.6.near_ref
  26.9 0.8 %middle_1.7.refs_2_ = f32[8,128,512]{2,1,0:T(8,128)S(1)} custom-call(f32[8,128,512]{2,1,0:T(8,128)S(1)} %middle_1.6.near_ref, bf16[8,64,512]{2,1,0:T(8,128)(2,1)S(1)} %collective-permute-done.1.edge_ref, bf16[4096,512]{1,0:T(8,128)(2,1)S(1)} %copy-done.1), custom_call_target="tpu_custom_call", output_to_operand_aliasing={{}: (0, {})} | custom-call | flops 671088640 | bytes 10000000 | tf_op jit(solution)/shard_map/cond/branch_0_fun/middle_1/pallas_call | solution.py:447
  27.8 1.3 %collective-permute-done.2.refs_4_ = bf16[12,64,128]{2,1,0:T(8,128)(2,1)S(1)} collective-permute-done((bf16[12,64,128]{2,1,0:T(8,128)(2,1)S(1)}, bf16[12,64,128]{2,1,0:T(8,128)(2,1)S(1)}, u32[]{:S(2)}, u32[]{:S(2)}) %collective-permute-start.2) | collective-permute-done | bytes 196640 | tf_op jit(solution)/shard_map/cond/branch_0_fun/ppermute | solution.py:362
  29.0 1.8 %far_1.3 = (bf16[8,128,512]{2,1,0:T(8,128)(2,1)S(1)}, bf16[8,64,512]{2,1,0:T(8,128)(2,1)S(1)}, bf16[8,64,512]{2,1,0:T(8,128)(2,1)S(1)}, bf16[32,64,128]{2,1,0:T(...) custom-call(s32[1,128]{1,0:T(1,128)S(1)} %get-tuple-element.47.refs_, ...), custom_call_target="tpu_custom_call" | custom-call | flops 536870912 | bytes 10000000 | tf_op jit(solution)/shard_map/cond/branch_0_fun/far_1/pallas_call | solution.py:469
  30.9 2.6 %collective-permute-start.6 = (bf16[8,64,512]{2,1,0:T(8,128)(2,1)S(1)}, bf16[8,64,512]{2,1,0:T(8,128)(2,1)S(1)}, u32[]{:S(2)}, u32[]{:S(2)}) collective-permute-start(bf16[8,64,512]{2,1,0:T(8,128)(2,1)S(1)} %get-tuple-element.78), channel_id=1, source_target_pairs={{0,28},{4,0},{8,4},{12,8},{16,12},{20,16},{24,20},{28,24},{1,29},{... | collective-permute-start | bytes 1572872 | tf_op jit(solution)/shard_map/cond/branch_0_fun/ppermute | solution.py:356
  33.6 2.4 %collective-permute-start.8 = (bf16[9,64,128]{2,1,0:T(8,128)(2,1)S(1)}, bf16[9,64,128]{2,1,0:T(8,128)(2,1)S(1)}, u32[]{:S(2)}, u32[]{:S(2)}) collective-permute-start(bf16[9,64,128]{2,1,0:T(8,128)(2,1)S(1)} %get-tuple-element.81), channel_id=1, source_target_pairs={{0,2},{1,3},{2,0},{3,1},{4,6},{5,7},{6,4},{7,5},{8,10},{9,11},{10,... | collective-permute-start | bytes 442376 | tf_op jit(solution)/shard_map/cond/branch_0_fun/ppermute | solution.py:362
  36.0 1.2 %collective-permute-start.9 = (bf16[9,64,128]{2,1,0:T(8,128)(2,1)S(1)}, bf16[9,64,128]{2,1,0:T(8,128)(2,1)S(1)}, u32[]{:S(2)}, u32[]{:S(2)}) collective-permute-start(bf16[9,64,128]{2,1,0:T(8,128)(2,1)S(1)} %get-tuple-element.82), channel_id=1, source_target_pairs={{0,3},{1,2},{2,1},{3,0},{4,7},{5,6},{6,5},{7,4},{8,11},{9,10},{10,... | collective-permute-start | bytes 442376 | tf_op jit(solution)/shard_map/cond/branch_0_fun/ppermute | solution.py:362
  37.2 3.8 %near_2.3.near_ref = f32[8,128,512]{2,1,0:T(8,128)S(1)} custom-call(bf16[8,128,512]{2,1,0:T(8,128)(2,1)S(1)} %get-tuple-element.76.refs_0_, bf16[8,512,512]{2,1,0:T(8,128)(2,1)S(1)} %copy-done.7, bf16[4096,512]{1,0:T(8,128)(2,1)S(1)} %copy-done.1, bf16[8,128,512]{2,1,0:T(8,128)(2,1)S(1)} %get-tuple-element.49.refs_0_.refs_3_), custom_call_target="tpu_custom_call" | custom-call | flops 3758096384 | bytes 10000000 | tf_op jit(solution)/shard_map/cond/branch_0_fun/near_2/pallas_call | solution.py:436
  41.0 4.3 %collective-permute-done.5.edge_ref = bf16[8,64,512]{2,1,0:T(8,128)(2,1)S(1)} collective-permute-done((bf16[8,64,512]{2,1,0:T(8,128)(2,1)S(1)}, bf16[8,64,512]{2,1,0:T(8,128)(2,1)S(1)}, u32[]{:S(2)}, u32[]{:S(2)}) %collective-permute-start.5) | collective-permute-done | bytes 524320 | tf_op jit(solution)/shard_map/cond/branch_0_fun/ppermute | solution.py:356
  45.2 0.8 middle_2.6.near_ref
  46.1 0.9 %middle_2.7.refs_2_ = f32[8,128,512]{2,1,0:T(8,128)S(1)} custom-call(f32[8,128,512]{2,1,0:T(8,128)S(1)} %middle_2.6.near_ref, bf16[8,64,512]{2,1,0:T(8,128)(2,1)S(1)} %collective-permute-done.6.edge_ref, bf16[4096,512]{1,0:T(8,128)(2,1)S(1)} %copy-done.1), custom_call_target="tpu_custom_call", output_to_operand_aliasing={{}: (0, {})} | custom-call | flops 671088640 | bytes 10000000 | tf_op jit(solution)/shard_map/cond/branch_0_fun/middle_2/pallas_call | solution.py:447
  47.0 0.9 %collective-permute-done.7.refs_4_ = bf16[12,64,128]{2,1,0:T(8,128)(2,1)S(1)} collective-permute-done((bf16[12,64,128]{2,1,0:T(8,128)(2,1)S(1)}, bf16[12,64,128]{2,1,0:T(8,128)(2,1)S(1)}, u32[]{:S(2)}, u32[]{:S(2)}) %collective-permute-start.7) | collective-permute-done | bytes 196640 | tf_op jit(solution)/shard_map/cond/branch_0_fun/ppermute | solution.py:362
  47.9 1.8 %far_2.3 = (bf16[8,128,512]{2,1,0:T(8,128)(2,1)S(1)}, bf16[8,64,512]{2,1,0:T(8,128)(2,1)S(1)}, bf16[8,64,512]{2,1,0:T(8,128)(2,1)S(1)}, bf16[32,64,128]{2,1,0:T(...) custom-call(s32[1,128]{1,0:T(1,128)S(1)} %get-tuple-element.47.refs_, ...), custom_call_target="tpu_custom_call" | custom-call | flops 536870912 | bytes 10000000 | tf_op jit(solution)/shard_map/cond/branch_0_fun/far_2/pallas_call | solution.py:469
  49.8 2.6 %collective-permute-start.11 = (bf16[8,64,512]{2,1,0:T(8,128)(2,1)S(1)}, bf16[8,64,512]{2,1,0:T(8,128)(2,1)S(1)}, u32[]{:S(2)}, u32[]{:S(2)}) collective-permute-start(bf16[8,64,512]{2,1,0:T(8,128)(2,1)S(1)} %get-tuple-element.88), channel_id=1, source_target_pairs={{0,28},{4,0},{8,4},{12,8},{16,12},{20,16},{24,20},{28,24},{1,29},{... | collective-permute-start | bytes 1572872 | tf_op jit(solution)/shard_map/cond/branch_0_fun/ppermute | solution.py:356
  52.5 2.4 %collective-permute-start.13 = (bf16[9,64,128]{2,1,0:T(8,128)(2,1)S(1)}, bf16[9,64,128]{2,1,0:T(8,128)(2,1)S(1)}, u32[]{:S(2)}, u32[]{:S(2)}) collective-permute-start(bf16[9,64,128]{2,1,0:T(8,128)(2,1)S(1)} %get-tuple-element.91), channel_id=1, source_target_pairs={{0,2},{1,3},{2,0},{3,1},{4,6},{5,7},{6,4},{7,5},{8,10},{9,11},{10,... | collective-permute-start | bytes 442376 | tf_op jit(solution)/shard_map/cond/branch_0_fun/ppermute | solution.py:362
  54.9 1.3 %collective-permute-start.14 = (bf16[9,64,128]{2,1,0:T(8,128)(2,1)S(1)}, bf16[9,64,128]{2,1,0:T(8,128)(2,1)S(1)}, u32[]{:S(2)}, u32[]{:S(2)}) collective-permute-start(bf16[9,64,128]{2,1,0:T(8,128)(2,1)S(1)} %get-tuple-element.92), channel_id=1, source_target_pairs={{0,3},{1,2},{2,1},{3,0},{4,7},{5,6},{6,5},{7,4},{8,11},{9,10},{10,... | collective-permute-start | bytes 442376 | tf_op jit(solution)/shard_map/cond/branch_0_fun/ppermute | solution.py:362
  56.1 5.3 %near_3.3 = (f32[8,128,512]{2,1,0:T(8,128)S(1)}, f32[128,128]{1,0:T(8,128)S(1)}, bf16[1024,512]{1,0:T(8,128)(2,1)}) custom-call(bf16[8,128,512]{2,1,0:T(8,128)(2,1)S(1)} %get-tuple-element.84.refs_0_.refs_8_, bf16[8,512,512]{2,1,0:T(8,128)(2,1)S(1)} %copy-done.7, bf16[4096,512]{1,0:T(8,128)(2,1)S(1)} %copy-done.1), custom_call_target="tpu_custom_call" | custom-call | flops 3758096384 | bytes 10000000 | tf_op jit(solution)/shard_map/cond/branch_0_fun/near_3/pallas_call | solution.py:436
  61.4 2.7 %collective-permute-done.10.edge_ref = bf16[8,64,512]{2,1,0:T(8,128)(2,1)S(1)} collective-permute-done((bf16[8,64,512]{2,1,0:T(8,128)(2,1)S(1)}, bf16[8,64,512]{2,1,0:T(8,128)(2,1)S(1)}, u32[]{:S(2)}, u32[]{:S(2)}) %collective-permute-start.10) | collective-permute-done | bytes 524320 | tf_op jit(solution)/shard_map/cond/branch_0_fun/ppermute | solution.py:356
  64.1 0.8 middle_3.6.near_ref
  65.0 0.8 middle_3.7.refs_2_
  65.9 1.0 %collective-permute-done.12.refs_4_ = bf16[12,64,128]{2,1,0:T(8,128)(2,1)S(1)} collective-permute-done((bf16[12,64,128]{2,1,0:T(8,128)(2,1)S(1)}, bf16[12,64,128]{2,1,0:T(8,128)(2,1)S(1)}, u32[]{:S(2)}, u32[]{:S(2)}) %collective-permute-start.12) | collective-permute-done | bytes 196640 | tf_op jit(solution)/shard_map/cond/branch_0_fun/ppermute | solution.py:362
  66.8 2.6 %far_3.3 = f32[32,128]{1,0:T(8,128)S(1)} custom-call(s32[1,128]{1,0:T(1,128)S(1)} %get-tuple-element.47.refs_0_, s32[8,128]{1,0:T(8,128)S(1)} %get-tuple-element.48.lists_ref.refs_1_, f32[8,128,512]{2,1,0:T(8,128)S(1)} %middle_3.7.refs_2_, bf16[32,64,128]{2,1,0:T(8,128)(2,1)S(1)} %get-tuple-element.89.refs_3_, ...), custom_call_target="tpu_custom_call" | custom-call | flops 536870912 | bytes 10000000 | tf_op jit(solution)/shard_map/cond/branch_0_fun/far_3/pallas_call | solution.py:469
  69.9 1.2 %collective-permute-done.48 = f32[32,128]{1,0:T(8,128)S(1)} collective-permute-done((f32[32,128]{1,0:T(8,128)S(1)}, f32[32,128]{1,0:T(8,128)S(1)}, u32[]{:S(2)}, u32[]{:S(2)}) %collective-permute-start.48) | collective-permute-done | bytes 16416 | tf_op jit(solution)/shard_map/ppermute | solution.py:372
  71.1 1.4 %collective-permute-start.51 = (f32[32,128]{1,0:T(8,128)S(1)}, f32[32,128]{1,0:T(8,128)S(1)}, u32[]{:S(2)}, u32[]{:S(2)}) collective-permute-start(f32[32,128]{1,0:T(8,128)S(1)} %add.146), channel_id=1, source_target_pairs={{0,24},{4,28},{8,16},{12,20},{16,8},{20,12},{24,0},{28,4},{1,25},{... | collective-permute-start | bytes 49160 | tf_op jit(solution)/shard_map/ppermute | solution.py:372
  72.5 0.7 collective-permute-start.50
  73.2 1.4 %collective-permute-start.49 = (f32[32,128]{1,0:T(8,128)S(1)}, f32[32,128]{1,0:T(8,128)S(1)}, u32[]{:S(2)}, u32[]{:S(2)}) collective-permute-start(f32[32,128]{1,0:T(8,128)S(1)} %add.146), channel_id=1, source_target_pairs={{0,8},{4,12},{8,0},{12,4},{16,24},{20,28},{24,16},{28,20},{1,9},{5... | collective-permute-start | bytes 49160 | tf_op jit(solution)/shard_map/ppermute | solution.py:372
  74.6 1.1 %collective-permute-done.51 = f32[32,128]{1,0:T(8,128)S(1)} collective-permute-done((f32[32,128]{1,0:T(8,128)S(1)}, f32[32,128]{1,0:T(8,128)S(1)}, u32[]{:S(2)}, u32[]{:S(2)}) %collective-permute-start.51) | collective-permute-done | bytes 16416 | tf_op jit(solution)/shard_map/ppermute | solution.py:372
  75.7 0.5 collective-permute-done.50
  76.2 0.7 collective-permute-done.49
  76.9 2.6 %collective-permute-start.54 = (f32[32,128]{1,0:T(8,128)S(1)}, f32[32,128]{1,0:T(8,128)S(1)}, u32[]{:S(2)}, u32[]{:S(2)}) collective-permute-start(f32[32,128]{1,0:T(8,128)S(1)} %add_add_fusion), channel_id=1, source_target_pairs={{0,3},{1,2},{2,1},{3,0},{4,7},{5,6},{6,5},{7,4},{8,11},{9,10},{10,... | collective-permute-start | bytes 49160 | tf_op jit(solution)/shard_map/ppermute | solution.py:372
  79.5 0.2 collective-permute-start.53
  79.7 1.6 %collective-permute-start.52 = (f32[32,128]{1,0:T(8,128)S(1)}, f32[32,128]{1,0:T(8,128)S(1)}, u32[]{:S(2)}, u32[]{:S(2)}) collective-permute-start(f32[32,128]{1,0:T(8,128)S(1)} %add_add_fusion), channel_id=1, source_target_pairs={{0,1},{1,0},{2,3},{3,2},{4,5},{5,4},{6,7},{7,6},{8,9},{9,8},{10,11... | collective-permute-start | bytes 49160 | tf_op jit(solution)/shard_map/ppermute | solution.py:372
  81.4 1.1 %collective-permute-done.54 = f32[32,128]{1,0:T(8,128)S(1)} collective-permute-done((f32[32,128]{1,0:T(8,128)S(1)}, f32[32,128]{1,0:T(8,128)S(1)}, u32[]{:S(2)}, u32[]{:S(2)}) %collective-permute-start.54) | collective-permute-done | bytes 16416 | tf_op jit(solution)/shard_map/ppermute | solution.py:372
  82.5 1.7 %collective-permute-done.53 = f32[32,128]{1,0:T(8,128)S(1)} collective-permute-done((f32[32,128]{1,0:T(8,128)S(1)}, f32[32,128]{1,0:T(8,128)S(1)}, u32[]{:S(2)}, u32[]{:S(2)}) %collective-permute-start.53) | collective-permute-done | bytes 16416 | tf_op jit(solution)/shard_map/ppermute | solution.py:372
  84.2 0.6 fusion.17
  (38 shorter events, 0.8 us)
Async XLA Ops:
  1.6 7.9 %collective-permute-start.47 = (s32[32,128]{1,0:T(8,128)S(1)}, s32[32,128]{1,0:T(8,128)S(1)}, u32[]{:S(2)}, u32[]{:S(2)}) collective-permute-start(s32[32,128]{1,0:T(8,128)S(1)} %broadcast_in_dim.19.refs_0_), channel_id=1, source_target_pairs={{0,3},{1,2},{2,1},{3,0},{4,7},{5,6},{6,5},{7,4},{8,11},{9,10},{10,... | collective-permute-start | bytes 49160 | tf_op jit(solution)/shard_map/ppermute | solution.py:362
  6.6 4.6 %collective-permute-start.46 = (s32[32,128]{1,0:T(8,128)S(1)}, s32[32,128]{1,0:T(8,128)S(1)}, u32[]{:S(2)}, u32[]{:S(2)}) collective-permute-start(s32[32,128]{1,0:T(8,128)S(1)} %broadcast_in_dim.19.refs_0_), channel_id=1, source_target_pairs={{0,2},{1,3},{2,0},{3,1},{4,6},{5,7},{6,4},{7,5},{8,10},{9,11},{10,... | collective-permute-start | bytes 49160 | tf_op jit(solution)/shard_map/ppermute | solution.py:362
  6.6 4.6 %collective-permute-start.45 = (s32[32,128]{1,0:T(8,128)S(1)}, s32[32,128]{1,0:T(8,128)S(1)}, u32[]{:S(2)}, u32[]{:S(2)}) collective-permute-start(s32[32,128]{1,0:T(8,128)S(1)} %broadcast_in_dim.19.refs_0_), channel_id=1, source_target_pairs={{0,1},{1,0},{2,3},{3,2},{4,5},{5,4},{6,7},{7,6},{8,9},{9,8},{10,11... | collective-permute-start | bytes 49160 | tf_op jit(solution)/shard_map/ppermute | solution.py:362
  7.4 1.2 %copy-start = (bf16[8,16,8,512]{3,2,1,0:T(8,128)(2,1)S(1)}, bf16[8,16,8,512]{3,2,1,0:T(8,128)(2,1)}, u32[]{:S(2)}) copy-start(bf16[8,16,8,512]{3,2,1,0:T(8,128)(2,1)} %param.10) | copy-start | bytes 3145732
  11.8 14.2 %collective-permute-start = (bf16[8,64,512]{2,1,0:T(8,128)(2,1)S(1)}, bf16[8,64,512]{2,1,0:T(8,128)(2,1)S(1)}, u32[]{:S(2)}, u32[]{:S(2)}) collective-permute-start(bf16[8,64,512]{2,1,0:T(8,128)(2,1)S(1)} %get-tuple-element.68), channel_id=1, source_target_pairs={{0,4},{4,8},{8,12},{12,16},{16,20},{20,24},{24,28},{28,0},{1,5},{5... | collective-permute-start | bytes 1572872 | tf_op jit(solution)/shard_map/cond/branch_0_fun/ppermute | solution.py:356
  11.9 15.0 %collective-permute-start.1 = (bf16[8,64,512]{2,1,0:T(8,128)(2,1)S(1)}, bf16[8,64,512]{2,1,0:T(8,128)(2,1)S(1)}, u32[]{:S(2)}, u32[]{:S(2)}) collective-permute-start(bf16[8,64,512]{2,1,0:T(8,128)(2,1)S(1)} %get-tuple-element.69), channel_id=1, source_target_pairs={{0,28},{4,0},{8,4},{12,8},{16,12},{20,16},{24,20},{28,24},{1,29},{... | collective-permute-start | bytes 1572872 | tf_op jit(solution)/shard_map/cond/branch_0_fun/ppermute | solution.py:356
  15.1 12.6 %collective-permute-start.3 = (bf16[9,64,128]{2,1,0:T(8,128)(2,1)S(1)}, bf16[9,64,128]{2,1,0:T(8,128)(2,1)S(1)}, u32[]{:S(2)}, u32[]{:S(2)}) collective-permute-start(bf16[9,64,128]{2,1,0:T(8,128)(2,1)S(1)} %get-tuple-element.72), channel_id=1, source_target_pairs={{0,2},{1,3},{2,0},{3,1},{4,6},{5,7},{6,4},{7,5},{8,10},{9,11},{10,... | collective-permute-start | bytes 442376 | tf_op jit(solution)/shard_map/cond/branch_0_fun/ppermute | solution.py:362
  17.2 10.5 %collective-permute-start.4 = (bf16[9,64,128]{2,1,0:T(8,128)(2,1)S(1)}, bf16[9,64,128]{2,1,0:T(8,128)(2,1)S(1)}, u32[]{:S(2)}, u32[]{:S(2)}) collective-permute-start(bf16[9,64,128]{2,1,0:T(8,128)(2,1)S(1)} %get-tuple-element.73), channel_id=1, source_target_pairs={{0,3},{1,2},{2,1},{3,0},{4,7},{5,6},{6,5},{7,4},{8,11},{9,10},{10,... | collective-permute-start | bytes 442376 | tf_op jit(solution)/shard_map/cond/branch_0_fun/ppermute | solution.py:362
  17.3 11.7 %collective-permute-start.2 = (bf16[12,64,128]{2,1,0:T(8,128)(2,1)S(1)}, bf16[12,64,128]{2,1,0:T(8,128)(2,1)S(1)}, u32[]{:S(2)}, u32[]{:S(2)}) collective-permute-start(bf16[12,64,128]{2,1,0:T(8,128)(2,1)S(1)} %get-tuple-element.71), channel_id=1, source_target_pairs={{0,1},{1,0},{2,3},{3,2},{4,5},{5,4},{6,7},{7,6},{8,9},{9,8},{10,11... | collective-permute-start | bytes 589832 | tf_op jit(solution)/shard_map/cond/branch_0_fun/ppermute | solution.py:362
  18.7 7.3 %copy-start.1 = (bf16[4096,512]{1,0:T(8,128)(2,1)S(1)}, bf16[4096,512]{1,0:T(8,128)(2,1)}, u32[]{:S(2)}) copy-start(bf16[4096,512]{1,0:T(8,128)(2,1)} %get-tuple-element.67.refs_2_.axial_ref) | copy-start | bytes 12582916 | tf_op jit(solution)/shard_map/cond
  26.9 2.2 %copy-start.4 = (bf16[8,256,512]{2,1,0:T(8,128)(2,1)S(1)}, bf16[8,256,512]{2,1,0:T(8,128)(2,1)}, u32[]{:S(2)}) copy-start(bf16[8,256,512]{2,1,0:T(8,128)(2,1)} %get-tuple-element.74.refs_7_) | copy-start | bytes 6291460 | tf_op jit(solution)/shard_map/cond
  29.0 8.2 %copy-start.7 = (bf16[8,512,512]{2,1,0:T(8,128)(2,1)S(1)}, bf16[8,512,512]{2,1,0:T(8,128)(2,1)}, u32[]{:S(2)}) copy-start(bf16[8,512,512]{2,1,0:T(8,128)(2,1)} %get-tuple-element.66.refs_1_) | copy-start | bytes 12582916 | tf_op jit(solution)/shard_map/cond
  30.9 14.4 %collective-permute-start.5 = (bf16[8,64,512]{2,1,0:T(8,128)(2,1)S(1)}, bf16[8,64,512]{2,1,0:T(8,128)(2,1)S(1)}, u32[]{:S(2)}, u32[]{:S(2)}) collective-permute-start(bf16[8,64,512]{2,1,0:T(8,128)(2,1)S(1)} %get-tuple-element.77), channel_id=1, source_target_pairs={{0,4},{4,8},{8,12},{12,16},{16,20},{20,24},{24,28},{28,0},{1,5},{5... | collective-permute-start | bytes 1572872 | tf_op jit(solution)/shard_map/cond/branch_0_fun/ppermute | solution.py:356
  30.9 15.2 %collective-permute-start.6 = (bf16[8,64,512]{2,1,0:T(8,128)(2,1)S(1)}, bf16[8,64,512]{2,1,0:T(8,128)(2,1)S(1)}, u32[]{:S(2)}, u32[]{:S(2)}) collective-permute-start(bf16[8,64,512]{2,1,0:T(8,128)(2,1)S(1)} %get-tuple-element.78), channel_id=1, source_target_pairs={{0,28},{4,0},{8,4},{12,8},{16,12},{20,16},{24,20},{28,24},{1,29},{... | collective-permute-start | bytes 1572872 | tf_op jit(solution)/shard_map/cond/branch_0_fun/ppermute | solution.py:356
  33.6 13.4 %collective-permute-start.8 = (bf16[9,64,128]{2,1,0:T(8,128)(2,1)S(1)}, bf16[9,64,128]{2,1,0:T(8,128)(2,1)S(1)}, u32[]{:S(2)}, u32[]{:S(2)}) collective-permute-start(bf16[9,64,128]{2,1,0:T(8,128)(2,1)S(1)} %get-tuple-element.81), channel_id=1, source_target_pairs={{0,2},{1,3},{2,0},{3,1},{4,6},{5,7},{6,4},{7,5},{8,10},{9,11},{10,... | collective-permute-start | bytes 442376 | tf_op jit(solution)/shard_map/cond/branch_0_fun/ppermute | solution.py:362
  36.0 11.0 %collective-permute-start.9 = (bf16[9,64,128]{2,1,0:T(8,128)(2,1)S(1)}, bf16[9,64,128]{2,1,0:T(8,128)(2,1)S(1)}, u32[]{:S(2)}, u32[]{:S(2)}) collective-permute-start(bf16[9,64,128]{2,1,0:T(8,128)(2,1)S(1)} %get-tuple-element.82), channel_id=1, source_target_pairs={{0,3},{1,2},{2,1},{3,0},{4,7},{5,6},{6,5},{7,4},{8,11},{9,10},{10,... | collective-permute-start | bytes 442376 | tf_op jit(solution)/shard_map/cond/branch_0_fun/ppermute | solution.py:362
  37.2 10.7 %collective-permute-start.7 = (bf16[12,64,128]{2,1,0:T(8,128)(2,1)S(1)}, bf16[12,64,128]{2,1,0:T(8,128)(2,1)S(1)}, u32[]{:S(2)}, u32[]{:S(2)}) collective-permute-start(bf16[12,64,128]{2,1,0:T(8,128)(2,1)S(1)} %get-tuple-element.80), channel_id=1, source_target_pairs={{0,1},{1,0},{2,3},{3,2},{4,5},{5,4},{6,7},{7,6},{8,9},{9,8},{10,11... | collective-permute-start | bytes 589832 | tf_op jit(solution)/shard_map/cond/branch_0_fun/ppermute | solution.py:362
  49.8 14.4 %collective-permute-start.10 = (bf16[8,64,512]{2,1,0:T(8,128)(2,1)S(1)}, bf16[8,64,512]{2,1,0:T(8,128)(2,1)S(1)}, u32[]{:S(2)}, u32[]{:S(2)}) collective-permute-start(bf16[8,64,512]{2,1,0:T(8,128)(2,1)S(1)} %get-tuple-element.87), channel_id=1, source_target_pairs={{0,4},{4,8},{8,12},{12,16},{16,20},{20,24},{24,28},{28,0},{1,5},{5... | collective-permute-start | bytes 1572872 | tf_op jit(solution)/shard_map/cond/branch_0_fun/ppermute | solution.py:356
  49.8 15.2 %collective-permute-start.11 = (bf16[8,64,512]{2,1,0:T(8,128)(2,1)S(1)}, bf16[8,64,512]{2,1,0:T(8,128)(2,1)S(1)}, u32[]{:S(2)}, u32[]{:S(2)}) collective-permute-start(bf16[8,64,512]{2,1,0:T(8,128)(2,1)S(1)} %get-tuple-element.88), channel_id=1, source_target_pairs={{0,28},{4,0},{8,4},{12,8},{16,12},{20,16},{24,20},{28,24},{1,29},{... | collective-permute-start | bytes 1572872 | tf_op jit(solution)/shard_map/cond/branch_0_fun/ppermute | solution.py:356
  52.5 13.4 %collective-permute-start.13 = (bf16[9,64,128]{2,1,0:T(8,128)(2,1)S(1)}, bf16[9,64,128]{2,1,0:T(8,128)(2,1)S(1)}, u32[]{:S(2)}, u32[]{:S(2)}) collective-permute-start(bf16[9,64,128]{2,1,0:T(8,128)(2,1)S(1)} %get-tuple-element.91), channel_id=1, source_target_pairs={{0,2},{1,3},{2,0},{3,1},{4,6},{5,7},{6,4},{7,5},{8,10},{9,11},{10,... | collective-permute-start | bytes 442376 | tf_op jit(solution)/shard_map/cond/branch_0_fun/ppermute | solution.py:362
  54.9 11.0 %collective-permute-start.14 = (bf16[9,64,128]{2,1,0:T(8,128)(2,1)S(1)}, bf16[9,64,128]{2,1,0:T(8,128)(2,1)S(1)}, u32[]{:S(2)}, u32[]{:S(2)}) collective-permute-start(bf16[9,64,128]{2,1,0:T(8,128)(2,1)S(1)} %get-tuple-element.92), channel_id=1, source_target_pairs={{0,3},{1,2},{2,1},{3,0},{4,7},{5,6},{6,5},{7,4},{8,11},{9,10},{10,... | collective-permute-start | bytes 442376 | tf_op jit(solution)/shard_map/cond/branch_0_fun/ppermute | solution.py:362
  56.1 10.7 %collective-permute-start.12 = (bf16[12,64,128]{2,1,0:T(8,128)(2,1)S(1)}, bf16[12,64,128]{2,1,0:T(8,128)(2,1)S(1)}, u32[]{:S(2)}, u32[]{:S(2)}) collective-permute-start(bf16[12,64,128]{2,1,0:T(8,128)(2,1)S(1)} %get-tuple-element.90), channel_id=1, source_target_pairs={{0,1},{1,0},{2,3},{3,2},{4,5},{5,4},{6,7},{7,6},{8,9},{9,8},{10,11... | collective-permute-start | bytes 589832 | tf_op jit(solution)/shard_map/cond/branch_0_fun/ppermute | solution.py:362
  69.8 1.2 %collective-permute-start.48 = (f32[32,128]{1,0:T(8,128)S(1)}, f32[32,128]{1,0:T(8,128)S(1)}, u32[]{:S(2)}, u32[]{:S(2)}) collective-permute-start(f32[32,128]{1,0:T(8,128)S(1)} %get-tuple-element.176), channel_id=1, source_target_pairs={{0,4},{4,0},{8,12},{12,8},{16,20},{20,16},{24,28},{28,24},{1,5},{5... | collective-permute-start | bytes 49160 | tf_op jit(solution)/shard_map/ppermute | solution.py:372
  71.1 4.6 %collective-permute-start.51 = (f32[32,128]{1,0:T(8,128)S(1)}, f32[32,128]{1,0:T(8,128)S(1)}, u32[]{:S(2)}, u32[]{:S(2)}) collective-permute-start(f32[32,128]{1,0:T(8,128)S(1)} %add.146), channel_id=1, source_target_pairs={{0,24},{4,28},{8,16},{12,20},{16,8},{20,12},{24,0},{28,4},{1,25},{... | collective-permute-start | bytes 49160 | tf_op jit(solution)/shard_map/ppermute | solution.py:372
  72.5 3.7 %collective-permute-start.50 = (f32[32,128]{1,0:T(8,128)S(1)}, f32[32,128]{1,0:T(8,128)S(1)}, u32[]{:S(2)}, u32[]{:S(2)}) collective-permute-start(f32[32,128]{1,0:T(8,128)S(1)} %add.146), channel_id=1, source_target_pairs={{0,16},{4,20},{8,24},{12,28},{16,0},{20,4},{24,8},{28,12},{1,17},{... | collective-permute-start | bytes 49160 | tf_op jit(solution)/shard_map/ppermute | solution.py:372
  73.2 3.7 %collective-permute-start.49 = (f32[32,128]{1,0:T(8,128)S(1)}, f32[32,128]{1,0:T(8,128)S(1)}, u32[]{:S(2)}, u32[]{:S(2)}) collective-permute-start(f32[32,128]{1,0:T(8,128)S(1)} %add.146), channel_id=1, source_target_pairs={{0,8},{4,12},{8,0},{12,4},{16,24},{20,28},{24,16},{28,20},{1,9},{5... | collective-permute-start | bytes 49160 | tf_op jit(solution)/shard_map/ppermute | solution.py:372
  76.9 5.6 %collective-permute-start.54 = (f32[32,128]{1,0:T(8,128)S(1)}, f32[32,128]{1,0:T(8,128)S(1)}, u32[]{:S(2)}, u32[]{:S(2)}) collective-permute-start(f32[32,128]{1,0:T(8,128)S(1)} %add_add_fusion), channel_id=1, source_target_pairs={{0,3},{1,2},{2,1},{3,0},{4,7},{5,6},{6,5},{7,4},{8,11},{9,10},{10,... | collective-permute-start | bytes 49160 | tf_op jit(solution)/shard_map/ppermute | solution.py:372
  79.5 4.7 %collective-permute-start.53 = (f32[32,128]{1,0:T(8,128)S(1)}, f32[32,128]{1,0:T(8,128)S(1)}, u32[]{:S(2)}, u32[]{:S(2)}) collective-permute-start(f32[32,128]{1,0:T(8,128)S(1)} %add_add_fusion), channel_id=1, source_target_pairs={{0,2},{1,3},{2,0},{3,1},{4,6},{5,7},{6,4},{7,5},{8,10},{9,11},{10,... | collective-permute-start | bytes 49160 | tf_op jit(solution)/shard_map/ppermute | solution.py:372
  79.7 4.4 %collective-permute-start.52 = (f32[32,128]{1,0:T(8,128)S(1)}, f32[32,128]{1,0:T(8,128)S(1)}, u32[]{:S(2)}, u32[]{:S(2)}) collective-permute-start(f32[32,128]{1,0:T(8,128)S(1)} %add_add_fusion), channel_id=1, source_target_pairs={{0,1},{1,0},{2,3},{3,2},{4,5},{5,4},{6,7},{7,6},{8,9},{9,8},{10,11... | collective-permute-start | bytes 49160 | tf_op jit(solution)/shard_map/ppermute | solution.py:372

commit v5 on v4

--- a/solution.py
+++ b/solution.py
@@ -22,7 +22,7 @@
 
 VMEM = pl.BlockSpec(memory_space=pltpu.VMEM)
 SMEM = pl.BlockSpec(memory_space=pltpu.SMEM)
-ANY = pl.BlockSpec(memory_space=pl.ANY)
+HBM = pl.BlockSpec(memory_space=pltpu.HBM)
 bf16 = jnp.bfloat16
 f32 = jnp.float32
 
@@ -220,6 +220,12 @@
     acc_ref[:, begin : begin + reach] += product.reshape(elements, reach, block)
 
 
+def add_offset_of(reach, position, begin, source, values_ref, axial_ref, acc_ref, e):
+    block = acc_ref.shape[2]
+    weights = axial_ref[position * block : (position + 1) * block]
+    acc_ref[e, begin : begin + reach] += dot(values_ref[e, source : source + reach], weights)
+
+
 def near_kernel(step, vectors, unroll, *refs):
     refs = list(refs)
     here_ref, diag_ref, axial_ref = refs[:3]
@@ -280,16 +286,20 @@
         each_tile(copy_ref.shape[0], ROW_TILE, narrow)
 
 
-def middle_kernel(side, vectors, near_ref, edge_ref, axial_ref, acc_ref):
+def middle_kernel(side, vectors, unroll, near_ref, edge_ref, axial_ref, acc_ref):
     del near_ref
     size = acc_ref.shape[1]
     edge = edge_ref.shape[1]
     for layers in range(1, HW + 1):
         reach = layers * vectors
         if side == 0:
-            add_offset(reach, HW - layers, 0, edge - reach, edge_ref, axial_ref, acc_ref)
+            terms = (reach, HW - layers, 0, edge - reach, edge_ref, axial_ref, acc_ref)
         else:
-            add_offset(reach, HW + layers - 1, size - reach, 0, edge_ref, axial_ref, acc_ref)
+            terms = (reach, HW + layers - 1, size - reach, 0, edge_ref, axial_ref, acc_ref)
+        if unroll > 1:
+            add_offset(*terms)
+        else:
+            each(acc_ref.shape[0], functools.partial(add_offset_of, *terms))
 
 
 def across(a, b):
@@ -408,7 +418,7 @@
     start, low, high, traces = pl.pallas_call(
         functools.partial(opening_kernel, elements),
         out_shape=[field, side, side, shape((per, size // 2, LANES))],
-        in_specs=[ANY, VMEM],
+        in_specs=[HBM, VMEM],
         out_specs=[VMEM] * 4,
         scratch_shapes=[
             pltpu.VMEM((rows, block), bf16),
@@ -445,7 +455,7 @@
         )(*operands)
         for which, arriving in enumerate((from_low, from_high)):
             near = pl.pallas_call(
-                functools.partial(middle_kernel, which, vectors),
+                functools.partial(middle_kernel, which, vectors, unroll),
                 out_shape=shape((elements, size, block), f32),
                 in_specs=[VMEM] * 3,
                 out_specs=VMEM,

time: 85 us -> 85 us (level)
  no operation moved by 1% of the time
where the time goes in v5:
time: 85 us; the launch traced here: 84.8 us
  starting transfers between devices  32.6 us (38%)
  Pallas kernels  29.6 us (35%)
  waiting for transfers between devices  18.3 us (22%)
  local copies, waits for them, and re-layouts  2.08 us (2%)
    ppermute x12, starting transfers between devices, send_traces(): return lax.ppermute(value, 'xs', [(i, i ^ r) for i in range(count)])  16.6 us
    pallas_call x3, Pallas kernels, one_round(): pl.pallas_call(functools.partial(near_kernel, step, vectors, unroll), out...  16.3 us
    ppermute x6, starting transfers between devices, rotate(): lax.ppermute(value, axis, [(i, (i + shift) % count) for i in range(count)])  8.07 us
    ppermute x7, starting transfers between devices, add_over(): lax.ppermute(value, axis, [(i, i ^ distance) for i in range(count)])  8.01 us
    ppermute x6, waiting for transfers between devices, rotate(): lax.ppermute(value, axis, [(i, (i + shift) % count) for i in range(count)])  7 us
    ppermute x7, waiting for transfers between devices, add_over(): lax.ppermute(value, axis, [(i, i ^ distance) for i in range(count)])  6.34 us
    pallas_call x3, Pallas kernels, one_round(): pl.pallas_call(functools.partial(far_kernel, step, shards, elements, unro...  6.23 us
    pallas_call x6, Pallas kernels, one_round(): pl.pallas_call(functools.partial(middle_kernel, which, vectors, unroll),...  5.08 us
  transfers between devices with their start and end apart: 25, of which 12 were waited for; matrix products, arithmetic and copies ran while one was open for 0% of the time, Pallas kernels for 27%

profile of v5, /device:TPU:0, one launch (start us, length us, event | category | flops | bytes accessed | tf_op | source)
XLA Modules:
  0.0 84.8 jit_solution(15300132237011814507)
XLA Ops:
  0.6 0.7 add_select_fusion.3
  1.6 5.1 %collective-permute-start.47 = (s32[32,128]{1,0:T(8,128)S(1)}, s32[32,128]{1,0:T(8,128)S(1)}, u32[]{:S(2)}, u32[]{:S(2)}) collective-permute-start(s32[32,128]{1,0:T(8,128)S(1)} %broadcast_in_dim.19.refs_0_), channel_id=1, source_target_pairs={{0,3},{1,2},{2,1},{3,0},{4,7},{5,6},{6,5},{7,4},{8,11},{9,10},{10,... | collective-permute-start | bytes 49160 | tf_op jit(solution)/shard_map/ppermute | solution.py:372
  6.6 0.6 collective-permute-start.45
  7.4 1.2 %copy-done = bf16[8,16,8,512]{3,2,1,0:T(8,128)(2,1)S(1)} copy-done((bf16[8,16,8,512]{3,2,1,0:T(8,128)(2,1)S(1)}, bf16[8,16,8,512]{3,2,1,0:T(8,128)(2,1)}, u32[]{:S(2)}) %copy-start) | copy-done | bytes 1048600
  8.6 0.9 %opening.1 = (bf16[8,128,512]{2,1,0:T(8,128)(2,1)S(1)}, bf16[8,64,512]{2,1,0:T(8,128)(2,1)S(1)}, bf16[8,64,512]{2,1,0:T(8,128)(2,1)S(1)}, bf16[32,64,128]{2,1,0:T(8,128)(2,1)S(1)}) custom-call(bf16[1024,512]{1,0:T(8,128)(2,1)S(1)} %bitcast.7, bf16[512,256]{1,0:T(8,128)(2,1)S(1)} %fusion.12.selector_ref), custom_call_target="tpu_custom_call" | custom-call | tf_op jit(solution)/shard_map/opening/pallas_call | solution.py:418
  9.5 1.7 %collective-permute-done.46.refs_2_ = s32[32,128]{1,0:T(8,128)S(1)} collective-permute-done((s32[32,128]{1,0:T(8,128)S(1)}, s32[32,128]{1,0:T(8,128)S(1)}, u32[]{:S(2)}, u32[]{:S(2)}) %collective-permute-start.46) | collective-permute-done | bytes 16416 | tf_op jit(solution)/shard_map/ppermute | solution.py:372
  11.3 0.4 pattern.1
  11.8 58.0 %conditional.1 = (bf16[1024,512]{1,0:T(8,128)(2,1)}, f32[32,128]{1,0:T(8,128)S(1)}) conditional(s32[]{:T(128)} %bitcast.1, (bf16[8,128,512]{2,1,0:T(8,128)(2,1)S(1)}, bf16[8,512,512]{2,1,0:T(8,128)(2,1)}, bf16[4096,512]{1,0:T(8,128)(2,1)}, bf16[8,64,512]{2,1,0:T(8,128)(2,1)S(1)}, bf16[8,64,512]{2,1,0:T(8,128)(2,1)S(1)}, ...), branch_computations={%region_0.1_spmd, %region_1.2_spmd, %region_2.3_spmd} | conditional | flops 16911433728 | bytes 193400976 | solution.py:508
  11.9 2.6 %collective-permute-start.1 = (bf16[8,64,512]{2,1,0:T(8,128)(2,1)S(1)}, bf16[8,64,512]{2,1,0:T(8,128)(2,1)S(1)}, u32[]{:S(2)}, u32[]{:S(2)}) collective-permute-start(bf16[8,64,512]{2,1,0:T(8,128)(2,1)S(1)} %get-tuple-element.69), channel_id=1, source_target_pairs={{0,28},{4,0},{8,4},{12,8},{16,12},{20,16},{24,20},{28,24},{1,29},{... | collective-permute-start | bytes 1572872 | tf_op jit(solution)/shard_map/cond/branch_0_fun/ppermute | solution.py:366
  14.5 0.6 picking.3
  15.1 2.1 %collective-permute-start.3 = (bf16[9,64,128]{2,1,0:T(8,128)(2,1)S(1)}, bf16[9,64,128]{2,1,0:T(8,128)(2,1)S(1)}, u32[]{:S(2)}, u32[]{:S(2)}) collective-permute-start(bf16[9,64,128]{2,1,0:T(8,128)(2,1)S(1)} %get-tuple-element.72), channel_id=1, source_target_pairs={{0,2},{1,3},{2,0},{3,1},{4,6},{5,7},{6,4},{7,5},{8,10},{9,11},{10,... | collective-permute-start | bytes 442376 | tf_op jit(solution)/shard_map/cond/branch_0_fun/ppermute | solution.py:372
  17.3 1.4 %collective-permute-start.2 = (bf16[12,64,128]{2,1,0:T(8,128)(2,1)S(1)}, bf16[12,64,128]{2,1,0:T(8,128)(2,1)S(1)}, u32[]{:S(2)}, u32[]{:S(2)}) collective-permute-start(bf16[12,64,128]{2,1,0:T(8,128)(2,1)S(1)} %get-tuple-element.71), channel_id=1, source_target_pairs={{0,1},{1,0},{2,3},{3,2},{4,5},{5,4},{6,7},{7,6},{8,9},{9,8},{10,11... | collective-permute-start | bytes 589832 | tf_op jit(solution)/shard_map/cond/branch_0_fun/ppermute | solution.py:372
  18.7 7.3 %near_1.3.near_ref = f32[8,128,512]{2,1,0:T(8,128)S(1)} custom-call(bf16[8,128,512]{2,1,0:T(8,128)(2,1)S(1)} %get-tuple-element.49.refs_0_.refs_3_, bf16[8,512,512]{2,1,0:T(8,128)(2,1)} %get-tuple-element.66.refs_1_, bf16[4096,512]{1,0:T(8,128)(2,1)} %get-tuple-element.67.refs_2_.axial_ref), custom_call_target="tpu_custom_call" | custom-call | flops 3758096384 | bytes 10000000 | tf_op jit(solution)/shard_map/cond/branch_0_fun/near_1/pallas_call | solution.py:446
  26.0 0.8 middle_1.6.near_ref
  26.9 0.8 %middle_1.7.refs_2_ = f32[8,128,512]{2,1,0:T(8,128)S(1)} custom-call(f32[8,128,512]{2,1,0:T(8,128)S(1)} %middle_1.6.near_ref, bf16[8,64,512]{2,1,0:T(8,128)(2,1)S(1)} %collective-permute-done.1.edge_ref, bf16[4096,512]{1,0:T(8,128)(2,1)S(1)} %copy-done.1), custom_call_target="tpu_custom_call", output_to_operand_aliasing={{}: (0, {})} | custom-call | flops 671088640 | bytes 10000000 | tf_op jit(solution)/shard_map/cond/branch_0_fun/middle_1/pallas_call | solution.py:457
  27.8 1.3 %collective-permute-done.2.refs_4_ = bf16[12,64,128]{2,1,0:T(8,128)(2,1)S(1)} collective-permute-done((bf16[12,64,128]{2,1,0:T(8,128)(2,1)S(1)}, bf16[12,64,128]{2,1,0:T(8,128)(2,1)S(1)}, u32[]{:S(2)}, u32[]{:S(2)}) %collective-permute-start.2) | collective-permute-done | bytes 196640 | tf_op jit(solution)/shard_map/cond/branch_0_fun/ppermute | solution.py:372
  29.0 1.8 %far_1.3 = (bf16[8,128,512]{2,1,0:T(8,128)(2,1)S(1)}, bf16[8,64,512]{2,1,0:T(8,128)(2,1)S(1)}, bf16[8,64,512]{2,1,0:T(8,128)(2,1)S(1)}, bf16[32,64,128]{2,1,0:T(...) custom-call(s32[1,128]{1,0:T(1,128)S(1)} %get-tuple-element.47.refs_, ...), custom_call_target="tpu_custom_call" | custom-call | flops 536870912 | bytes 10000000 | tf_op jit(solution)/shard_map/cond/branch_0_fun/far_1/pallas_call | solution.py:479
  30.9 2.6 %collective-permute-start.6 = (bf16[8,64,512]{2,1,0:T(8,128)(2,1)S(1)}, bf16[8,64,512]{2,1,0:T(8,128)(2,1)S(1)}, u32[]{:S(2)}, u32[]{:S(2)}) collective-permute-start(bf16[8,64,512]{2,1,0:T(8,128)(2,1)S(1)} %get-tuple-element.78), channel_id=1, source_target_pairs={{0,28},{4,0},{8,4},{12,8},{16,12},{20,16},{24,20},{28,24},{1,29},{... | collective-permute-start | bytes 1572872 | tf_op jit(solution)/shard_map/cond/branch_0_fun/ppermute | solution.py:366
  33.6 2.4 %collective-permute-start.8 = (bf16[9,64,128]{2,1,0:T(8,128)(2,1)S(1)}, bf16[9,64,128]{2,1,0:T(8,128)(2,1)S(1)}, u32[]{:S(2)}, u32[]{:S(2)}) collective-permute-start(bf16[9,64,128]{2,1,0:T(8,128)(2,1)S(1)} %get-tuple-element.81), channel_id=1, source_target_pairs={{0,2},{1,3},{2,0},{3,1},{4,6},{5,7},{6,4},{7,5},{8,10},{9,11},{10,... | collective-permute-start | bytes 442376 | tf_op jit(solution)/shard_map/cond/branch_0_fun/ppermute | solution.py:372
  36.0 1.2 %collective-permute-start.9 = (bf16[9,64,128]{2,1,0:T(8,128)(2,1)S(1)}, bf16[9,64,128]{2,1,0:T(8,128)(2,1)S(1)}, u32[]{:S(2)}, u32[]{:S(2)}) collective-permute-start(bf16[9,64,128]{2,1,0:T(8,128)(2,1)S(1)} %get-tuple-element.82), channel_id=1, source_target_pairs={{0,3},{1,2},{2,1},{3,0},{4,7},{5,6},{6,5},{7,4},{8,11},{9,10},{10,... | collective-permute-start | bytes 442376 | tf_op jit(solution)/shard_map/cond/branch_0_fun/ppermute | solution.py:372
  37.2 3.8 %near_2.3.near_ref = f32[8,128,512]{2,1,0:T(8,128)S(1)} custom-call(bf16[8,128,512]{2,1,0:T(8,128)(2,1)S(1)} %get-tuple-element.76.refs_0_, bf16[8,512,512]{2,1,0:T(8,128)(2,1)S(1)} %copy-done.7, bf16[4096,512]{1,0:T(8,128)(2,1)S(1)} %copy-done.1, bf16[8,128,512]{2,1,0:T(8,128)(2,1)S(1)} %get-tuple-element.49.refs_0_.refs_3_), custom_call_target="tpu_custom_call" | custom-call | flops 3758096384 | bytes 10000000 | tf_op jit(solution)/shard_map/cond/branch_0_fun/near_2/pallas_call | solution.py:446
  41.0 4.3 %collective-permute-done.5.edge_ref = bf16[8,64,512]{2,1,0:T(8,128)(2,1)S(1)} collective-permute-done((bf16[8,64,512]{2,1,0:T(8,128)(2,1)S(1)}, bf16[8,64,512]{2,1,0:T(8,128)(2,1)S(1)}, u32[]{:S(2)}, u32[]{:S(2)}) %collective-permute-start.5) | collective-permute-done | bytes 524320 | tf_op jit(solution)/shard_map/cond/branch_0_fun/ppermute | solution.py:366
  45.2 0.8 middle_2.6.near_ref
  46.1 0.9 %middle_2.7.refs_2_ = f32[8,128,512]{2,1,0:T(8,128)S(1)} custom-call(f32[8,128,512]{2,1,0:T(8,128)S(1)} %middle_2.6.near_ref, bf16[8,64,512]{2,1,0:T(8,128)(2,1)S(1)} %collective-permute-done.6.edge_ref, bf16[4096,512]{1,0:T(8,128)(2,1)S(1)} %copy-done.1), custom_call_target="tpu_custom_call", output_to_operand_aliasing={{}: (0, {})} | custom-call | flops 671088640 | bytes 10000000 | tf_op jit(solution)/shard_map/cond/branch_0_fun/middle_2/pallas_call | solution.py:457
  47.0 0.9 %collective-permute-done.7.refs_4_ = bf16[12,64,128]{2,1,0:T(8,128)(2,1)S(1)} collective-permute-done((bf16[12,64,128]{2,1,0:T(8,128)(2,1)S(1)}, bf16[12,64,128]{2,1,0:T(8,128)(2,1)S(1)}, u32[]{:S(2)}, u32[]{:S(2)}) %collective-permute-start.7) | collective-permute-done | bytes 196640 | tf_op jit(solution)/shard_map/cond/branch_0_fun/ppermute | solution.py:372
  47.9 1.8 %far_2.3 = (bf16[8,128,512]{2,1,0:T(8,128)(2,1)S(1)}, bf16[8,64,512]{2,1,0:T(8,128)(2,1)S(1)}, bf16[8,64,512]{2,1,0:T(8,128)(2,1)S(1)}, bf16[32,64,128]{2,1,0:T(...) custom-call(s32[1,128]{1,0:T(1,128)S(1)} %get-tuple-element.47.refs_, ...), custom_call_target="tpu_custom_call" | custom-call | flops 536870912 | bytes 10000000 | tf_op jit(solution)/shard_map/cond/branch_0_fun/far_2/pallas_call | solution.py:479
  49.8 2.6 %collective-permute-start.11 = (bf16[8,64,512]{2,1,0:T(8,128)(2,1)S(1)}, bf16[8,64,512]{2,1,0:T(8,128)(2,1)S(1)}, u32[]{:S(2)}, u32[]{:S(2)}) collective-permute-start(bf16[8,64,512]{2,1,0:T(8,128)(2,1)S(1)} %get-tuple-element.88), channel_id=1, source_target_pairs={{0,28},{4,0},{8,4},{12,8},{16,12},{20,16},{24,20},{28,24},{1,29},{... | collective-permute-start | bytes 1572872 | tf_op jit(solution)/shard_map/cond/branch_0_fun/ppermute | solution.py:366
  52.5 2.4 %collective-permute-start.13 = (bf16[9,64,128]{2,1,0:T(8,128)(2,1)S(1)}, bf16[9,64,128]{2,1,0:T(8,128)(2,1)S(1)}, u32[]{:S(2)}, u32[]{:S(2)}) collective-permute-start(bf16[9,64,128]{2,1,0:T(8,128)(2,1)S(1)} %get-tuple-element.91), channel_id=1, source_target_pairs={{0,2},{1,3},{2,0},{3,1},{4,6},{5,7},{6,4},{7,5},{8,10},{9,11},{10,... | collective-permute-start | bytes 442376 | tf_op jit(solution)/shard_map/cond/branch_0_fun/ppermute | solution.py:372
  54.9 1.3 %collective-permute-start.14 = (bf16[9,64,128]{2,1,0:T(8,128)(2,1)S(1)}, bf16[9,64,128]{2,1,0:T(8,128)(2,1)S(1)}, u32[]{:S(2)}, u32[]{:S(2)}) collective-permute-start(bf16[9,64,128]{2,1,0:T(8,128)(2,1)S(1)} %get-tuple-element.92), channel_id=1, source_target_pairs={{0,3},{1,2},{2,1},{3,0},{4,7},{5,6},{6,5},{7,4},{8,11},{9,10},{10,... | collective-permute-start | bytes 442376 | tf_op jit(solution)/shard_map/cond/branch_0_fun/ppermute | solution.py:372
  56.1 5.3 %near_3.3 = (f32[8,128,512]{2,1,0:T(8,128)S(1)}, f32[128,128]{1,0:T(8,128)S(1)}, bf16[1024,512]{1,0:T(8,128)(2,1)}) custom-call(bf16[8,128,512]{2,1,0:T(8,128)(2,1)S(1)} %get-tuple-element.84.refs_0_.refs_8_, bf16[8,512,512]{2,1,0:T(8,128)(2,1)S(1)} %copy-done.7, bf16[4096,512]{1,0:T(8,128)(2,1)S(1)} %copy-done.1), custom_call_target="tpu_custom_call" | custom-call | flops 3758096384 | bytes 10000000 | tf_op jit(solution)/shard_map/cond/branch_0_fun/near_3/pallas_call | solution.py:446
  61.4 2.7 %collective-permute-done.10.edge_ref = bf16[8,64,512]{2,1,0:T(8,128)(2,1)S(1)} collective-permute-done((bf16[8,64,512]{2,1,0:T(8,128)(2,1)S(1)}, bf16[8,64,512]{2,1,0:T(8,128)(2,1)S(1)}, u32[]{:S(2)}, u32[]{:S(2)}) %collective-permute-start.10) | collective-permute-done | bytes 524320 | tf_op jit(solution)/shard_map/cond/branch_0_fun/ppermute | solution.py:366
  64.1 0.8 middle_3.6.near_ref
  65.0 0.8 middle_3.7.refs_2_
  65.9 1.0 %collective-permute-done.12.refs_4_ = bf16[12,64,128]{2,1,0:T(8,128)(2,1)S(1)} collective-permute-done((bf16[12,64,128]{2,1,0:T(8,128)(2,1)S(1)}, bf16[12,64,128]{2,1,0:T(8,128)(2,1)S(1)}, u32[]{:S(2)}, u32[]{:S(2)}) %collective-permute-start.12) | collective-permute-done | bytes 196640 | tf_op jit(solution)/shard_map/cond/branch_0_fun/ppermute | solution.py:372
  66.8 2.6 %far_3.3 = f32[32,128]{1,0:T(8,128)S(1)} custom-call(s32[1,128]{1,0:T(1,128)S(1)} %get-tuple-element.47.refs_0_, s32[8,128]{1,0:T(8,128)S(1)} %get-tuple-element.48.lists_ref.refs_1_, f32[8,128,512]{2,1,0:T(8,128)S(1)} %middle_3.7.refs_2_, bf16[32,64,128]{2,1,0:T(8,128)(2,1)S(1)} %get-tuple-element.89.refs_3_, ...), custom_call_target="tpu_custom_call" | custom-call | flops 536870912 | bytes 10000000 | tf_op jit(solution)/shard_map/cond/branch_0_fun/far_3/pallas_call | solution.py:479
  69.9 1.2 %collective-permute-done.48 = f32[32,128]{1,0:T(8,128)S(1)} collective-permute-done((f32[32,128]{1,0:T(8,128)S(1)}, f32[32,128]{1,0:T(8,128)S(1)}, u32[]{:S(2)}, u32[]{:S(2)}) %collective-permute-start.48) | collective-permute-done | bytes 16416 | tf_op jit(solution)/shard_map/ppermute | solution.py:382
  71.1 1.4 %collective-permute-start.51 = (f32[32,128]{1,0:T(8,128)S(1)}, f32[32,128]{1,0:T(8,128)S(1)}, u32[]{:S(2)}, u32[]{:S(2)}) collective-permute-start(f32[32,128]{1,0:T(8,128)S(1)} %add.146), channel_id=1, source_target_pairs={{0,24},{4,28},{8,16},{12,20},{16,8},{20,12},{24,0},{28,4},{1,25},{... | collective-permute-start | bytes 49160 | tf_op jit(solution)/shard_map/ppermute | solution.py:382
  72.5 0.7 collective-permute-start.50
  73.2 1.4 %collective-permute-start.49 = (f32[32,128]{1,0:T(8,128)S(1)}, f32[32,128]{1,0:T(8,128)S(1)}, u32[]{:S(2)}, u32[]{:S(2)}) collective-permute-start(f32[32,128]{1,0:T(8,128)S(1)} %add.146), channel_id=1, source_target_pairs={{0,8},{4,12},{8,0},{12,4},{16,24},{20,28},{24,16},{28,20},{1,9},{5... | collective-permute-start | bytes 49160 | tf_op jit(solution)/shard_map/ppermute | solution.py:382
  74.6 1.1 %collective-permute-done.51 = f32[32,128]{1,0:T(8,128)S(1)} collective-permute-done((f32[32,128]{1,0:T(8,128)S(1)}, f32[32,128]{1,0:T(8,128)S(1)}, u32[]{:S(2)}, u32[]{:S(2)}) %collective-permute-start.51) | collective-permute-done | bytes 16416 | tf_op jit(solution)/shard_map/ppermute | solution.py:382
  75.7 0.5 collective-permute-done.50
  76.2 0.7 collective-permute-done.49
  76.9 2.6 %collective-permute-start.54 = (f32[32,128]{1,0:T(8,128)S(1)}, f32[32,128]{1,0:T(8,128)S(1)}, u32[]{:S(2)}, u32[]{:S(2)}) collective-permute-start(f32[32,128]{1,0:T(8,128)S(1)} %add_add_fusion), channel_id=1, source_target_pairs={{0,3},{1,2},{2,1},{3,0},{4,7},{5,6},{6,5},{7,4},{8,11},{9,10},{10,... | collective-permute-start | bytes 49160 | tf_op jit(solution)/shard_map/ppermute | solution.py:382
  79.5 0.2 collective-permute-start.53
  79.7 1.6 %collective-permute-start.52 = (f32[32,128]{1,0:T(8,128)S(1)}, f32[32,128]{1,0:T(8,128)S(1)}, u32[]{:S(2)}, u32[]{:S(2)}) collective-permute-start(f32[32,128]{1,0:T(8,128)S(1)} %add_add_fusion), channel_id=1, source_target_pairs={{0,1},{1,0},{2,3},{3,2},{4,5},{5,4},{6,7},{7,6},{8,9},{9,8},{10,11... | collective-permute-start | bytes 49160 | tf_op jit(solution)/shard_map/ppermute | solution.py:382
  81.4 1.1 %collective-permute-done.54 = f32[32,128]{1,0:T(8,128)S(1)} collective-permute-done((f32[32,128]{1,0:T(8,128)S(1)}, f32[32,128]{1,0:T(8,128)S(1)}, u32[]{:S(2)}, u32[]{:S(2)}) %collective-permute-start.54) | collective-permute-done | bytes 16416 | tf_op jit(solution)/shard_map/ppermute | solution.py:382
  82.5 1.7 %collective-permute-done.53 = f32[32,128]{1,0:T(8,128)S(1)} collective-permute-done((f32[32,128]{1,0:T(8,128)S(1)}, f32[32,128]{1,0:T(8,128)S(1)}, u32[]{:S(2)}, u32[]{:S(2)}) %collective-permute-start.53) | collective-permute-done | bytes 16416 | tf_op jit(solution)/shard_map/ppermute | solution.py:382
  84.2 0.6 fusion.17
  (38 shorter events, 0.8 us)
Async XLA Ops:
  1.6 7.9 %collective-permute-start.47 = (s32[32,128]{1,0:T(8,128)S(1)}, s32[32,128]{1,0:T(8,128)S(1)}, u32[]{:S(2)}, u32[]{:S(2)}) collective-permute-start(s32[32,128]{1,0:T(8,128)S(1)} %broadcast_in_dim.19.refs_0_), channel_id=1, source_target_pairs={{0,3},{1,2},{2,1},{3,0},{4,7},{5,6},{6,5},{7,4},{8,11},{9,10},{10,... | collective-permute-start | bytes 49160 | tf_op jit(solution)/shard_map/ppermute | solution.py:372
  6.6 4.6 %collective-permute-start.46 = (s32[32,128]{1,0:T(8,128)S(1)}, s32[32,128]{1,0:T(8,128)S(1)}, u32[]{:S(2)}, u32[]{:S(2)}) collective-permute-start(s32[32,128]{1,0:T(8,128)S(1)} %broadcast_in_dim.19.refs_0_), channel_id=1, source_target_pairs={{0,2},{1,3},{2,0},{3,1},{4,6},{5,7},{6,4},{7,5},{8,10},{9,11},{10,... | collective-permute-start | bytes 49160 | tf_op jit(solution)/shard_map/ppermute | solution.py:372
  6.6 4.6 %collective-permute-start.45 = (s32[32,128]{1,0:T(8,128)S(1)}, s32[32,128]{1,0:T(8,128)S(1)}, u32[]{:S(2)}, u32[]{:S(2)}) collective-permute-start(s32[32,128]{1,0:T(8,128)S(1)} %broadcast_in_dim.19.refs_0_), channel_id=1, source_target_pairs={{0,1},{1,0},{2,3},{3,2},{4,5},{5,4},{6,7},{7,6},{8,9},{9,8},{10,11... | collective-permute-start | bytes 49160 | tf_op jit(solution)/shard_map/ppermute | solution.py:372
  7.4 1.2 %copy-start = (bf16[8,16,8,512]{3,2,1,0:T(8,128)(2,1)S(1)}, bf16[8,16,8,512]{3,2,1,0:T(8,128)(2,1)}, u32[]{:S(2)}) copy-start(bf16[8,16,8,512]{3,2,1,0:T(8,128)(2,1)} %param.10) | copy-start | bytes 3145732
  11.8 14.2 %collective-permute-start = (bf16[8,64,512]{2,1,0:T(8,128)(2,1)S(1)}, bf16[8,64,512]{2,1,0:T(8,128)(2,1)S(1)}, u32[]{:S(2)}, u32[]{:S(2)}) collective-permute-start(bf16[8,64,512]{2,1,0:T(8,128)(2,1)S(1)} %get-tuple-element.68), channel_id=1, source_target_pairs={{0,4},{4,8},{8,12},{12,16},{16,20},{20,24},{24,28},{28,0},{1,5},{5... | collective-permute-start | bytes 1572872 | tf_op jit(solution)/shard_map/cond/branch_0_fun/ppermute | solution.py:366
  11.9 15.0 %collective-permute-start.1 = (bf16[8,64,512]{2,1,0:T(8,128)(2,1)S(1)}, bf16[8,64,512]{2,1,0:T(8,128)(2,1)S(1)}, u32[]{:S(2)}, u32[]{:S(2)}) collective-permute-start(bf16[8,64,512]{2,1,0:T(8,128)(2,1)S(1)} %get-tuple-element.69), channel_id=1, source_target_pairs={{0,28},{4,0},{8,4},{12,8},{16,12},{20,16},{24,20},{28,24},{1,29},{... | collective-permute-start | bytes 1572872 | tf_op jit(solution)/shard_map/cond/branch_0_fun/ppermute | solution.py:366
  15.1 12.6 %collective-permute-start.3 = (bf16[9,64,128]{2,1,0:T(8,128)(2,1)S(1)}, bf16[9,64,128]{2,1,0:T(8,128)(2,1)S(1)}, u32[]{:S(2)}, u32[]{:S(2)}) collective-permute-start(bf16[9,64,128]{2,1,0:T(8,128)(2,1)S(1)} %get-tuple-element.72), channel_id=1, source_target_pairs={{0,2},{1,3},{2,0},{3,1},{4,6},{5,7},{6,4},{7,5},{8,10},{9,11},{10,... | collective-permute-start | bytes 442376 | tf_op jit(solution)/shard_map/cond/branch_0_fun/ppermute | solution.py:372
  17.2 10.5 %collective-permute-start.4 = (bf16[9,64,128]{2,1,0:T(8,128)(2,1)S(1)}, bf16[9,64,128]{2,1,0:T(8,128)(2,1)S(1)}, u32[]{:S(2)}, u32[]{:S(2)}) collective-permute-start(bf16[9,64,128]{2,1,0:T(8,128)(2,1)S(1)} %get-tuple-element.73), channel_id=1, source_target_pairs={{0,3},{1,2},{2,1},{3,0},{4,7},{5,6},{6,5},{7,4},{8,11},{9,10},{10,... | collective-permute-start | bytes 442376 | tf_op jit(solution)/shard_map/cond/branch_0_fun/ppermute | solution.py:372
  17.3 11.7 %collective-permute-start.2 = (bf16[12,64,128]{2,1,0:T(8,128)(2,1)S(1)}, bf16[12,64,128]{2,1,0:T(8,128)(2,1)S(1)}, u32[]{:S(2)}, u32[]{:S(2)}) collective-permute-start(bf16[12,64,128]{2,1,0:T(8,128)(2,1)S(1)} %get-tuple-element.71), channel_id=1, source_target_pairs={{0,1},{1,0},{2,3},{3,2},{4,5},{5,4},{6,7},{7,6},{8,9},{9,8},{10,11... | collective-permute-start | bytes 589832 | tf_op jit(solution)/shard_map/cond/branch_0_fun/ppermute | solution.py:372
  18.7 7.3 %copy-start.1 = (bf16[4096,512]{1,0:T(8,128)(2,1)S(1)}, bf16[4096,512]{1,0:T(8,128)(2,1)}, u32[]{:S(2)}) copy-start(bf16[4096,512]{1,0:T(8,128)(2,1)} %get-tuple-element.67.refs_2_.axial_ref) | copy-start | bytes 12582916 | tf_op jit(solution)/shard_map/cond
  26.9 2.2 %copy-start.4 = (bf16[8,256,512]{2,1,0:T(8,128)(2,1)S(1)}, bf16[8,256,512]{2,1,0:T(8,128)(2,1)}, u32[]{:S(2)}) copy-start(bf16[8,256,512]{2,1,0:T(8,128)(2,1)} %get-tuple-element.74.refs_7_) | copy-start | bytes 6291460 | tf_op jit(solution)/shard_map/cond
  29.0 8.2 %copy-start.7 = (bf16[8,512,512]{2,1,0:T(8,128)(2,1)S(1)}, bf16[8,512,512]{2,1,0:T(8,128)(2,1)}, u32[]{:S(2)}) copy-start(bf16[8,512,512]{2,1,0:T(8,128)(2,1)} %get-tuple-element.66.refs_1_) | copy-start | bytes 12582916 | tf_op jit(solution)/shard_map/cond
  30.9 14.4 %collective-permute-start.5 = (bf16[8,64,512]{2,1,0:T(8,128)(2,1)S(1)}, bf16[8,64,512]{2,1,0:T(8,128)(2,1)S(1)}, u32[]{:S(2)}, u32[]{:S(2)}) collective-permute-start(bf16[8,64,512]{2,1,0:T(8,128)(2,1)S(1)} %get-tuple-element.77), channel_id=1, source_target_pairs={{0,4},{4,8},{8,12},{12,16},{16,20},{20,24},{24,28},{28,0},{1,5},{5... | collective-permute-start | bytes 1572872 | tf_op jit(solution)/shard_map/cond/branch_0_fun/ppermute | solution.py:366
  30.9 15.2 %collective-permute-start.6 = (bf16[8,64,512]{2,1,0:T(8,128)(2,1)S(1)}, bf16[8,64,512]{2,1,0:T(8,128)(2,1)S(1)}, u32[]{:S(2)}, u32[]{:S(2)}) collective-permute-start(bf16[8,64,512]{2,1,0:T(8,128)(2,1)S(1)} %get-tuple-element.78), channel_id=1, source_target_pairs={{0,28},{4,0},{8,4},{12,8},{16,12},{20,16},{24,20},{28,24},{1,29},{... | collective-permute-start | bytes 1572872 | tf_op jit(solution)/shard_map/cond/branch_0_fun/ppermute | solution.py:366
  33.6 13.4 %collective-permute-start.8 = (bf16[9,64,128]{2,1,0:T(8,128)(2,1)S(1)}, bf16[9,64,128]{2,1,0:T(8,128)(2,1)S(1)}, u32[]{:S(2)}, u32[]{:S(2)}) collective-permute-start(bf16[9,64,128]{2,1,0:T(8,128)(2,1)S(1)} %get-tuple-element.81), channel_id=1, source_target_pairs={{0,2},{1,3},{2,0},{3,1},{4,6},{5,7},{6,4},{7,5},{8,10},{9,11},{10,... | collective-permute-start | bytes 442376 | tf_op jit(solution)/shard_map/cond/branch_0_fun/ppermute | solution.py:372
  36.0 11.0 %collective-permute-start.9 = (bf16[9,64,128]{2,1,0:T(8,128)(2,1)S(1)}, bf16[9,64,128]{2,1,0:T(8,128)(2,1)S(1)}, u32[]{:S(2)}, u32[]{:S(2)}) collective-permute-start(bf16[9,64,128]{2,1,0:T(8,128)(2,1)S(1)} %get-tuple-element.82), channel_id=1, source_target_pairs={{0,3},{1,2},{2,1},{3,0},{4,7},{5,6},{6,5},{7,4},{8,11},{9,10},{10,... | collective-permute-start | bytes 442376 | tf_op jit(solution)/shard_map/cond/branch_0_fun/ppermute | solution.py:372
  37.2 10.7 %collective-permute-start.7 = (bf16[12,64,128]{2,1,0:T(8,128)(2,1)S(1)}, bf16[12,64,128]{2,1,0:T(8,128)(2,1)S(1)}, u32[]{:S(2)}, u32[]{:S(2)}) collective-permute-start(bf16[12,64,128]{2,1,0:T(8,128)(2,1)S(1)} %get-tuple-element.80), channel_id=1, source_target_pairs={{0,1},{1,0},{2,3},{3,2},{4,5},{5,4},{6,7},{7,6},{8,9},{9,8},{10,11... | collective-permute-start | bytes 589832 | tf_op jit(solution)/shard_map/cond/branch_0_fun/ppermute | solution.py:372
  49.8 14.4 %collective-permute-start.10 = (bf16[8,64,512]{2,1,0:T(8,128)(2,1)S(1)}, bf16[8,64,512]{2,1,0:T(8,128)(2,1)S(1)}, u32[]{:S(2)}, u32[]{:S(2)}) collective-permute-start(bf16[8,64,512]{2,1,0:T(8,128)(2,1)S(1)} %get-tuple-element.87), channel_id=1, source_target_pairs={{0,4},{4,8},{8,12},{12,16},{16,20},{20,24},{24,28},{28,0},{1,5},{5... | collective-permute-start | bytes 1572872 | tf_op jit(solution)/shard_map/cond/branch_0_fun/ppermute | solution.py:366
  49.8 15.2 %collective-permute-start.11 = (bf16[8,64,512]{2,1,0:T(8,128)(2,1)S(1)}, bf16[8,64,512]{2,1,0:T(8,128)(2,1)S(1)}, u32[]{:S(2)}, u32[]{:S(2)}) collective-permute-start(bf16[8,64,512]{2,1,0:T(8,128)(2,1)S(1)} %get-tuple-element.88), channel_id=1, source_target_pairs={{0,28},{4,0},{8,4},{12,8},{16,12},{20,16},{24,20},{28,24},{1,29},{... | collective-permute-start | bytes 1572872 | tf_op jit(solution)/shard_map/cond/branch_0_fun/ppermute | solution.py:366
  52.5 13.4 %collective-permute-start.13 = (bf16[9,64,128]{2,1,0:T(8,128)(2,1)S(1)}, bf16[9,64,128]{2,1,0:T(8,128)(2,1)S(1)}, u32[]{:S(2)}, u32[]{:S(2)}) collective-permute-start(bf16[9,64,128]{2,1,0:T(8,128)(2,1)S(1)} %get-tuple-element.91), channel_id=1, source_target_pairs={{0,2},{1,3},{2,0},{3,1},{4,6},{5,7},{6,4},{7,5},{8,10},{9,11},{10,... | collective-permute-start | bytes 442376 | tf_op jit(solution)/shard_map/cond/branch_0_fun/ppermute | solution.py:372
  54.9 11.0 %collective-permute-start.14 = (bf16[9,64,128]{2,1,0:T(8,128)(2,1)S(1)}, bf16[9,64,128]{2,1,0:T(8,128)(2,1)S(1)}, u32[]{:S(2)}, u32[]{:S(2)}) collective-permute-start(bf16[9,64,128]{2,1,0:T(8,128)(2,1)S(1)} %get-tuple-element.92), channel_id=1, source_target_pairs={{0,3},{1,2},{2,1},{3,0},{4,7},{5,6},{6,5},{7,4},{8,11},{9,10},{10,... | collective-permute-start | bytes 442376 | tf_op jit(solution)/shard_map/cond/branch_0_fun/ppermute | solution.py:372
  56.1 10.7 %collective-permute-start.12 = (bf16[12,64,128]{2,1,0:T(8,128)(2,1)S(1)}, bf16[12,64,128]{2,1,0:T(8,128)(2,1)S(1)}, u32[]{:S(2)}, u32[]{:S(2)}) collective-permute-start(bf16[12,64,128]{2,1,0:T(8,128)(2,1)S(1)} %get-tuple-element.90), channel_id=1, source_target_pairs={{0,1},{1,0},{2,3},{3,2},{4,5},{5,4},{6,7},{7,6},{8,9},{9,8},{10,11... | collective-permute-start | bytes 589832 | tf_op jit(solution)/shard_map/cond/branch_0_fun/ppermute | solution.py:372
  69.8 1.2 %collective-permute-start.48 = (f32[32,128]{1,0:T(8,128)S(1)}, f32[32,128]{1,0:T(8,128)S(1)}, u32[]{:S(2)}, u32[]{:S(2)}) collective-permute-start(f32[32,128]{1,0:T(8,128)S(1)} %get-tuple-element.176), channel_id=1, source_target_pairs={{0,4},{4,0},{8,12},{12,8},{16,20},{20,16},{24,28},{28,24},{1,5},{5... | collective-permute-start | bytes 49160 | tf_op jit(solution)/shard_map/ppermute | solution.py:382
  71.1 4.6 %collective-permute-start.51 = (f32[32,128]{1,0:T(8,128)S(1)}, f32[32,128]{1,0:T(8,128)S(1)}, u32[]{:S(2)}, u32[]{:S(2)}) collective-permute-start(f32[32,128]{1,0:T(8,128)S(1)} %add.146), channel_id=1, source_target_pairs={{0,24},{4,28},{8,16},{12,20},{16,8},{20,12},{24,0},{28,4},{1,25},{... | collective-permute-start | bytes 49160 | tf_op jit(solution)/shard_map/ppermute | solution.py:382
  72.5 3.7 %collective-permute-start.50 = (f32[32,128]{1,0:T(8,128)S(1)}, f32[32,128]{1,0:T(8,128)S(1)}, u32[]{:S(2)}, u32[]{:S(2)}) collective-permute-start(f32[32,128]{1,0:T(8,128)S(1)} %add.146), channel_id=1, source_target_pairs={{0,16},{4,20},{8,24},{12,28},{16,0},{20,4},{24,8},{28,12},{1,17},{... | collective-permute-start | bytes 49160 | tf_op jit(solution)/shard_map/ppermute | solution.py:382
  73.2 3.7 %collective-permute-start.49 = (f32[32,128]{1,0:T(8,128)S(1)}, f32[32,128]{1,0:T(8,128)S(1)}, u32[]{:S(2)}, u32[]{:S(2)}) collective-permute-start(f32[32,128]{1,0:T(8,128)S(1)} %add.146), channel_id=1, source_target_pairs={{0,8},{4,12},{8,0},{12,4},{16,24},{20,28},{24,16},{28,20},{1,9},{5... | collective-permute-start | bytes 49160 | tf_op jit(solution)/shard_map/ppermute | solution.py:382
  76.9 5.6 %collective-permute-start.54 = (f32[32,128]{1,0:T(8,128)S(1)}, f32[32,128]{1,0:T(8,128)S(1)}, u32[]{:S(2)}, u32[]{:S(2)}) collective-permute-start(f32[32,128]{1,0:T(8,128)S(1)} %add_add_fusion), channel_id=1, source_target_pairs={{0,3},{1,2},{2,1},{3,0},{4,7},{5,6},{6,5},{7,4},{8,11},{9,10},{10,... | collective-permute-start | bytes 49160 | tf_op jit(solution)/shard_map/ppermute | solution.py:382
  79.5 4.7 %collective-permute-start.53 = (f32[32,128]{1,0:T(8,128)S(1)}, f32[32,128]{1,0:T(8,128)S(1)}, u32[]{:S(2)}, u32[]{:S(2)}) collective-permute-start(f32[32,128]{1,0:T(8,128)S(1)} %add_add_fusion), channel_id=1, source_target_pairs={{0,2},{1,3},{2,0},{3,1},{4,6},{5,7},{6,4},{7,5},{8,10},{9,11},{10,... | collective-permute-start | bytes 49160 | tf_op jit(solution)/shard_map/ppermute | solution.py:382
  79.7 4.4 %collective-permute-start.52 = (f32[32,128]{1,0:T(8,128)S(1)}, f32[32,128]{1,0:T(8,128)S(1)}, u32[]{:S(2)}, u32[]{:S(2)}) collective-permute-start(f32[32,128]{1,0:T(8,128)S(1)} %add_add_fusion), channel_id=1, source_target_pairs={{0,1},{1,0},{2,3},{3,2},{4,5},{5,4},{6,7},{7,6},{8,9},{9,8},{10,11... | collective-permute-start | bytes 49160 | tf_op jit(solution)/shard_map/ppermute | solution.py:382
